TPU v7x, 32 devices: a whole 2x2x4 slice. The times are simulated.
32 devices in a mesh: groups: 2 (over x), blk: 16 (over z, y, core).
Axes of the slice: x: 2, y: 2, z: 4, core: 2. Of those that a mesh axis runs over, the one named last changes fastest.
Arguments:
- heads: float32 [16384, 400], P(('groups', 'blk')), parts along dimension 0, may hold values from -2.4 to 2.4
- head_state: float32 [16384], P(('groups', 'blk')), parts along dimension 0, may hold values from 0.02 to 0.5
- tails: float32 [16384, 400], P(('groups', 'blk')), parts along dimension 0, may hold values from -2.4 to 2.4
- tail_state: float32 [16384], P(('groups', 'blk')), parts along dimension 0, may hold values from 0.02 to 0.5
- relations: float32 [1000, 400], P('groups'), parts along dimension 0, may hold values from -1.8 to 1.8
- rel_state: float32 [1000], P('groups'), parts along dimension 0, may hold values from 0.02 to 0.5
- edge_src: int32 [2, 32768], P(None, ('groups', 'blk')), parts along dimension 1, may hold values from 0 to 511
- edge_rel: int32 [2, 32768], P(None, ('groups', 'blk')), parts along dimension 1, may hold values from 0 to 499
- edge_dst: int32 [2, 32768], P(None, ('groups', 'blk')), parts along dimension 1, may hold values from 0 to 511
- negatives: int32 [2, 64, 512], P(None, ('groups', 'blk')), parts along dimension 1, may hold values from 0 to 511
Outputs:
- heads_out: float32 [16384, 400], P(('groups', 'blk')), parts along dimension 0
- head_state_out: float32 [16384], P(('groups', 'blk')), parts along dimension 0
- tails_out: float32 [16384, 400], P(('groups', 'blk')), parts along dimension 0
- tail_state_out: float32 [16384], P(('groups', 'blk')), parts along dimension 0
- relations_out: float32 [1000, 400], P('groups'), parts along dimension 0
- rel_state_out: float32 [1000], P('groups'), parts along dimension 0
There are 2 independent parts, one for each index of `groups`. A program takes and returns all parts, laid end to end along the dimension named above; each array names one. Nothing has to cross between parts.
Inputs may be any that keep to these rules, and one draw needn't show every extreme that they name: `edge_src`: a row within one partition. `edge_dst`: a row within one partition. `negatives`: rows within one partition, repeats allowed.
All inputs are finite; a program needn't handle non-finite values.
Results may differ from a plain program's by a relative error of at most 0.002.
Values sent between devices are 32-bit elements; how exact they have to be, the bound alone decides.
No kernel may reach another device: no remote copies, remote signals or barrier semaphores. Data moves between devices by JAX's collectives and lax.ppermute only.
A program may use at most 64 MiB of HBM per device.

v0:
```python
import jax
import jax.numpy as jnp
from jax import lax
from jax.sharding import PartitionSpec as P

neg_weight = 0.03125
learn_rate = 0.1
epsilon = 1e-06


def from_behind(value, axis, steps):
    count = lax.axis_size(axis)
    pairs = [(source, (source + steps) % count) for source in range(count)]
    return lax.ppermute(value, axis, pairs)


def product(form, left, right):
    return jnp.einsum(form, left, right, preferred_element_type=jnp.float32)


def complex_product(left, right):
    half = left.shape[1] // 2
    left_re, left_im = (left[:, :half], left[:, half:])
    right_re, right_im = (right[:, :half], right[:, half:])
    return jnp.concatenate(
        [left_re * right_re - left_im * right_im, left_re * right_im + left_im * right_re], axis=1
    )


def conj_product(grad, other):
    half = grad.shape[1] // 2
    grad_re, grad_im = (grad[:, :half], grad[:, half:])
    other_re, other_im = (other[:, :half], other[:, half:])
    return jnp.concatenate(
        [grad_re * other_re + grad_im * other_im, grad_im * other_re - grad_re * other_im], axis=1
    )


def one_hot(index, count):
    return (index[:, None] == jnp.arange(count, dtype=jnp.int32)[None, :]).astype(jnp.bfloat16)


def sum_into(index, values, count):
    selector = one_hot(index, count)
    upper = values.astype(jnp.bfloat16)
    lower = (values - upper.astype(jnp.float32)).astype(jnp.bfloat16)
    return product("er,ed->rd", selector, upper) + product("er,ed->rd", selector, lower)


def block_grads(head_rows, tail_rows, relations, sources, kinds, targets, negatives):
    width = head_rows.shape[1]
    row_count = head_rows.shape[0]
    heads_e = jnp.take(head_rows, sources, axis=0)
    rel_e = jnp.take(relations, kinds, axis=0)
    tails_e = jnp.take(tail_rows, targets, axis=0)
    query = complex_product(heads_e, rel_e)
    positive = jnp.sum(query * tails_e, axis=1)
    pos_grad = -jax.nn.sigmoid(-positive)
    tail_half = tail_rows.astype(jnp.bfloat16)
    query_half = query.astype(jnp.bfloat16)
    spans, neg_count = negatives.shape
    query_blocks = query_half.reshape(spans, -1, width)
    flat_neg = negatives.reshape(-1)
    picked = jnp.dot(one_hot(flat_neg, row_count), tail_half, preferred_element_type=jnp.float32)
    neg_rows = picked.astype(jnp.bfloat16).reshape(spans, neg_count, width)
    scores = product("ced,cnd->cen", query_blocks, neg_rows)
    neg_grad = (neg_weight * jax.nn.sigmoid(scores)).astype(jnp.bfloat16)
    query_grad = pos_grad[:, None] * tails_e + product("cen,cnd->ced", neg_grad, neg_rows).reshape(
        -1, width
    )
    row_grad = product("cen,ced->cnd", neg_grad, query_blocks).reshape(-1, width)
    tail_index = jnp.concatenate([targets, flat_neg], axis=0)
    tail_values = jnp.concatenate([pos_grad[:, None] * query, row_grad], axis=0)
    tail_grad = sum_into(tail_index, tail_values, row_count)
    head_grad = sum_into(sources, conj_product(query_grad, rel_e), row_count)
    rel_grad = sum_into(kinds, conj_product(query_grad, heads_e), relations.shape[0])
    return (head_grad, tail_grad, rel_grad)


def adagrad(param, state, grad):
    new_state = state + jnp.mean(grad * grad, axis=1)
    return (param - learn_rate * grad / (jnp.sqrt(new_state) + epsilon)[:, None], new_state)


def update_relations(relations, rel_state, rel_grad):
    total = lax.psum(rel_grad, "blk")
    return adagrad(relations, rel_state, total)


def per_device(
    heads,
    head_state,
    tails,
    tail_state,
    relations,
    rel_state,
    edge_src,
    edge_rel,
    edge_dst,
    negatives,
):
    for step in range(edge_src.shape[0]):
        if step > 0:
            tails, tail_state = from_behind((tails, tail_state), "blk", 1)
        head_grad, tail_grad, rel_grad = block_grads(
            heads, tails, relations, edge_src[step], edge_rel[step], edge_dst[step], negatives[step]
        )
        heads, head_state = adagrad(heads, head_state, head_grad)
        tails, tail_state = adagrad(tails, tail_state, tail_grad)
        relations, rel_state = update_relations(relations, rel_state, rel_grad)
    return (heads, head_state, tails, tail_state, relations, rel_state)


def solution(mesh):
    in_specs = (
        P(("groups", "blk"), None),
        P(("groups", "blk")),
        P(("groups", "blk"), None),
        P(("groups", "blk")),
        P("groups", None),
        P("groups"),
        P(None, ("groups", "blk")),
        P(None, ("groups", "blk")),
        P(None, ("groups", "blk")),
        P(None, ("groups", "blk"), None),
    )
    out_specs = (
        P(("groups", "blk"), None),
        P(("groups", "blk")),
        P(("groups", "blk"), None),
        P(("groups", "blk")),
        P("groups", None),
        P("groups"),
    )
    return jax.shard_map(
        per_device, mesh=mesh, in_specs=in_specs, out_specs=out_specs, check_vma=False
    )
```

profile of v0, /device:TPU:0, one launch (start us, length us, event | category | flops | bytes accessed | tf_op | source)
XLA Modules:
  0.0 300.8 jit_solution(11560100093035926849)
XLA Ops:
  14.4 4.9 %gather_fusion = f32[1024,400]{1,0:T(8,128)} fusion(f32[512,400]{1,0:T(8,128)S(1)} %copy.26, s32[1024]{0:T(1024)S(1)} %fusion.68), kind=kCustom, calls=%fused_computation.clone | custom fusion | bytes 3280896 | tf_op jit(solution)/shard_map/jit(_take)/gather | solution.py:53
  19.3 4.9 %gather_fusion.1 = f32[1024,400]{1,0:T(8,128)} fusion(f32[500,400]{1,0:T(8,128)S(1)} %copy.27, s32[1024]{0:T(1024)S(1)} %fusion.69), kind=kCustom, calls=%fused_computation.1.clone | custom fusion | bytes 3280896 | tf_op jit(solution)/shard_map/jit(_take)/gather | solution.py:54
  24.2 2.6 broadcast_select_fusion.2
  36.3 2.1 fusion.65
  38.5 2.1 fusion.57
  40.6 4.9 %gather_fusion.2 = f32[1024,400]{1,0:T(8,128)} fusion(f32[512,400]{1,0:T(8,128)S(1)} %copy.28, s32[1024]{0:T(1024)S(1)} %copy-done.36), kind=kCustom, calls=%fused_computation.2.clone | custom fusion | bytes 3280896 | tf_op jit(solution)/shard_map/jit(_take)/gather | solution.py:55
  45.5 3.3 %multiply_reduce_fusion.1 = f32[1024]{0:T(1024)S(1)} fusion(f32[1024,400]{1,0:T(8,128)} %gather_fusion.2, f32[1024,200]{1,0:T(8,128)} %get-tuple-element.35, f32[1024,200]{1,0:T(8,128)} %get-tuple-element.21, pred[1024]{0:T(1024)(128)(4,1)S(1)} %copy-done.41), kind=kLoop, calls=%fused_computation.48 | loop fusion | flops 1637376 | bytes 3281920 | tf_op jit(solution)/shard_map/reduce_sum | solution.py:57
  48.9 2.6 fusion.27
  60.2 2.1 fusion.32
  62.4 2.7 collective-permute-start.1
  69.6 4.9 %gather_fusion.3 = f32[1024,400]{1,0:T(8,128)} fusion(f32[512,400]{1,0:T(8,128)S(1)} %copy.37, s32[1024]{0:T(1024)S(1)} %fusion.71), kind=kCustom, calls=%fused_computation.3.clone | custom fusion | bytes 3280896 | tf_op jit(solution)/shard_map/jit(_take)/gather | solution.py:53
  77.0 79.6 %all-reduce.3.cloned.1.call-done = f32[500,400]{0,1:T(8,128)} async-done(((f32[500,400]{0,1:T(8,128)}), f32[500,400]{0,1:T(8,128)}) %all-reduce.3.cloned.1.call-update) | async-done | bytes 800016 | tf_op jit(solution)/shard_map/psum | solution.py:86
  158.5 2.2 divide_subtract_fusion.4
  162.2 4.9 %gather_fusion.4 = f32[1024,400]{1,0:T(8,128)} fusion(f32[500,400]{1,0:T(8,128)S(1)} %copy.38, s32[1024]{0:T(1024)S(1)} %fusion.72), kind=kCustom, calls=%fused_computation.5.clone | custom fusion | bytes 3280896 | tf_op jit(solution)/shard_map/jit(_take)/gather | solution.py:54
  174.4 2.1 fusion.54
  176.5 2.1 fusion.64
  180.1 5.1 %gather_fusion.5 = f32[1024,400]{1,0:T(8,128)} fusion(f32[512,400]{1,0:T(8,128)S(1)} %copy.41, s32[1024]{0:T(1024)} %fusion.73), kind=kCustom, calls=%fused_computation.4.clone | custom fusion | bytes 3280896 | tf_op jit(solution)/shard_map/jit(_take)/gather | solution.py:55
  185.2 3.3 %multiply_reduce_fusion = f32[1024]{0:T(1024)S(1)} fusion(f32[1024,400]{1,0:T(8,128)} %gather_fusion.5, f32[1024,200]{1,0:T(8,128)} %get-tuple-element.29, f32[1024,200]{1,0:T(8,128)} %get-tuple-element.15, pred[1024]{0:T(1024)(128)(4,1)S(1)} %copy-done.40), kind=kLoop, calls=%fused_computation.35 | loop fusion | flops 1637376 | bytes 3281920 | tf_op jit(solution)/shard_map/reduce_sum | solution.py:57
  188.6 3.7 %fusion.24 = (f32[1024,400]{1,0:T(8,128)}, f32[1024,400]{1,0:T(8,128)S(1)}) fusion(f32[1024,200]{1,0:T(8,128)S(1)} %copy-done.9, f32[1024,200]{1,0:T(8,128)S(1)} %copy-done.8, f32[1024]{0:T(1024)S(1)} %divide_negate_fusion, f32[2,512,400]{2,1,0:T(8,128)} %fusion.54, f32[1024,400]{1,0:T(8,128)S(1)} %copy-done.5, pred[1024]{0:T(1024)(128)(4,1)S(1)} %copy-done.40), kind=kLoop, calls=%fused_computation.56 | loop fusion | flops 2048000 | bytes 8197120 | tf_op jit(solution)/shard_map/mul | solution.py:73
  195.7 2.1 fusion.33
  197.9 3.3 %fusion = f32[512,400]{0,1:T(8,128)S(1)} fusion(s32[2048]{0:T(1024)S(1)} %copy-done.48, f32[1024,400]{1,0:T(8,128)} %bitcast.42, f32[1024,400]{1,0:T(8,128)S(1)} %copy-done.17), kind=kOutput, calls=%fused_computation.10 | convolution fusion | flops 844005376 | bytes 4104192 | tf_op jit(solution)/shard_map/er,ed->rd/dot_general | solution.py:18
  208.3 2.2 divide_subtract_fusion.1
  210.5 79.3 %all-reduce.5.cloned.1.call-done = f32[500,400]{0,1:T(8,128)} async-done(((f32[500,400]{0,1:T(8,128)}), f32[500,400]{0,1:T(8,128)}) %all-reduce.5.cloned.1.call-update) | async-done | bytes 800016 | tf_op jit(solution)/shard_map/psum | solution.py:86
  291.7 2.2 divide_subtract_fusion
  (169 shorter events, 56.6 us)
Async XLA Ops:
  7.2 6.9 %copy-start.15 = (f32[500,400]{0,1:T(8,128)S(1)}, f32[500,400]{0,1:T(8,128)}, u32[]{:S(2)}) copy-start(f32[500,400]{0,1:T(8,128)} %param.18) | copy-start | bytes 2400004
  7.2 149.4 %all-reduce.3.cloned.1.call-start = ((), (), s32[]{:S(2)}) async-start(), calls=%async_computation | async-start | bytes 1638400 | tf_op jit(solution)/shard_map/psum | solution.py:86
  40.6 4.9 %copy-start.41 = (pred[1024]{0:T(1024)(128)(4,1)S(1)}, pred[1024]{0:T(1024)(128)(4,1)}, u32[]{:S(2)}) copy-start(pred[1024]{0:T(1024)(128)(4,1)} %compare_and_fusion.3) | copy-start | bytes 3076
  45.5 3.4 %copy-start.6 = (f32[1024,200]{1,0:T(8,128)S(1)}, f32[1024,200]{1,0:T(8,128)}, u32[]{:S(2)}) copy-start(f32[1024,200]{1,0:T(8,128)} %get-tuple-element.21) | copy-start | bytes 2457604
  45.5 3.4 %copy-start.7 = (f32[1024,200]{1,0:T(8,128)S(1)}, f32[1024,200]{1,0:T(8,128)}, u32[]{:S(2)}) copy-start(f32[1024,200]{1,0:T(8,128)} %get-tuple-element.35) | copy-start | bytes 2457604
  56.3 115.1 %collective-permute-start = (f32[512,400]{0,1:T(8,128)}, f32[512,400]{0,1:T(8,128)}, u32[]{:S(2)}, u32[]{:S(2)}) collective-permute-start(f32[512,400]{0,1:T(8,128)} %divide_subtract_fusion.3), channel_id=1, source_target_pairs={{0,1},{1,2},{2,3},{3,4},{4,5},{5,6},{6,7},{7,8},{8,9},{9,10},{10,1... | collective-permute-start | bytes 2457608 | tf_op jit(solution)/shard_map/ppermute | solution.py:14
  60.2 4.9 %copy-start.26 = (s32[1,1024]{1,0:T(1,128)S(1)}, s32[1,1024]{1,0:T(1,128)}, u32[]{:S(2)}) copy-start(s32[1,1024]{1,0:T(1,128)} %get-tuple-element.44) | copy-start | bytes 12292
  60.2 4.9 %copy-start.30 = (s32[1,1024]{1,0:T(1,128)S(1)}, s32[1,1024]{1,0:T(1,128)}, u32[]{:S(2)}) copy-start(s32[1,1024]{1,0:T(1,128)} %get-tuple-element.42) | copy-start | bytes 12292
  60.2 4.9 %copy-start.23 = (s32[1,1024]{1,0:T(1,128)S(1)}, s32[1,1024]{1,0:T(1,128)}, u32[]{:S(2)}) copy-start(s32[1,1024]{1,0:T(1,128)} %get-tuple-element.40) | copy-start | bytes 12292
  60.2 6.1 %copy-start.37 = (s32[1,4,2,128]{3,2,1,0:T(2,128)S(1)}, s32[1,4,2,128]{3,2,1,0:T(2,128)}, u32[]{:S(2)}) copy-start(s32[1,4,2,128]{3,2,1,0:T(2,128)} %get-tuple-element.46) | copy-start | bytes 12292
  60.2 6.1 %copy-start.21 = (f32[1024,200]{1,0:T(8,128)S(1)}, f32[1024,200]{1,0:T(8,128)}, u32[]{:S(2)}) copy-start(f32[1024,200]{1,0:T(8,128)} %get-tuple-element.39) | copy-start | bytes 2457604
  60.2 6.1 %copy-start.33 = (s32[1,1024]{1,0:T(1,128)S(1)}, s32[1,1024]{1,0:T(1,128)}, u32[]{:S(2)}) copy-start(s32[1,1024]{1,0:T(1,128)} %copy-done.32) | copy-start | bytes 12292
  62.4 227.5 %all-reduce.5.cloned.1.call-start = ((), (), s32[]{:S(2)}) async-start(), calls=%async_computation.1 | async-start | bytes 1638400 | tf_op jit(solution)/shard_map/psum | solution.py:86
  62.4 144.6 %collective-permute-start.1 = (f32[512]{0:T(512)}, f32[512]{0:T(512)}, u32[]{:S(2)}, u32[]{:S(2)}) collective-permute-start(f32[512]{0:T(512)} %get-tuple-element.19), channel_id=1, source_target_pairs={{0,1},{1,2},{2,3},{3,4},{4,5},{5,6},{6,7},{7,8},{8,9},{9,10},{10,1... | collective-permute-start | bytes 6152 | tf_op jit(solution)/shard_map/ppermute | solution.py:14
  66.3 8.2 %copy-start.38 = (s32[1,4,2,128]{3,1,2,0:T(4,128)}, s32[1,4,2,128]{3,1,2,0:T(4,128)S(1)}, u32[]{:S(2)}) copy-start(s32[1,4,2,128]{3,1,2,0:T(4,128)S(1)} %copy.71) | copy-start | bytes 12292
  69.2 5.3 %copy-start.11 = (f32[512,400]{0,1:T(8,128)}, f32[512,400]{0,1:T(8,128)S(1)}, u32[]{:S(2)}) copy-start(f32[512,400]{0,1:T(8,128)S(1)} %divide_subtract_fusion.5) | copy-start | bytes 2457604
  75.1 83.3 %copy-start.44 = (f32[500]{0:T(512)S(1)}, f32[500]{0:T(512)}, u32[]{:S(2)}) copy-start(f32[500]{0:T(512)} %param.19) | copy-start | bytes 6004
  75.1 83.3 %copy-start.16 = (f32[500,400]{0,1:T(8,128)S(1)}, f32[500,400]{0,1:T(8,128)}, u32[]{:S(2)}) copy-start(f32[500,400]{0,1:T(8,128)} %param.18) | copy-start | bytes 2400004
  180.0 5.2 %copy-start.40 = (pred[1024]{0:T(1024)(128)(4,1)S(1)}, pred[1024]{0:T(1024)(128)(4,1)}, u32[]{:S(2)}) copy-start(pred[1024]{0:T(1024)(128)(4,1)} %compare_and_fusion) | copy-start | bytes 3076
  185.2 3.4 %copy-start.9 = (f32[1024,200]{1,0:T(8,128)S(1)}, f32[1024,200]{1,0:T(8,128)}, u32[]{:S(2)}) copy-start(f32[1024,200]{1,0:T(8,128)} %get-tuple-element.29) | copy-start | bytes 2457604
  188.6 3.7 %copy-start.3 = (f32[1024,400]{1,0:T(8,128)S(1)}, f32[1024,400]{1,0:T(8,128)}, u32[]{:S(2)}) copy-start(f32[1024,400]{1,0:T(8,128)} %copy-done.2) | copy-start | bytes 4915204
  207.0 84.1 %copy-start.35 = (f32[500]{0:T(512)S(1)}, f32[500]{0:T(512)}, u32[]{:S(2)}) copy-start(f32[500]{0:T(512)} %copy-done.34) | copy-start | bytes 6004
  207.0 84.1 %copy-start.45 = (f32[500]{0:T(512)S(1)}, f32[500]{0:T(512)}, u32[]{:S(2)}) copy-start(f32[500]{0:T(512)} %param.19) | copy-start | bytes 6004
  207.0 84.7 %copy-start.10 = (f32[500,400]{0,1:T(8,128)S(1)}, f32[500,400]{0,1:T(8,128)}, u32[]{:S(2)}) copy-start(f32[500,400]{0,1:T(8,128)} %divide_subtract_fusion.4) | copy-start | bytes 2400004
  (30 other events, 57.3 us)
Sparse Core Ops, SparseCore 0:
  62.5 94.0 all-reduce.2
  197.9 91.8 all-reduce.4
where the time goes:
time: 302 us; the launch traced here: 301 us
  waiting for transfers between devices  159 us (53%)
  local copies, waits for them, and re-layouts  44.7 us (15%)
  other arithmetic  44.7 us (15%)
  matrix products  34.4 us (11%)
  between operations  14.8 us (5%)
  starting transfers between devices  3.22 us (1%)
    psum x2, waiting for transfers between devices, update_relations(): total = lax.psum(rel_grad, 'blk')  159 us
    dot_general x14, matrix products, product(): return jnp.einsum(form, left, right, preferred_element_type=jnp.float32)  22 us
    gather x2, local copies, waits for them, and re-layouts, block_grads(): tails_e = jnp.take(tail_rows, targets, axis=0)  10.1 us
    gather x2, local copies, waits for them, and re-layouts, block_grads(): rel_e = jnp.take(relations, kinds, axis=0)  9.82 us
    gather x2, local copies, waits for them, and re-layouts, block_grads(): heads_e = jnp.take(head_rows, sources, axis=0)  9.82 us
    sub x6, other arithmetic, adagrad(): param - learn_rate * grad / (jnp.sqrt(new_state) + epsilon)[:, None]  9.02 us
    reduce_sum x2, other arithmetic, block_grads(): positive = jnp.sum(query * tails_e, axis=1)  6.62 us
    mul x2, other arithmetic, block_grads(): tail_values = jnp.concatenate([pos_grad[:, None] * query, row_grad], axis=0)  6.32 us
  transfers between devices with their start and end apart: 4, of which 2 were waited for; matrix products, arithmetic and copies ran while one was open for 23% of the time, Pallas kernels for 0%

commit v1 on v0

v1 whole, which is shorter than its diff:
```python
import functools

import jax
import jax.numpy as jnp
from jax import lax
from jax.experimental import pallas as pl
from jax.experimental.pallas import tpu as pltpu
from jax.sharding import PartitionSpec as P

neg_weight = 0.03125
learn_rate = 0.1
epsilon = 1e-06
LANES = 128
SPLITS = 3
f32 = jnp.float32
bf16 = jnp.bfloat16
NN = ((1,), (0,))
NT = ((1,), (1,))
TN = ((0,), (0,))


def dot(left, right, dims):
    return lax.dot_general(left, right, (dims, ((), ())), preferred_element_type=f32)


def split(values):
    upper = values.astype(bf16)
    return upper, (values - upper.astype(f32)).astype(bf16)


def matches(index, count):
    return lax.broadcasted_iota(jnp.int32, (count, index.shape[1]), 0) == index


def one_hot(index, count):
    return jnp.where(matches(index, count), 1.0, 0.0).astype(bf16)


def complex_product(left, right):
    half = left.shape[0] // 2
    left_re, left_im = left[:half], left[half:]
    right_re, right_im = right[:half], right[half:]
    return jnp.concatenate(
        [left_re * right_re - left_im * right_im, left_re * right_im + left_im * right_re], axis=0
    )


def conj_product(grad, other):
    half = grad.shape[0] // 2
    grad_re, grad_im = grad[:half], grad[half:]
    other_re, other_im = other[:half], other[half:]
    return jnp.concatenate(
        [grad_re * other_re + grad_im * other_im, grad_im * other_re - grad_re * other_im], axis=0
    )


def adagrad(param, state, grad):
    new_state = state + jnp.sum(grad * grad, axis=0, keepdims=True) * (1.0 / grad.shape[0])
    return param - grad * (learn_rate / (jnp.sqrt(new_state) + epsilon)), new_state


def gather(upper, lower, selector):
    return dot(upper, selector, NN) + dot(lower, selector, NN)


def padded_lanes(count):
    return -(-count // LANES) * LANES


def front_kernel(
    step, bit_ref, head_ref, tail_ref, rel_ref, src_ref, kind_ref, dst_ref, neg_ref,
    keep_ref, send_ref, y_ref, q_ref, w_ref, pg_ref,
    head_hi, head_lo, tail_hi, tail_lo, rel_hi, rel_lo, rel_pad, total,
):
    width, rows = head_ref.shape
    kinds = rel_ref.shape[1]
    rel_pad[...] = jnp.zeros_like(rel_pad)
    rel_pad[:, 0:kinds] = rel_ref[...]
    head_hi[...], head_lo[...] = split(head_ref[...])
    tail_hi[...], tail_lo[...] = split(tail_ref[0:width, :])
    rel_hi[...], rel_lo[...] = split(rel_pad[...])
    spans = neg_ref.shape[1]
    span = src_ref.shape[1] // spans
    groups = rel_pad.shape[1] // LANES
    half_groups = groups // 2
    for s in range(spans):
        e = slice(s * span, (s + 1) * span)
        h = gather(head_hi[...], head_lo[...], one_hot(src_ref[step : step + 1, e], rows))
        kind_hot = one_hot(kind_ref[step : step + 1, e], rel_pad.shape[1])
        r = gather(rel_hi[...], rel_lo[...], kind_hot)
        t = gather(tail_hi[...], tail_lo[...], one_hot(dst_ref[step : step + 1, e], rows))
        query = complex_product(h, r)
        q_ref[:, e] = query
        positive = jnp.sum(query * t, axis=0, keepdims=True)
        pos_grad = -1.0 / (1.0 + jnp.exp(positive))
        pg_ref[:, e] = pos_grad
        drawn = jnp.where(matches(neg_ref[step, s : s + 1, :], rows), 1.0, 0.0)
        times = jnp.sum(drawn, axis=1, keepdims=True)
        scores = dot(tail_hi[...], query.astype(bf16), TN)
        half_weight = 0.5 * neg_weight
        neg_grad = (half_weight * jnp.tanh(0.5 * scores) + half_weight).astype(bf16)
        w = (neg_grad.astype(f32) * times).astype(bf16)
        w_ref[:, e] = w
        query_grad = dot(tail_hi[...], w, NN) + pos_grad * t
        y_ref[:, e] = conj_product(query_grad, r)
        x_hi, x_lo = split(conj_product(query_grad, h))
        grad = dot(x_hi, kind_hot, NT) + dot(x_lo, kind_hot, NT)
        for g in range(groups):
            half, at = g // half_groups, (g % half_groups) * width
            part = grad[:, g * LANES : (g + 1) * LANES]
            if s == 0:
                total[half, at : at + width, :] = part
            else:
                total[half, at : at + width, :] += part
    bit = bit_ref[0]
    keep_ref[...] = total[bit]
    send_ref[...] = total[1 - bit]


def back_kernel(
    step, joined, head_ref, head_state_ref, tail_ref, tail_state_ref, src_ref, dst_ref,
    y_ref, q_ref, w_ref, pg_ref,
    head_out, head_state_out, tail_out, *tail_state_out,
):
    width, rows = head_ref.shape
    y_hi, y_lo = split(y_ref[...])
    src_hot = one_hot(src_ref[step : step + 1, :], rows)
    head_grad = dot(y_hi, src_hot, NT) + dot(y_lo, src_hot, NT)
    head_out[...], head_state_out[...] = adagrad(head_ref[...], head_state_ref[...], head_grad)
    query = q_ref[...]
    p_hi, p_lo = split(query * pg_ref[...])
    dst_hot = one_hot(dst_ref[step : step + 1, :], rows)
    tail_grad = (
        dot(query.astype(bf16), w_ref[...], NT) + dot(p_hi, dst_hot, NT) + dot(p_lo, dst_hot, NT)
    )
    tail, state = adagrad(tail_ref[0:width, :], tail_state_ref[...], tail_grad)
    tail_out[0:width, :] = tail
    if joined:
        tail_out[width : width + 8, :] = jnp.broadcast_to(state, (8, rows))
    else:
        tail_state_out[0][...] = state


def rel_kernel(bit_ref, rel_ref, state_ref, mine_ref, other_ref, rel_out, state_out, total, grad):
    width, kinds = rel_ref.shape
    groups = grad.shape[1] // LANES
    half_groups = groups // 2
    bit = bit_ref[0]
    total[bit] = mine_ref[...]
    total[1 - bit] = other_ref[...]
    for g in range(groups):
        half, at = g // half_groups, (g % half_groups) * width
        grad[:, g * LANES : (g + 1) * LANES] = total[half, at : at + width, :]
    rel_out[...], state_out[...] = adagrad(rel_ref[...], state_ref[...], grad[:, 0:kinds])


VMEM = pl.BlockSpec(memory_space=pltpu.VMEM)
SMEM = pl.BlockSpec(memory_space=pltpu.SMEM)
PARAMS = pltpu.CompilerParams(vmem_limit_bytes=40 * 1024 * 1024)


def shape(*dims, dtype=f32):
    return jax.ShapeDtypeStruct(dims, dtype)


def front(step, bit, heads, tails, relations, sources, kinds, targets, negatives):
    width, rows = heads.shape
    edges = sources.shape[1]
    lanes = -(-relations.shape[1] // (2 * LANES)) * 2 * LANES
    half = width * lanes // LANES // 2
    return pl.pallas_call(
        functools.partial(front_kernel, step),
        out_shape=[
            shape(half, LANES), shape(half, LANES), shape(width, edges), shape(width, edges),
            shape(rows, edges, dtype=bf16), shape(1, edges),
        ],
        in_specs=[SMEM] + [VMEM] * 7,
        out_specs=[VMEM] * 6,
        scratch_shapes=[pltpu.VMEM((width, rows), bf16)] * 4
        + [pltpu.VMEM((width, lanes), bf16)] * 2
        + [pltpu.VMEM((width, lanes), f32), pltpu.VMEM((2, half, LANES), f32)],
        compiler_params=PARAMS,
        name="front",
    )(bit, heads, tails, relations, sources, kinds, targets, negatives)


def back(step, joined, heads, head_state, tails, tail_state, sources, targets, made):
    width, rows = heads.shape
    outs = [shape(width, rows), shape(1, rows), shape(width + 8 * joined, rows)]
    outs += [] if joined else [shape(1, rows)]
    return pl.pallas_call(
        functools.partial(back_kernel, step, joined),
        out_shape=outs,
        in_specs=[VMEM] * 10,
        out_specs=[VMEM] * len(outs),
        compiler_params=PARAMS,
        name="back",
    )(heads, head_state, tails, tail_state, sources, targets, *made)


def update_relations(bit, relations, state, mine, other):
    width = relations.shape[0]
    lanes = mine.shape[0] * 2 // width * LANES
    return pl.pallas_call(
        rel_kernel,
        out_shape=[shape(*relations.shape), shape(*state.shape)],
        in_specs=[SMEM] + [VMEM] * 4,
        out_specs=[VMEM] * 2,
        scratch_shapes=[pltpu.VMEM((2,) + mine.shape, f32), pltpu.VMEM((width, lanes), f32)],
        compiler_params=PARAMS,
        name="relations",
    )(bit, relations, state, mine, other)


def swap(value, distance):
    count = lax.axis_size("blk")
    return lax.ppermute(value, "blk", [(i, i ^ distance) for i in range(count)])


def reduce_halves(keep, send):
    count = lax.axis_size("blk")
    me = lax.axis_index("blk")
    distances = [1 << k for k in range((count - 1).bit_length())]
    current = keep + swap(send, distances[0])
    halving = distances[1:SPLITS]
    for distance in halving:
        half = current.shape[0] // 2
        bit = (me // distance) % 2
        kept = lax.dynamic_slice_in_dim(current, bit * half, half, 0)
        sent = lax.dynamic_slice_in_dim(current, (1 - bit) * half, half, 0)
        current = kept + swap(sent, distance)
    for distance in distances[SPLITS:]:
        current = current + swap(current, distance)
    for distance in reversed(halving):
        bit = (me // distance) % 2
        got = swap(current, distance)
        current = jnp.where(
            bit == 0, jnp.concatenate([current, got], 0), jnp.concatenate([got, current], 0)
        )
    return current, swap(current, distances[0])


def per_device(
    heads,
    head_state,
    tails,
    tail_state,
    relations,
    rel_state,
    edge_src,
    edge_rel,
    edge_dst,
    negatives,
):
    count = lax.axis_size("blk")
    bit = (lax.axis_index("blk") % 2).astype(jnp.int32).reshape(1)
    heads, tails, relations = heads.T, tails.T, relations.T
    head_state, tail_state, rel_state = head_state[None], tail_state[None], rel_state[None]
    width = heads.shape[0]
    steps = edge_src.shape[0]
    for step in range(steps):
        joined = step < steps - 1
        keep, send, *made = front(
            step, bit, heads, tails, relations, edge_src, edge_rel, edge_dst, negatives
        )
        heads, head_state, tails, *rest = back(
            step, joined, heads, head_state, tails, tail_state, edge_src, edge_dst, made
        )
        if joined:
            tails = lax.ppermute(tails, "blk", [(i, (i + 1) % count) for i in range(count)])
            tail_state = tails[width : width + 1]
        else:
            tail_state = rest[0]
        mine, other = reduce_halves(keep, send)
        relations, rel_state = update_relations(bit, relations, rel_state, mine, other)
    return (heads.T, head_state[0], tails.T, tail_state[0], relations.T, rel_state[0])


def solution(mesh):
    in_specs = (
        P(("groups", "blk"), None),
        P(("groups", "blk")),
        P(("groups", "blk"), None),
        P(("groups", "blk")),
        P("groups", None),
        P("groups"),
        P(None, ("groups", "blk")),
        P(None, ("groups", "blk")),
        P(None, ("groups", "blk")),
        P(None, ("groups", "blk"), None),
    )
    out_specs = (
        P(("groups", "blk"), None),
        P(("groups", "blk")),
        P(("groups", "blk"), None),
        P(("groups", "blk")),
        P("groups", None),
        P("groups"),
    )
    return jax.shard_map(
        per_device, mesh=mesh, in_specs=in_specs, out_specs=out_specs, check_vma=False
    )
```

time: 302 us -> 110 us (0.36)
  waiting for transfers between devices: 159 us -> 54.9 us
  other arithmetic: 44.7 us -> 3.05 us
  matrix products: 34.4 us -> 0 us
  local copies, waits for them, and re-layouts: 44.7 us -> 12.1 us
  Pallas kernels: 0 us -> 21.2 us
  starting transfers between devices: 3.22 us -> 17.1 us
  between operations: 14.8 us -> 0.92 us
    psum x2 -> x0, waiting for transfers between devices: 159 us -> none  [update_relations(): total = lax.psum(rel_grad, 'blk')]
    ppermute x2 -> x15, waiting for transfers between devices: 0.01 us -> 54.9 us  [the longest x14 54.9 us: swap(): return lax.ppermute(value, 'blk', [(i, i ^ distance) for i in range(count)])]
    gather x6 -> x0, local copies, waits for them, and re-layouts: 29.7 us -> none  [the longest x2 10.1 us: block_grads(): tails_e = jnp.take(tail_rows, targets, axis=0)]
    dot_general x16 -> x0, matrix products: 25.9 us -> none  [the longest x14 22 us: product(): return jnp.einsum(form, left, right, preferred_element_type=jnp.float32)]
    pallas_call x0 -> x6, Pallas kernels: none -> 21.2 us  [the longest x2 12.4 us: front(): pl.pallas_call(functools.partial(front_kernel, step), out_shape=[shape(ha...]
    ppermute x2 -> x15, starting transfers between devices: 3.14 us -> 17.1 us  [the longest x14 17.1 us: swap(): return lax.ppermute(value, 'blk', [(i, i ^ distance) for i in range(count)])]
    reduce_sum x4 -> x0, other arithmetic: 9.1 us -> none  [the longest x2 6.62 us: block_grads(): positive = jnp.sum(query * tails_e, axis=1)]
    sub x6 -> x0, other arithmetic: 9.02 us -> none  [adagrad(): param - learn_rate * grad / (jnp.sqrt(new_state) + epsilon)[:, None]]
  transfers between devices with their start and end apart: 4 -> 15, of which waited for: 2 -> 12; matrix products, arithmetic and copies ran while one was open for 23% -> 1% of each run, Pallas kernels for 0% -> 7%
where the time goes in v1:
time: 110 us; the launch traced here: 109 us
  waiting for transfers between devices  54.9 us (50%)
  Pallas kernels  21.2 us (19%)
  starting transfers between devices  17.1 us (16%)
  local copies, waits for them, and re-layouts  12.1 us (11%)
  other arithmetic  3.05 us (3%)
    ppermute x14, waiting for transfers between devices, swap(): return lax.ppermute(value, 'blk', [(i, i ^ distance) for i in range(count)])  54.9 us
    ppermute x14, starting transfers between devices, swap(): return lax.ppermute(value, 'blk', [(i, i ^ distance) for i in range(count)])  17.1 us
    pallas_call x2, Pallas kernels, front(): pl.pallas_call(functools.partial(front_kernel, step), out_shape=[shape(ha...  12.4 us
    unnamed x46, local copies, waits for them, and re-layouts  12 us
    pallas_call x2, Pallas kernels, back(): pl.pallas_call(functools.partial(back_kernel, step, joined), out_shape=ou...  7.32 us
  transfers between devices with their start and end apart: 15, of which 12 were waited for; matrix products, arithmetic and copies ran while one was open for 1% of the time, Pallas kernels for 7%

profile of v1, /device:TPU:0, one launch (start us, length us, event | category | flops | bytes accessed | tf_op | source)
XLA Modules:
  0.0 109.3 jit_solution(18200628128924381787)
XLA Ops:
  6.9 6.2 %front.2 = (f32[800,128]{1,0:T(8,128)S(1)}, f32[800,128]{1,0:T(8,128)S(1)}, f32[400,1024]{1,0:T(8,128)S(1)}, f32[400,1024]{1,0:T(8,128)S(1)}, bf16[512,1024]{1,0:T(8,128)(2,1)S(1)}, /*index=5*/f32[1,1024]{1,0:T(1,128)S(1)}) custom-call(s32[1]{0:T(128)} %bitcast.4.bit_ref, f32[400,512]{1,0:T(8,128)S(1)} %bitcast.15, f32[400,512]{1,0:T(8,128)S(1)} %bitcast.17, ...), custom_call_target="tpu_custom_call" | custom-call | tf_op jit(solution)/shard_map/front/pallas_call | solution.py:171
  16.0 1.5 %collective-permute-done.1 = f32[800,128]{1,0:T(8,128)} collective-permute-done((f32[800,128]{1,0:T(8,128)S(1)}, f32[800,128]{1,0:T(8,128)}, u32[]{:S(2)}, u32[]{:S(2)}) %collective-permute-start.1) | collective-permute-done | bytes 409632 | tf_op jit(solution)/shard_map/ppermute | solution.py:217
  18.6 3.0 %collective-permute-start.2 = (f32[400,128]{1,0:T(8,128)S(1)}, f32[400,128]{1,0:T(8,128)S(1)}, u32[]{:S(2)}, u32[]{:S(2)}) collective-permute-start(f32[400,128]{1,0:T(8,128)S(1)} %constant_dynamic-slice_fusion.3), channel_id=1, source_target_pairs={{0,2},{1,3},{2,0},{3,1},{4,6},{5,7},{6,4},{7,5},{8,10},{9,11},{10,... | collective-permute-start | bytes 614408 | tf_op jit(solution)/shard_map/ppermute | solution.py:217
  21.5 5.4 %collective-permute-done.2 = f32[400,128]{1,0:T(8,128)S(1)} collective-permute-done((f32[400,128]{1,0:T(8,128)S(1)}, f32[400,128]{1,0:T(8,128)S(1)}, u32[]{:S(2)}, u32[]{:S(2)}) %collective-permute-start.2) | collective-permute-done | bytes 204832 | tf_op jit(solution)/shard_map/ppermute | solution.py:217
  27.0 1.9 %collective-permute-start.3 = (f32[200,128]{1,0:T(8,128)S(1)}, f32[200,128]{1,0:T(8,128)S(1)}, u32[]{:S(2)}, u32[]{:S(2)}) collective-permute-start(f32[200,128]{1,0:T(8,128)S(1)} %constant_dynamic-slice_fusion.2), channel_id=1, source_target_pairs={{0,4},{1,5},{2,6},{3,7},{4,0},{5,1},{6,2},{7,3},{8,12},{9,13},{10,... | collective-permute-start | bytes 307208 | tf_op jit(solution)/shard_map/ppermute | solution.py:217
  28.8 2.9 %collective-permute-done.3 = f32[200,128]{1,0:T(8,128)S(1)} collective-permute-done((f32[200,128]{1,0:T(8,128)S(1)}, f32[200,128]{1,0:T(8,128)S(1)}, u32[]{:S(2)}, u32[]{:S(2)}) %collective-permute-start.3) | collective-permute-done | bytes 102432 | tf_op jit(solution)/shard_map/ppermute | solution.py:217
  31.7 2.9 %collective-permute-start.4 = (f32[200,128]{1,0:T(8,128)S(1)}, f32[200,128]{1,0:T(8,128)S(1)}, u32[]{:S(2)}, u32[]{:S(2)}) collective-permute-start(f32[200,128]{1,0:T(8,128)S(1)} %dynamic-slice_add_fusion.3), channel_id=1, source_target_pairs={{0,8},{1,9},{2,10},{3,11},{4,12},{5,13},{6,14},{7,15},{8,0},{9,1},... | collective-permute-start | bytes 307208 | tf_op jit(solution)/shard_map/ppermute | solution.py:217
  34.6 2.8 %collective-permute-done.4 = f32[200,128]{1,0:T(8,128)S(1)} collective-permute-done((f32[200,128]{1,0:T(8,128)S(1)}, f32[200,128]{1,0:T(8,128)S(1)}, u32[]{:S(2)}, u32[]{:S(2)}) %collective-permute-start.4) | collective-permute-done | bytes 102432 | tf_op jit(solution)/shard_map/ppermute | solution.py:217
  38.0 2.0 %collective-permute-start.5 = (f32[200,128]{1,0:T(8,128)}, f32[200,128]{1,0:T(8,128)}, u32[]{:S(2)}, u32[]{:S(2)}) collective-permute-start(f32[200,128]{1,0:T(8,128)} %add.68), channel_id=1, source_target_pairs={{0,4},{1,5},{2,6},{3,7},{4,0},{5,1},{6,2},{7,3},{8,12},{9,13},{10,... | collective-permute-start | bytes 307208 | tf_op jit(solution)/shard_map/ppermute | solution.py:217
  40.0 1.4 %copy-done.7 = f32[400,1024]{1,0:T(8,128)S(1)} copy-done((f32[400,1024]{1,0:T(8,128)S(1)}, f32[400,1024]{1,0:T(8,128)}, u32[]{:S(2)}) %copy-start.7) | copy-done | bytes 1638424
  41.4 1.4 %copy-done.9 = f32[400,1024]{1,0:T(8,128)S(1)} copy-done((f32[400,1024]{1,0:T(8,128)S(1)}, f32[400,1024]{1,0:T(8,128)}, u32[]{:S(2)}) %copy-start.9) | copy-done | bytes 1638424
  42.9 3.7 %back.2 = (f32[400,512]{1,0:T(8,128)S(1)}, f32[1,512]{1,0:T(1,128)S(1)}, f32[408,512]{1,0:T(8,128)}) custom-call(f32[400,512]{1,0:T(8,128)S(1)} %bitcast.16, f32[1,512]{1,0:T(1,128)S(1)} %bitcast.19, f32[400,512]{1,0:T(8,128)S(1)} %bitcast.18, f32[1,512]{1,0:T(1,128)S(1)} %bitcast.20, s32[2,1024]{1,0:T(2,128)S(1)} %copy-done.11, s32[2,1024]{1,0:T(2,128)S(1)} %copy-done.13, ...), custom_call_target="tpu_custom_call" | custom-call | tf_op jit(solution)/shard_map/back/pallas_call | solution.py:191
  48.3 1.6 %collective-permute-start.6 = (f32[400,128]{1,0:T(8,128)S(1)}, f32[400,128]{1,0:T(8,128)S(1)}, u32[]{:S(2)}, u32[]{:S(2)}) collective-permute-start(f32[400,128]{1,0:T(8,128)S(1)} %maximum_select_fusion.2), channel_id=1, source_target_pairs={{0,2},{1,3},{2,0},{3,1},{4,6},{5,7},{6,4},{7,5},{8,10},{9,11},{10,... | collective-permute-start | bytes 614408 | tf_op jit(solution)/shard_map/ppermute | solution.py:217
  49.9 14.8 %collective-permute-done.6 = f32[400,128]{1,0:T(8,128)S(1)} collective-permute-done((f32[400,128]{1,0:T(8,128)S(1)}, f32[400,128]{1,0:T(8,128)S(1)}, u32[]{:S(2)}, u32[]{:S(2)}) %collective-permute-start.6) | collective-permute-done | bytes 204832 | tf_op jit(solution)/shard_map/ppermute | solution.py:217
  65.2 1.4 %collective-permute-done.7.other_ref = f32[800,128]{1,0:T(8,128)S(1)} collective-permute-done((f32[800,128]{1,0:T(8,128)S(1)}, f32[800,128]{1,0:T(8,128)S(1)}, u32[]{:S(2)}, u32[]{:S(2)}) %collective-permute-start.7) | collective-permute-done | bytes 409632 | tf_op jit(solution)/shard_map/ppermute | solution.py:217
  66.9 6.2 %front.3 = (f32[800,128]{1,0:T(8,128)S(1)}, f32[800,128]{1,0:T(8,128)S(1)}, f32[400,1024]{1,0:T(8,128)S(1)}, f32[400,1024]{1,0:T(8,128)S(1)}, bf16[512,1024]{1,0:T(8,128)(2,1)S(1)}, /*index=5*/f32[1,1024]{1,0:T(1,128)S(1)}) custom-call(s32[1]{0:T(128)} %bitcast.4.bit_ref, f32[400,512]{1,0:T(8,128)S(1)} %get-tuple-element.33.head_ref, ...), custom_call_target="tpu_custom_call" | custom-call | tf_op jit(solution)/shard_map/front/pallas_call | solution.py:171
  73.5 1.4 %collective-permute-done.8 = f32[800,128]{1,0:T(8,128)S(1)} collective-permute-done((f32[800,128]{1,0:T(8,128)S(1)}, f32[800,128]{1,0:T(8,128)S(1)}, u32[]{:S(2)}, u32[]{:S(2)}) %collective-permute-start.8) | collective-permute-done | bytes 409632 | tf_op jit(solution)/shard_map/ppermute | solution.py:217
  75.1 7.3 %collective-permute-done.9 = f32[400,128]{1,0:T(8,128)S(1)} collective-permute-done((f32[400,128]{1,0:T(8,128)S(1)}, f32[400,128]{1,0:T(8,128)S(1)}, u32[]{:S(2)}, u32[]{:S(2)}) %collective-permute-start.9) | collective-permute-done | bytes 204832 | tf_op jit(solution)/shard_map/ppermute | solution.py:217
  82.5 4.6 %collective-permute-done.10 = f32[200,128]{1,0:T(8,128)S(1)} collective-permute-done((f32[200,128]{1,0:T(8,128)S(1)}, f32[200,128]{1,0:T(8,128)S(1)}, u32[]{:S(2)}, u32[]{:S(2)}) %collective-permute-start.10) | collective-permute-done | bytes 102432 | tf_op jit(solution)/shard_map/ppermute | solution.py:217
  87.2 3.7 %collective-permute-start.11 = (f32[200,128]{1,0:T(8,128)S(1)}, f32[200,128]{1,0:T(8,128)S(1)}, u32[]{:S(2)}, u32[]{:S(2)}) collective-permute-start(f32[200,128]{1,0:T(8,128)S(1)} %dynamic-slice_add_fusion.2), channel_id=1, source_target_pairs={{0,8},{1,9},{2,10},{3,11},{4,12},{5,13},{6,14},{7,15},{8,0},{9,1},... | collective-permute-start | bytes 307208 | tf_op jit(solution)/shard_map/ppermute | solution.py:217
  90.9 2.8 %collective-permute-done.11 = f32[200,128]{1,0:T(8,128)S(1)} collective-permute-done((f32[200,128]{1,0:T(8,128)S(1)}, f32[200,128]{1,0:T(8,128)S(1)}, u32[]{:S(2)}, u32[]{:S(2)}) %collective-permute-start.11) | collective-permute-done | bytes 102432 | tf_op jit(solution)/shard_map/ppermute | solution.py:217
  93.8 4.6 %collective-permute-done.12 = f32[200,128]{1,0:T(8,128)S(1)} collective-permute-done((f32[200,128]{1,0:T(8,128)S(1)}, f32[200,128]{1,0:T(8,128)S(1)}, u32[]{:S(2)}, u32[]{:S(2)}) %collective-permute-start.12) | collective-permute-done | bytes 102432 | tf_op jit(solution)/shard_map/ppermute | solution.py:217
  99.0 5.3 %collective-permute-done.13 = f32[400,128]{1,0:T(8,128)S(1)} collective-permute-done((f32[400,128]{1,0:T(8,128)S(1)}, f32[400,128]{1,0:T(8,128)S(1)}, u32[]{:S(2)}, u32[]{:S(2)}) %collective-permute-start.13) | collective-permute-done | bytes 204832 | tf_op jit(solution)/shard_map/ppermute | solution.py:217
  104.4 3.7 %back.3 = (f32[400,512]{1,0:T(8,128)}, f32[1,512]{1,0:T(1,128)}, f32[400,512]{1,0:T(8,128)}, f32[1,512]{1,0:T(1,128)}) custom-call(f32[400,512]{1,0:T(8,128)S(1)} %get-tuple-element.33.head_ref, f32[1,512]{1,0:T(1,128)S(1)} %copy-done.22, f32[408,512]{1,0:T(8,128)S(1)} %collective-permute-done.tail_ref, f32[1,512]{1,0:T(1,128)S(1)} %slice.4.tail_state_ref, ...), custom_call_target="tpu_custom_call" | custom-call | tf_op jit(solution)/shard_map/back/pallas_call | solution.py:191
  (75 shorter events, 16.0 us)
Async XLA Ops:
  15.4 24.5 %copy-start.3 = (f32[512,400]{0,1:T(8,128)S(1)}, f32[512,400]{0,1:T(8,128)}, u32[]{:S(2)}) copy-start(f32[512,400]{0,1:T(8,128)} %param.10) | copy-start | bytes 2457604
  15.4 24.5 %copy-start.5 = (f32[512,400]{0,1:T(8,128)S(1)}, f32[512,400]{0,1:T(8,128)}, u32[]{:S(2)}) copy-start(f32[512,400]{0,1:T(8,128)} %param.12) | copy-start | bytes 2457604
  15.4 24.5 %copy-start.11 = (s32[2,1024]{1,0:T(2,128)S(1)}, s32[2,1024]{1,0:T(2,128)}, u32[]{:S(2)}) copy-start(s32[2,1024]{1,0:T(2,128)} %src_ref.7) | copy-start | bytes 24580
  15.4 24.5 %copy-start.13 = (s32[2,1024]{1,0:T(2,128)S(1)}, s32[2,1024]{1,0:T(2,128)}, u32[]{:S(2)}) copy-start(s32[2,1024]{1,0:T(2,128)} %dst_ref.7) | copy-start | bytes 24580
  15.5 24.5 %copy-start.18 = (f32[512]{0:T(512)S(1)}, f32[512]{0:T(512)}, u32[]{:S(2)}) copy-start(f32[512]{0:T(512)} %param.11) | copy-start | bytes 6148
  15.5 24.5 %copy-start.19 = (f32[512]{0:T(512)S(1)}, f32[512]{0:T(512)}, u32[]{:S(2)}) copy-start(f32[512]{0:T(512)} %param.13) | copy-start | bytes 6148
  15.5 2.0 %collective-permute-start.1 = (f32[800,128]{1,0:T(8,128)S(1)}, f32[800,128]{1,0:T(8,128)}, u32[]{:S(2)}, u32[]{:S(2)}) collective-permute-start(f32[800,128]{1,0:T(8,128)S(1)} %get-tuple-element.37), channel_id=1, source_target_pairs={{0,1},{1,0},{2,3},{3,2},{4,5},{5,4},{6,7},{7,6},{8,9},{9,8},{10,11... | collective-permute-start | bytes 1228808 | tf_op jit(solution)/shard_map/ppermute | solution.py:217
  18.6 8.3 %collective-permute-start.2 = (f32[400,128]{1,0:T(8,128)S(1)}, f32[400,128]{1,0:T(8,128)S(1)}, u32[]{:S(2)}, u32[]{:S(2)}) collective-permute-start(f32[400,128]{1,0:T(8,128)S(1)} %constant_dynamic-slice_fusion.3), channel_id=1, source_target_pairs={{0,2},{1,3},{2,0},{3,1},{4,6},{5,7},{6,4},{7,5},{8,10},{9,11},{10,... | collective-permute-start | bytes 614408 | tf_op jit(solution)/shard_map/ppermute | solution.py:217
  27.0 4.7 %collective-permute-start.3 = (f32[200,128]{1,0:T(8,128)S(1)}, f32[200,128]{1,0:T(8,128)S(1)}, u32[]{:S(2)}, u32[]{:S(2)}) collective-permute-start(f32[200,128]{1,0:T(8,128)S(1)} %constant_dynamic-slice_fusion.2), channel_id=1, source_target_pairs={{0,4},{1,5},{2,6},{3,7},{4,0},{5,1},{6,2},{7,3},{8,12},{9,13},{10,... | collective-permute-start | bytes 307208 | tf_op jit(solution)/shard_map/ppermute | solution.py:217
  31.7 5.6 %collective-permute-start.4 = (f32[200,128]{1,0:T(8,128)S(1)}, f32[200,128]{1,0:T(8,128)S(1)}, u32[]{:S(2)}, u32[]{:S(2)}) collective-permute-start(f32[200,128]{1,0:T(8,128)S(1)} %dynamic-slice_add_fusion.3), channel_id=1, source_target_pairs={{0,8},{1,9},{2,10},{3,11},{4,12},{5,13},{6,14},{7,15},{8,0},{9,1},... | collective-permute-start | bytes 307208 | tf_op jit(solution)/shard_map/ppermute | solution.py:217
  38.0 9.1 %collective-permute-start.5 = (f32[200,128]{1,0:T(8,128)}, f32[200,128]{1,0:T(8,128)}, u32[]{:S(2)}, u32[]{:S(2)}) collective-permute-start(f32[200,128]{1,0:T(8,128)} %add.68), channel_id=1, source_target_pairs={{0,4},{1,5},{2,6},{3,7},{4,0},{5,1},{6,2},{7,3},{8,12},{9,13},{10,... | collective-permute-start | bytes 307208 | tf_op jit(solution)/shard_map/ppermute | solution.py:217
  42.9 23.7 %copy-start.20 = (f32[500]{0:T(512)S(1)}, f32[500]{0:T(512)}, u32[]{:S(2)}) copy-start(f32[500]{0:T(512)} %param.15) | copy-start | bytes 6004
  47.1 19.8 %copy-start.17 = (s32[2,2,512]{2,1,0:T(2,128)S(1)}, s32[2,2,512]{2,1,0:T(2,128)}, u32[]{:S(2)}) copy-start(s32[2,2,512]{2,1,0:T(2,128)} %neg_ref.3) | copy-start | bytes 24580
  47.1 19.8 %collective-permute-start = (f32[408,512]{1,0:T(8,128)}, f32[408,512]{1,0:T(8,128)S(1)}, u32[]{:S(2)}, u32[]{:S(2)}) collective-permute-start(f32[408,512]{1,0:T(8,128)} %get-tuple-element.35), channel_id=1, source_target_pairs={{0,1},{1,2},{2,3},{3,4},{4,5},{5,6},{6,7},{7,8},{8,9},{9,10},{10,1... | collective-permute-start | bytes 2506760 | tf_op jit(solution)/shard_map/ppermute | solution.py:270
  48.3 16.4 %collective-permute-start.6 = (f32[400,128]{1,0:T(8,128)S(1)}, f32[400,128]{1,0:T(8,128)S(1)}, u32[]{:S(2)}, u32[]{:S(2)}) collective-permute-start(f32[400,128]{1,0:T(8,128)S(1)} %maximum_select_fusion.2), channel_id=1, source_target_pairs={{0,2},{1,3},{2,0},{3,1},{4,6},{5,7},{6,4},{7,5},{8,10},{9,11},{10,... | collective-permute-start | bytes 614408 | tf_op jit(solution)/shard_map/ppermute | solution.py:217
  64.7 1.8 %collective-permute-start.7 = (f32[800,128]{1,0:T(8,128)S(1)}, f32[800,128]{1,0:T(8,128)S(1)}, u32[]{:S(2)}, u32[]{:S(2)}) collective-permute-start(f32[800,128]{1,0:T(8,128)S(1)} %maximum_select_fusion.mine_ref), channel_id=1, source_target_pairs={{0,1},{1,0},{2,3},{3,2},{4,5},{5,4},{6,7},{7,6},{8,9},{9,8},{10,11... | collective-permute-start | bytes 1228808 | tf_op jit(solution)/shard_map/ppermute | solution.py:217
  73.1 1.8 %collective-permute-start.8 = (f32[800,128]{1,0:T(8,128)S(1)}, f32[800,128]{1,0:T(8,128)S(1)}, u32[]{:S(2)}, u32[]{:S(2)}) collective-permute-start(f32[800,128]{1,0:T(8,128)S(1)} %get-tuple-element.49), channel_id=1, source_target_pairs={{0,1},{1,0},{2,3},{3,2},{4,5},{5,4},{6,7},{7,6},{8,9},{9,8},{10,11... | collective-permute-start | bytes 1228808 | tf_op jit(solution)/shard_map/ppermute | solution.py:217
  74.9 29.5 %copy-start.22 = (f32[1,512]{1,0:T(1,128)S(1)}, f32[1,512]{1,0:T(1,128)}, u32[]{:S(2)}) copy-start(f32[1,512]{1,0:T(1,128)} %copy-done.21) | copy-start | bytes 6148
  75.0 7.4 %collective-permute-start.9 = (f32[400,128]{1,0:T(8,128)S(1)}, f32[400,128]{1,0:T(8,128)S(1)}, u32[]{:S(2)}, u32[]{:S(2)}) collective-permute-start(f32[400,128]{1,0:T(8,128)S(1)} %constant_dynamic-slice_fusion.1), channel_id=1, source_target_pairs={{0,2},{1,3},{2,0},{3,1},{4,6},{5,7},{6,4},{7,5},{8,10},{9,11},{10,... | collective-permute-start | bytes 614408 | tf_op jit(solution)/shard_map/ppermute | solution.py:217
  82.4 4.7 %collective-permute-start.10 = (f32[200,128]{1,0:T(8,128)S(1)}, f32[200,128]{1,0:T(8,128)S(1)}, u32[]{:S(2)}, u32[]{:S(2)}) collective-permute-start(f32[200,128]{1,0:T(8,128)S(1)} %constant_dynamic-slice_fusion), channel_id=1, source_target_pairs={{0,4},{1,5},{2,6},{3,7},{4,0},{5,1},{6,2},{7,3},{8,12},{9,13},{10,... | collective-permute-start | bytes 307208 | tf_op jit(solution)/shard_map/ppermute | solution.py:217
  87.2 6.5 %collective-permute-start.11 = (f32[200,128]{1,0:T(8,128)S(1)}, f32[200,128]{1,0:T(8,128)S(1)}, u32[]{:S(2)}, u32[]{:S(2)}) collective-permute-start(f32[200,128]{1,0:T(8,128)S(1)} %dynamic-slice_add_fusion.2), channel_id=1, source_target_pairs={{0,8},{1,9},{2,10},{3,11},{4,12},{5,13},{6,14},{7,15},{8,0},{9,1},... | collective-permute-start | bytes 307208 | tf_op jit(solution)/shard_map/ppermute | solution.py:217
  93.7 4.7 %collective-permute-start.12 = (f32[200,128]{1,0:T(8,128)S(1)}, f32[200,128]{1,0:T(8,128)S(1)}, u32[]{:S(2)}, u32[]{:S(2)}) collective-permute-start(f32[200,128]{1,0:T(8,128)S(1)} %add.72), channel_id=1, source_target_pairs={{0,4},{1,5},{2,6},{3,7},{4,0},{5,1},{6,2},{7,3},{8,12},{9,13},{10,... | collective-permute-start | bytes 307208 | tf_op jit(solution)/shard_map/ppermute | solution.py:217
  98.5 5.8 %collective-permute-start.13 = (f32[400,128]{1,0:T(8,128)S(1)}, f32[400,128]{1,0:T(8,128)S(1)}, u32[]{:S(2)}, u32[]{:S(2)}) collective-permute-start(f32[400,128]{1,0:T(8,128)S(1)} %maximum_select_fusion.3), channel_id=1, source_target_pairs={{0,2},{1,3},{2,0},{3,1},{4,6},{5,7},{6,4},{7,5},{8,10},{9,11},{10,... | collective-permute-start | bytes 614408 | tf_op jit(solution)/shard_map/ppermute | solution.py:217
  104.3 3.8 %collective-permute-start.14 = (f32[800,128]{1,0:T(8,128)S(1)}, f32[800,128]{1,0:T(8,128)S(1)}, u32[]{:S(2)}, u32[]{:S(2)}) collective-permute-start(f32[800,128]{1,0:T(8,128)S(1)} %maximum_select_fusion.1.mine_ref), channel_id=1, source_target_pairs={{0,1},{1,0},{2,3},{3,2},{4,5},{5,4},{6,7},{7,6},{8,9},{9,8},{10,11... | collective-permute-start | bytes 1228808 | tf_op jit(solution)/shard_map/ppermute | solution.py:217
  (14 other events, 51.3 us)

commit v2 on v1

v2 whole, which is shorter than its diff:
```python
import functools

import jax
import jax.numpy as jnp
from jax import lax
from jax.experimental import pallas as pl
from jax.experimental.pallas import tpu as pltpu
from jax.sharding import PartitionSpec as P

neg_weight = 0.03125
learn_rate = 0.1
epsilon = 1e-06
LANES = 128
SPLITS = 3
PIECES = 3
LAG = 2
f32 = jnp.float32
bf16 = jnp.bfloat16
NN = ((1,), (0,))
NT = ((1,), (1,))
TN = ((0,), (0,))


def dot(left, right, dims):
    return lax.dot_general(left, right, (dims, ((), ())), preferred_element_type=f32)


def split(values):
    upper = values.astype(bf16)
    return upper, (values - upper.astype(f32)).astype(bf16)


def matches(index, count):
    return lax.broadcasted_iota(jnp.int32, (count, index.shape[1]), 0) == index


def one_hot(index, count):
    return jnp.where(matches(index, count), 1.0, 0.0).astype(bf16)


def complex_product(left, right):
    half = left.shape[0] // 2
    left_re, left_im = left[:half], left[half:]
    right_re, right_im = right[:half], right[half:]
    return jnp.concatenate(
        [left_re * right_re - left_im * right_im, left_re * right_im + left_im * right_re], axis=0
    )


def conj_product(grad, other):
    half = grad.shape[0] // 2
    grad_re, grad_im = grad[:half], grad[half:]
    other_re, other_im = other[:half], other[half:]
    return jnp.concatenate(
        [grad_re * other_re + grad_im * other_im, grad_im * other_re - grad_re * other_im], axis=0
    )


def adagrad(param, state, grad):
    new_state = state + jnp.sum(grad * grad, axis=0, keepdims=True) * (1.0 / grad.shape[0])
    return param - grad * (learn_rate / (jnp.sqrt(new_state) + epsilon)), new_state


def gather(upper, lower, selector):
    return dot(upper, selector, NN) + dot(lower, selector, NN)


def padded_lanes(count):
    return -(-count // LANES) * LANES


def spread(total, grad, at_step):
    width = grad.shape[0]
    groups = grad.shape[1] // LANES
    for g in range(groups):
        half, at = g // (groups // 2), (g % (groups // 2)) * width
        part = grad[:, g * LANES : (g + 1) * LANES]
        if at_step == 0:
            total[half, at : at + width, :] = part
        else:
            total[half, at : at + width, :] += part


def multiplicity(drawn, rows):
    return jnp.sum(jnp.where(matches(drawn, rows), 1.0, 0.0), axis=1, keepdims=True)


def span_grads(h, r, t, tail_hi, tail_rows, times, e, y_ref, q_ref, w_ref, pg_ref):
    query = complex_product(h, r)
    q_ref[:, e] = query
    positive = jnp.sum(query * t, axis=0, keepdims=True)
    pos_grad = -1.0 / (1.0 + jnp.exp(positive))
    pg_ref[:, e] = pos_grad
    scores = dot(tail_rows, query.astype(bf16), NN)
    half_weight = 0.5 * neg_weight
    neg_grad = (half_weight * jnp.tanh(0.5 * scores) + half_weight).astype(bf16)
    w = (neg_grad.astype(f32) * times).astype(bf16)
    w_ref[:, e] = w
    query_grad = dot(tail_hi, w, NN) + pos_grad * t
    y_ref[:, e] = conj_product(query_grad, r)
    return split(conj_product(query_grad, h))


def times_kernel(neg_ref, times_ref):
    steps, spans, _ = neg_ref.shape
    for step in range(steps):
        for s in range(spans):
            at = step * spans + s
            drawn = neg_ref[step, s : s + 1, :]
            times_ref[:, at : at + 1] = multiplicity(drawn, times_ref.shape[0])


def front_kernel(
    step, head_ref, rel_ref, tail_ref, src_ref, kind_ref, dst_ref, times_ref,
    keep_ref, send_ref, y_ref, q_ref, w_ref, pg_ref,
    head_hi, head_lo, tail_hi, tail_lo, rel_hi, rel_lo, rel_pad, total,
):
    rows = head_ref.shape[1]
    kinds = rel_ref.shape[1]
    rel_pad[...] = jnp.zeros_like(rel_pad)
    head_hi[...], head_lo[...] = split(head_ref[...])
    rel_pad[:, 0:kinds] = rel_ref[...]
    rel_hi[...], rel_lo[...] = split(rel_pad[...])
    tail_hi[...], tail_lo[...] = split(tail_ref[...])
    tail_rows = tail_ref[...].T.astype(bf16)
    spans = times_ref.shape[1] // src_ref.shape[0]
    span = src_ref.shape[1] // spans
    for s in range(spans):
        e = slice(s * span, (s + 1) * span)
        h = gather(head_hi[...], head_lo[...], one_hot(src_ref[step : step + 1, e], rows))
        kind_hot = one_hot(kind_ref[step : step + 1, e], rel_pad.shape[1])
        r = gather(rel_hi[...], rel_lo[...], kind_hot)
        t = gather(tail_hi[...], tail_lo[...], one_hot(dst_ref[step : step + 1, e], rows))
        at = step * spans + s
        x_hi, x_lo = span_grads(
            h, r, t, tail_hi[...], tail_rows, times_ref[:, at : at + 1],
            e, y_ref, q_ref, w_ref, pg_ref,
        )
        spread(total, dot(x_hi, kind_hot, NT) + dot(x_lo, kind_hot, NT), s)
    bit = lax.axis_index("blk") & 1
    keep_ref[...] = total[bit]
    send_ref[...] = total[1 - bit]


def pick_heads_kernel(step, head_ref, src_ref, h_ref):
    head_hi, head_lo = split(head_ref[...])
    src_hot = one_hot(src_ref[step : step + 1, :], head_ref.shape[1])
    h_ref[...] = gather(head_hi, head_lo, src_hot)


def pick_tails_kernel(step, width, dst_ref, *refs):
    *tail_refs, t_ref, tail_hi_ref, tail_rows_ref = refs
    rows = tail_refs[0].shape[1]
    tail = whole(tail_refs, width)
    tail_hi, tail_lo = split(tail)
    tail_hi_ref[...] = tail_hi
    tail_rows_ref[...] = tail.T.astype(bf16)
    t_ref[...] = gather(tail_hi, tail_lo, one_hot(dst_ref[step : step + 1, :], rows))


def updated_relations(rel_ref, state_ref, mine_ref, other_ref, rel_out, state_out, total, grad):
    width, kinds = rel_ref.shape
    groups = grad.shape[1] // LANES
    half_groups = groups // 2
    bit = lax.axis_index("blk") & 1
    total[bit] = mine_ref[...]
    total[1 - bit] = other_ref[...]
    for g in range(groups):
        half, at = g // half_groups, (g % half_groups) * width
        grad[:, g * LANES : (g + 1) * LANES] = total[half, at : at + width, :]
    rel_out[...], state_out[...] = adagrad(rel_ref[...], state_ref[...], grad[:, 0:kinds])


def main_kernel(
    step, rel_ref, state_ref, mine_ref, other_ref, kind_ref,
    h_ref, t_ref, tail_hi_ref, tail_rows_ref, times_ref,
    rel_out, state_out, keep_ref, send_ref, y_ref, q_ref, w_ref, pg_ref,
    rel_hi, rel_lo, rel_pad, total,
):
    kinds = rel_ref.shape[1]
    updated_relations(
        rel_ref, state_ref, mine_ref, other_ref, rel_out, state_out, total, rel_pad
    )
    rel_pad[...] = jnp.zeros_like(rel_pad)
    rel_pad[:, 0:kinds] = rel_out[...]
    rel_hi[...], rel_lo[...] = split(rel_pad[...])
    spans = times_ref.shape[1] // kind_ref.shape[0]
    span = h_ref.shape[1] // spans
    for s in range(spans):
        e = slice(s * span, (s + 1) * span)
        kind_hot = one_hot(kind_ref[step : step + 1, e], rel_pad.shape[1])
        r = gather(rel_hi[...], rel_lo[...], kind_hot)
        x_hi, x_lo = span_grads(
            h_ref[:, e], r, t_ref[:, e], tail_hi_ref[...], tail_rows_ref[...],
            times_ref[:, step * spans + s : step * spans + s + 1], e, y_ref, q_ref, w_ref, pg_ref,
        )
        spread(total, dot(x_hi, kind_hot, NT) + dot(x_lo, kind_hot, NT), s)
    bit = lax.axis_index("blk") & 1
    keep_ref[...] = total[bit]
    send_ref[...] = total[1 - bit]


def whole(pieces, width):
    return jnp.concatenate([piece[...] for piece in pieces], axis=0)[0:width]


def back_kernel(
    step, parts, head_ref, head_state_ref, tail_state_ref, src_ref, dst_ref,
    y_ref, q_ref, w_ref, pg_ref, *refs,
):
    tail_refs, head_out, head_state_out, outs = refs[:parts], *refs[parts : parts + 2], refs[parts + 2 :]
    width, rows = head_ref.shape
    y_hi, y_lo = split(y_ref[...])
    src_hot = one_hot(src_ref[step : step + 1, :], rows)
    head_grad = dot(y_hi, src_hot, NT) + dot(y_lo, src_hot, NT)
    head_out[...], head_state_out[...] = adagrad(head_ref[...], head_state_ref[...], head_grad)
    query = q_ref[...]
    p_hi, p_lo = split(query * pg_ref[...])
    dst_hot = one_hot(dst_ref[step : step + 1, :], rows)
    tail_grad = (
        dot(query.astype(bf16), w_ref[...], NT) + dot(p_hi, dst_hot, NT) + dot(p_lo, dst_hot, NT)
    )
    tail, state = adagrad(whole(tail_refs, width), tail_state_ref[...], tail_grad)
    if len(outs) == 2:
        outs[0][...], outs[1][...] = tail, state
        return
    joined = jnp.concatenate([tail, jnp.broadcast_to(state, (8, rows))], axis=0)
    at = 0
    for piece in outs:
        piece[...] = joined[at : at + piece.shape[0]]
        at += piece.shape[0]


VMEM = pl.BlockSpec(memory_space=pltpu.VMEM)


def settings(megabytes):
    return pltpu.CompilerParams(vmem_limit_bytes=megabytes * 1024 * 1024)


def shape(*dims, dtype=f32):
    return jax.ShapeDtypeStruct(dims, dtype)


def cost(products, bytes_accessed):
    return pl.CostEstimate(
        flops=2 * products, bytes_accessed=bytes_accessed, transcendentals=0
    )


def lanes_of(relations):
    return -(-relations.shape[1] // (2 * LANES)) * 2 * LANES


def made_shapes(width, rows, edges, half):
    return [
        shape(half, LANES), shape(half, LANES), shape(width, edges), shape(width, edges),
        shape(rows, edges, dtype=bf16), shape(1, edges),
    ]


def multiplicities(rows, negatives):
    steps, spans, drawn = negatives.shape
    return pl.pallas_call(
        times_kernel,
        out_shape=shape(rows, steps * spans),
        in_specs=[VMEM],
        out_specs=VMEM,
        compiler_params=settings(8),
        cost_estimate=cost(4 * steps * spans * drawn * rows * 400, 4 * rows * 128),
        name="times",
    )(negatives)


def front(step, heads, tails, relations, sources, kinds, targets, times):
    width, rows = heads.shape
    edges = sources.shape[1]
    lanes = lanes_of(relations)
    half = width * lanes // LANES // 2
    return pl.pallas_call(
        functools.partial(front_kernel, step),
        out_shape=made_shapes(width, rows, edges, half),
        in_specs=[VMEM] * 7,
        out_specs=[VMEM] * 6,
        scratch_shapes=[pltpu.VMEM((width, rows), bf16)] * 4
        + [pltpu.VMEM((width, lanes), bf16)] * 2
        + [pltpu.VMEM((width, lanes), f32), pltpu.VMEM((2, half, LANES), f32)],
        compiler_params=settings(24),
        name="front",
    )(heads, relations, tails, sources, kinds, targets, times)


def pick_heads(step, heads, sources):
    width, rows = heads.shape
    edges = sources.shape[1]
    return pl.pallas_call(
        functools.partial(pick_heads_kernel, step),
        out_shape=shape(width, edges),
        in_specs=[VMEM] * 2,
        out_specs=VMEM,
        compiler_params=settings(16),
        cost_estimate=cost(2 * edges * rows * width, 4 * width * (rows + edges)),
        name="pick_heads",
    )(heads, sources)


def pick_tails(step, width, tails, targets):
    rows = tails[0].shape[1]
    edges = targets.shape[1]
    return pl.pallas_call(
        functools.partial(pick_tails_kernel, step, width),
        out_shape=[
            shape(width, edges), shape(width, rows, dtype=bf16), shape(rows, width, dtype=bf16)
        ],
        in_specs=[VMEM] * (1 + len(tails)),
        out_specs=[VMEM] * 3,
        compiler_params=settings(16),
        cost_estimate=cost(2 * edges * rows * width, 4 * width * (rows + edges)),
        name="pick_tails",
    )(targets, *tails)


def main(step, relations, state, mine, other, kinds, picked):
    width = relations.shape[0]
    edges = kinds.shape[1]
    rows = picked[2].shape[1]
    lanes = lanes_of(relations)
    half = width * lanes // LANES // 2
    return pl.pallas_call(
        functools.partial(main_kernel, step),
        out_shape=[shape(*relations.shape), shape(*state.shape)]
        + made_shapes(width, rows, edges, half),
        in_specs=[VMEM] * 10,
        out_specs=[VMEM] * 8,
        scratch_shapes=[pltpu.VMEM((width, lanes), bf16)] * 2
        + [pltpu.VMEM((width, lanes), f32), pltpu.VMEM((2, half, LANES), f32)],
        compiler_params=settings(24),
        name="main",
    )(relations, state, mine, other, kinds, *picked)


def back(step, joined, heads, head_state, tails, tail_state, sources, targets, made):
    width, rows = heads.shape
    outs = [shape(width, rows), shape(1, rows)]
    if joined:
        full = -(-(width + 8) // (8 * PIECES)) * 8
        sizes = [full] * (PIECES - 1) + [width + 8 - full * (PIECES - 1)]
        outs += [shape(size, rows) for size in sizes]
    else:
        outs += [shape(width, rows), shape(1, rows)]
    return pl.pallas_call(
        functools.partial(back_kernel, step, len(tails)),
        out_shape=outs,
        in_specs=[VMEM] * (9 + len(tails)),
        out_specs=[VMEM] * len(outs),
        compiler_params=settings(24),
        cost_estimate=cost(5 * rows * width * sources.shape[1], 4 * width * 6 * rows),
        name="back",
    )(heads, head_state, tail_state, sources, targets, *made, *tails)


def update_relations(relations, state, mine, other):
    width = relations.shape[0]
    return pl.pallas_call(
        updated_relations,
        out_shape=[shape(*relations.shape), shape(*state.shape)],
        in_specs=[VMEM] * 4,
        out_specs=[VMEM] * 2,
        scratch_shapes=[
            pltpu.VMEM((2,) + mine.shape, f32), pltpu.VMEM((width, lanes_of(relations)), f32)
        ],
        compiler_params=settings(16),
        name="relations",
    )(relations, state, mine, other)


def swap(value, distance):
    count = lax.axis_size("blk")
    return lax.ppermute(value, "blk", [(i, i ^ distance) for i in range(count)])


def place(level, half):
    bit = (lax.axis_index("blk") >> level) & 1
    return pl.multiple_of(bit * half, 8), pl.multiple_of((1 - bit) * half, 8)


def halve_kernel(level, keep_ref, got_ref, kept_ref, sent_ref):
    half = kept_ref.shape[0]
    own, others = place(level, half)
    kept_ref[...] = keep_ref[pl.ds(own, half), :] + got_ref[pl.ds(own, half), :]
    sent_ref[...] = keep_ref[pl.ds(others, half), :] + got_ref[pl.ds(others, half), :]


def join_kernel(level, mine_ref, got_ref, joined_ref):
    half = mine_ref.shape[0]
    own, others = place(level, half)
    joined_ref[pl.ds(own, half), :] = mine_ref[...]
    joined_ref[pl.ds(others, half), :] = got_ref[...]


def halve(level, keep, got):
    half = shape(keep.shape[0] // 2, keep.shape[1])
    return pl.pallas_call(
        functools.partial(halve_kernel, level),
        out_shape=[half, half],
        in_specs=[VMEM] * 2,
        out_specs=[VMEM] * 2,
        compiler_params=settings(4),
        cost_estimate=cost(keep.size // 2, 16 * keep.size),
        name="halve",
    )(keep, got)


def join(level, mine, got):
    return pl.pallas_call(
        functools.partial(join_kernel, level),
        out_shape=shape(mine.shape[0] * 2, mine.shape[1]),
        in_specs=[VMEM] * 2,
        out_specs=VMEM,
        compiler_params=settings(4),
        cost_estimate=cost(mine.size, 16 * mine.size),
        name="join",
    )(mine, got)


def reduce_halves(keep, send, beside, pieces):
    levels = (lax.axis_size("blk") - 1).bit_length()
    splits = min(levels, SPLITS)
    waiting, rolled, count = list(pieces), [], 0

    def exchange(value, distance):
        nonlocal waiting, count
        due = count - LAG
        count += 1
        if 0 <= due < len(rolled):
            value, rolled[due] = lax.optimization_barrier((value, rolled[due]))
        if rolled and waiting:
            value, waiting = lax.optimization_barrier((value, waiting))
        got = swap(value, distance)
        if waiting:
            rolled.append(roll(waiting.pop(0)))
        return value, got

    got = swap(send, 1)
    for level in range(1, splits):
        keep, send = halve(level, keep, got)
        if level == 2:
            send, beside = lax.optimization_barrier((send, beside))
        send, got = exchange(send, 1 << level)
    total = keep + got
    for level in range(splits, levels):
        total, got = exchange(total, 1 << level)
        total = total + got
    for level in reversed(range(1, splits)):
        total, got = exchange(total, 1 << level)
        total = join(level, total, got)
    total, got = exchange(total, 1)
    rolled += [roll(piece) for piece in waiting]
    return total, got, beside, rolled


def roll(value):
    count = lax.axis_size("blk")
    return lax.ppermute(value, "blk", [(i, (i + 1) % count) for i in range(count)])


def per_device(
    heads,
    head_state,
    tails,
    tail_state,
    relations,
    rel_state,
    edge_src,
    edge_rel,
    edge_dst,
    negatives,
):
    heads, tails, relations = heads.T, [tails.T], relations.T
    head_state, tail_state, rel_state = head_state[None], tail_state[None], rel_state[None]
    width = heads.shape[0]
    steps = edge_src.shape[0]
    mine = other = None
    times = multiplicities(heads.shape[1], negatives)
    for step in range(steps):
        joined = step < steps - 1
        if step == 0:
            keep, send, *made = front(
                step, heads, tails[0], relations, edge_src, edge_rel, edge_dst, times
            )
        else:
            h = pick_heads(step, heads, edge_src)
            picked = (h, *pick_tails(step, width, tails, edge_dst), times)
            relations, rel_state, keep, send, *made = main(
                step, relations, rel_state, mine, other, edge_rel, picked
            )
        heads, head_state, *rest = back(
            step, joined, heads, head_state, tails, tail_state, edge_src, edge_dst, made
        )
        beside, pieces = ((heads,), rest) if joined else ((heads, *rest), [])
        mine, other, beside, tails = reduce_halves(keep, send, beside, pieces)
        if joined:
            tail_state = tails[-1][-8:-7]
        else:
            heads, *rest = beside
    tails, tail_state = rest
    relations, rel_state = update_relations(relations, rel_state, mine, other)
    return (heads.T, head_state[0], tails.T, tail_state[0], relations.T, rel_state[0])


def solution(mesh):
    in_specs = (
        P(("groups", "blk"), None),
        P(("groups", "blk")),
        P(("groups", "blk"), None),
        P(("groups", "blk")),
        P("groups", None),
        P("groups"),
        P(None, ("groups", "blk")),
        P(None, ("groups", "blk")),
        P(None, ("groups", "blk")),
        P(None, ("groups", "blk"), None),
    )
    out_specs = (
        P(("groups", "blk"), None),
        P(("groups", "blk")),
        P(("groups", "blk"), None),
        P(("groups", "blk")),
        P("groups", None),
        P("groups"),
    )
    return jax.shard_map(
        per_device, mesh=mesh, in_specs=in_specs, out_specs=out_specs, check_vma=False
    )
```

time: 110 us -> 90.3 us (0.82)
  local copies, waits for them, and re-layouts: 12.1 us -> 1.09 us
  waiting for transfers between devices: 54.9 us -> 46.8 us
  other arithmetic: 3.05 us -> 0.06 us
  starting transfers between devices: 17.1 us -> 19.4 us
    unnamed x46 -> x20, local copies, waits for them, and re-layouts: 12 us -> 1.09 us
    ppermute x14, waiting for transfers between devices: 54.9 us -> 45.4 us  [swap(): return lax.ppermute(value, 'blk', [(i, i ^ distance) for i in range(count)])]
    ppermute x14, starting transfers between devices: 17.1 us -> 19.3 us  [swap(): return lax.ppermute(value, 'blk', [(i, i ^ distance) for i in range(count)])]
    add x8 -> x4, other arithmetic: 1.83 us -> 0.06 us  [the longest x2 0.03 us: reduce_halves(): total = total + got]
    ppermute x1 -> x3, waiting for transfers between devices: 0.01 us -> 1.41 us  [roll(): lax.ppermute(value, 'blk', [(i, (i + 1) % count) for i in range(count)])]
    select_n x4 -> x0, other arithmetic: 1.22 us -> none  [reduce_halves(): jnp.where(bit == 0, jnp.concatenate([current, got], 0), jnp.concatenate([...]
    pallas_call x6 -> x16, Pallas kernels: 21.2 us -> 21.9 us  [the longest x2 6.45 us: back(): pl.pallas_call(functools.partial(back_kernel, step, len(tails)), out_shap...]
  transfers between devices with their start and end apart: 15 -> 17, of which waited for: 12 -> 14; matrix products, arithmetic and copies ran while one was open for 1% -> 0% of each run, Pallas kernels for 7% -> 10%
where the time goes in v2:
time: 90.3 us; the launch traced here: 90.1 us
  waiting for transfers between devices  46.8 us (52%)
  Pallas kernels  21.9 us (24%)
  starting transfers between devices  19.4 us (21%)
  local copies, waits for them, and re-layouts  1.09 us (1%)
    ppermute x14, waiting for transfers between devices, swap(): return lax.ppermute(value, 'blk', [(i, i ^ distance) for i in range(count)])  45.4 us
    ppermute x14, starting transfers between devices, swap(): return lax.ppermute(value, 'blk', [(i, i ^ distance) for i in range(count)])  19.3 us
    pallas_call x2, Pallas kernels, back(): pl.pallas_call(functools.partial(back_kernel, step, len(tails)), out_shap...  6.45 us
    pallas_call x1, Pallas kernels, front(): pl.pallas_call(functools.partial(front_kernel, step), out_shape=made_shap...  6.2 us
    pallas_call x1, Pallas kernels, main(): pl.pallas_call(functools.partial(main_kernel, step), out_shape=[shape(*re...  5 us
  transfers between devices with their start and end apart: 17, of which 14 were waited for; matrix products, arithmetic and copies ran while one was open for 0% of the time, Pallas kernels for 10%

profile of v2, /device:TPU:0, one launch (start us, length us, event | category | flops | bytes accessed | tf_op | source)
XLA Modules:
  0.0 90.1 jit_solution(3708498750886390763)
XLA Ops:
  2.3 6.2 %front.1 = (f32[800,128]{1,0:T(8,128)S(1)}, f32[800,128]{1,0:T(8,128)S(1)}, f32[400,1024]{1,0:T(8,128)S(1)}, f32[400,1024]{1,0:T(8,128)S(1)}, bf16[512,1024]{1,0:T(8,128)(2,1)S(1)}, /*index=5*/f32[1,1024]{1,0:T(1,128)S(1)}) custom-call(f32[400,512]{1,0:T(8,128)S(1)} %bitcast.14, f32[400,500]{1,0:T(8,128)S(1)} %bitcast.12, f32[400,512]{1,0:T(8,128)S(1)} %bitcast.16, ...), custom_call_target="tpu_custom_call" | custom-call | tf_op jit(solution)/shard_map/front/pallas_call | solution.py:280
  9.1 1.4 %collective-permute-done.got_ref = f32[800,128]{1,0:T(8,128)S(1)} collective-permute-done((f32[800,128]{1,0:T(8,128)S(1)}, f32[800,128]{1,0:T(8,128)S(1)}, u32[]{:S(2)}, u32[]{:S(2)}) %collective-permute-start) | collective-permute-done | bytes 409632 | tf_op jit(solution)/shard_map/ppermute | solution.py:379
  10.5 2.9 %collective-permute-start.1 = (f32[400,128]{1,0:T(8,128)S(1)}, f32[400,128]{1,0:T(8,128)S(1)}, u32[]{:S(2)}, u32[]{:S(2)}) collective-permute-start(f32[400,128]{1,0:T(8,128)S(1)} %get-tuple-element.61), channel_id=1, source_target_pairs={{0,2},{1,3},{2,0},{3,1},{4,6},{5,7},{6,4},{7,5},{8,10},{9,11},{10,... | collective-permute-start | bytes 614408 | tf_op jit(solution)/shard_map/ppermute | solution.py:379
  13.4 2.8 %back.2 = (f32[400,512]{1,0:T(8,128)S(1)}, f32[1,512]{1,0:T(1,128)S(1)}, f32[136,512]{1,0:T(8,128)S(1)}, f32[136,512]{1,0:T(8,128)S(1)}, f32[136,512]{1,0:T(8,128)S(1)}) custom-call(f32[400,512]{1,0:T(8,128)S(1)} %bitcast.15, f32[1,512]{1,0:T(1,128)S(1)} %bitcast.19, f32[1,512]{1,0:T(1,128)S(1)} %bitcast.20, s32[2,1024]{1,0:T(2,128)S(1)} %copy-done.4, ...), custom_call_target="tpu_custom_call" | custom-call | flops 2097152000 | bytes 4915200 | tf_op jit(solution)/shard_map/back/pallas_call | solution.py:351
  16.3 2.6 %collective-permute-done.1.got_ref = f32[400,128]{1,0:T(8,128)S(1)} collective-permute-done((f32[400,128]{1,0:T(8,128)S(1)}, f32[400,128]{1,0:T(8,128)S(1)}, u32[]{:S(2)}, u32[]{:S(2)}) %collective-permute-start.1) | collective-permute-done | bytes 204832 | tf_op jit(solution)/shard_map/ppermute | solution.py:379
  18.9 1.8 %collective-permute-start.2 = (f32[200,128]{1,0:T(8,128)S(1)}, f32[200,128]{1,0:T(8,128)S(1)}, u32[]{:S(2)}, u32[]{:S(2)}) collective-permute-start(f32[200,128]{1,0:T(8,128)S(1)} %get-tuple-element.72), channel_id=1, source_target_pairs={{0,4},{1,5},{2,6},{3,7},{4,0},{5,1},{6,2},{7,3},{8,12},{9,13},{10,... | collective-permute-start | bytes 307208 | tf_op jit(solution)/shard_map/ppermute | solution.py:379
  20.7 2.9 %collective-permute-done.2 = f32[200,128]{1,0:T(8,128)S(1)} collective-permute-done((f32[200,128]{1,0:T(8,128)S(1)}, f32[200,128]{1,0:T(8,128)S(1)}, u32[]{:S(2)}, u32[]{:S(2)}) %collective-permute-start.2) | collective-permute-done | bytes 102432 | tf_op jit(solution)/shard_map/ppermute | solution.py:379
  23.6 1.4 %collective-permute-done.3.refs_0_ = f32[136,512]{1,0:T(8,128)S(1)} collective-permute-done((f32[136,512]{1,0:T(8,128)S(1)}, f32[136,512]{1,0:T(8,128)S(1)}, u32[]{:S(2)}, u32[]{:S(2)}) %collective-permute-start.3) | collective-permute-done | bytes 278560 | tf_op jit(solution)/shard_map/ppermute | solution.py:464
  25.0 1.6 %collective-permute-start.4 = (f32[200,128]{1,0:T(8,128)S(1)}, f32[200,128]{1,0:T(8,128)S(1)}, u32[]{:S(2)}, u32[]{:S(2)}) collective-permute-start(f32[200,128]{1,0:T(8,128)S(1)} %add.12), channel_id=1, source_target_pairs={{0,8},{1,9},{2,10},{3,11},{4,12},{5,13},{6,14},{7,15},{8,0},{9,1},... | collective-permute-start | bytes 307208 | tf_op jit(solution)/shard_map/ppermute | solution.py:379
  26.7 5.0 %collective-permute-done.4 = f32[200,128]{1,0:T(8,128)S(1)} collective-permute-done((f32[200,128]{1,0:T(8,128)S(1)}, f32[200,128]{1,0:T(8,128)S(1)}, u32[]{:S(2)}, u32[]{:S(2)}) %collective-permute-start.4) | collective-permute-done | bytes 102432 | tf_op jit(solution)/shard_map/ppermute | solution.py:379
  31.8 4.6 %collective-permute-done.6.got_ref = f32[200,128]{1,0:T(8,128)S(1)} collective-permute-done((f32[200,128]{1,0:T(8,128)S(1)}, f32[200,128]{1,0:T(8,128)S(1)}, u32[]{:S(2)}, u32[]{:S(2)}) %collective-permute-start.6) | collective-permute-done | bytes 102432 | tf_op jit(solution)/shard_map/ppermute | solution.py:379
  36.5 7.2 %collective-permute-start.8 = (f32[400,128]{1,0:T(8,128)S(1)}, f32[400,128]{1,0:T(8,128)S(1)}, u32[]{:S(2)}, u32[]{:S(2)}) collective-permute-start(f32[400,128]{1,0:T(8,128)S(1)} %join.4.mine_ref), channel_id=1, source_target_pairs={{0,2},{1,3},{2,0},{3,1},{4,6},{5,7},{6,4},{7,5},{8,10},{9,11},{10,... | collective-permute-start | bytes 614408 | tf_op jit(solution)/shard_map/ppermute | solution.py:379
  43.7 4.4 %collective-permute-done.8.got_ref = f32[400,128]{1,0:T(8,128)S(1)} collective-permute-done((f32[400,128]{1,0:T(8,128)S(1)}, f32[400,128]{1,0:T(8,128)S(1)}, u32[]{:S(2)}, u32[]{:S(2)}) %collective-permute-start.8) | collective-permute-done | bytes 204832 | tf_op jit(solution)/shard_map/ppermute | solution.py:379
  50.5 5.0 %main.1 = (f32[400,500]{1,0:T(8,128)S(1)}, f32[1,500]{1,0:T(1,128)S(1)}, f32[800,128]{1,0:T(8,128)S(1)}, f32[800,128]{1,0:T(8,128)S(1)}, f32[400,1024]{1,0:T(8,1...) custom-call(f32[400,500]{1,0:T(8,128)S(1)} %bitcast.13, ...), custom_call_target="tpu_custom_call" | custom-call | tf_op jit(solution)/shard_map/main/pallas_call | solution.py:329
  56.1 1.4 %collective-permute-done.10.got_ref = f32[800,128]{1,0:T(8,128)S(1)} collective-permute-done((f32[800,128]{1,0:T(8,128)S(1)}, f32[800,128]{1,0:T(8,128)S(1)}, u32[]{:S(2)}, u32[]{:S(2)}) %collective-permute-start.10) | collective-permute-done | bytes 409632 | tf_op jit(solution)/shard_map/ppermute | solution.py:379
  57.5 1.8 %collective-permute-start.11 = (f32[400,128]{1,0:T(8,128)S(1)}, f32[400,128]{1,0:T(8,128)S(1)}, u32[]{:S(2)}, u32[]{:S(2)}) collective-permute-start(f32[400,128]{1,0:T(8,128)S(1)} %get-tuple-element.90), channel_id=1, source_target_pairs={{0,2},{1,3},{2,0},{3,1},{4,6},{5,7},{6,4},{7,5},{8,10},{9,11},{10,... | collective-permute-start | bytes 614408 | tf_op jit(solution)/shard_map/ppermute | solution.py:379
  59.4 3.7 %back.3 = (f32[400,512]{1,0:T(8,128)}, f32[1,512]{1,0:T(1,128)}, f32[400,512]{1,0:T(8,128)}, f32[1,512]{1,0:T(1,128)}) custom-call(f32[400,512]{1,0:T(8,128)S(1)} %get-tuple-element.68.head_ref, f32[1,512]{1,0:T(1,128)S(1)} %get-tuple-element.92.head_state_ref, f32[1,512]{1,0:T(1,128)S(1)} %slice.3.tail_state_ref, s32[2,1024]{1,0:T(2,128)S(1)} %copy-done.4, ...), custom_call_target="tpu_custom_call" | custom-call | flops 2097152000 | bytes 4915200 | tf_op jit(solution)/shard_map/back/pallas_call | solution.py:351
  63.0 1.9 %collective-permute-done.11.got_ref = f32[400,128]{1,0:T(8,128)S(1)} collective-permute-done((f32[400,128]{1,0:T(8,128)S(1)}, f32[400,128]{1,0:T(8,128)S(1)}, u32[]{:S(2)}, u32[]{:S(2)}) %collective-permute-start.11) | collective-permute-done | bytes 204832 | tf_op jit(solution)/shard_map/ppermute | solution.py:379
  65.6 4.1 %collective-permute-done.12 = f32[200,128]{1,0:T(8,128)S(1)} collective-permute-done((f32[200,128]{1,0:T(8,128)S(1)}, f32[200,128]{1,0:T(8,128)S(1)}, u32[]{:S(2)}, u32[]{:S(2)}) %collective-permute-start.12) | collective-permute-done | bytes 102432 | tf_op jit(solution)/shard_map/ppermute | solution.py:379
  69.8 6.6 %collective-permute-done.13 = f32[200,128]{1,0:T(8,128)S(1)} collective-permute-done((f32[200,128]{1,0:T(8,128)S(1)}, f32[200,128]{1,0:T(8,128)S(1)}, u32[]{:S(2)}, u32[]{:S(2)}) %collective-permute-start.13) | collective-permute-done | bytes 102432 | tf_op jit(solution)/shard_map/ppermute | solution.py:379
  76.5 4.6 %collective-permute-done.14.got_ref = f32[200,128]{1,0:T(8,128)S(1)} collective-permute-done((f32[200,128]{1,0:T(8,128)S(1)}, f32[200,128]{1,0:T(8,128)S(1)}, u32[]{:S(2)}, u32[]{:S(2)}) %collective-permute-start.14) | collective-permute-done | bytes 102432 | tf_op jit(solution)/shard_map/ppermute | solution.py:379
  81.2 1.8 %collective-permute-start.15 = (f32[400,128]{1,0:T(8,128)S(1)}, f32[400,128]{1,0:T(8,128)S(1)}, u32[]{:S(2)}, u32[]{:S(2)}) collective-permute-start(f32[400,128]{1,0:T(8,128)S(1)} %join.6.mine_ref), channel_id=1, source_target_pairs={{0,2},{1,3},{2,0},{3,1},{4,6},{5,7},{6,4},{7,5},{8,10},{9,11},{10,... | collective-permute-start | bytes 614408 | tf_op jit(solution)/shard_map/ppermute | solution.py:379
  83.0 4.0 %collective-permute-done.15.got_ref = f32[400,128]{1,0:T(8,128)S(1)} collective-permute-done((f32[400,128]{1,0:T(8,128)S(1)}, f32[400,128]{1,0:T(8,128)S(1)}, u32[]{:S(2)}, u32[]{:S(2)}) %collective-permute-start.15) | collective-permute-done | bytes 204832 | tf_op jit(solution)/shard_map/ppermute | solution.py:379
  87.2 1.7 %collective-permute-done.16.other_ref = f32[800,128]{1,0:T(8,128)S(1)} collective-permute-done((f32[800,128]{1,0:T(8,128)S(1)}, f32[800,128]{1,0:T(8,128)S(1)}, u32[]{:S(2)}, u32[]{:S(2)}) %collective-permute-start.16) | collective-permute-done | bytes 409632 | tf_op jit(solution)/shard_map/ppermute | solution.py:379
  (51 shorter events, 7.6 us)
Async XLA Ops:
  0.6 1.4 %copy-start = (f32[500,400]{0,1:T(8,128)S(1)}, f32[500,400]{0,1:T(8,128)}, u32[]{:S(2)}) copy-start(f32[500,400]{0,1:T(8,128)} %param.14) | copy-start | bytes 2400004
  0.7 1.6 %copy-start.2 = (f32[512,400]{0,1:T(8,128)S(1)}, f32[512,400]{0,1:T(8,128)}, u32[]{:S(2)}) copy-start(f32[512,400]{0,1:T(8,128)} %param.12) | copy-start | bytes 2457604
  0.7 1.6 %copy-start.4 = (s32[2,1024]{1,0:T(2,128)S(1)}, s32[2,1024]{1,0:T(2,128)}, u32[]{:S(2)}) copy-start(s32[2,1024]{1,0:T(2,128)} %src_ref.7) | copy-start | bytes 24580
  0.7 1.6 %copy-start.3 = (s32[2,1024]{1,0:T(2,128)S(1)}, s32[2,1024]{1,0:T(2,128)}, u32[]{:S(2)}) copy-start(s32[2,1024]{1,0:T(2,128)} %kind_ref.3) | copy-start | bytes 24580
  0.7 1.6 %copy-start.5 = (s32[2,1024]{1,0:T(2,128)S(1)}, s32[2,1024]{1,0:T(2,128)}, u32[]{:S(2)}) copy-start(s32[2,1024]{1,0:T(2,128)} %dst_ref.7) | copy-start | bytes 24580
  2.3 11.1 %copy-start.8 = (f32[512]{0:T(512)S(1)}, f32[512]{0:T(512)}, u32[]{:S(2)}) copy-start(f32[512]{0:T(512)} %param.11) | copy-start | bytes 6148
  2.3 11.1 %copy-start.9 = (f32[512]{0:T(512)S(1)}, f32[512]{0:T(512)}, u32[]{:S(2)}) copy-start(f32[512]{0:T(512)} %param.13) | copy-start | bytes 6148
  8.5 1.9 %collective-permute-start = (f32[800,128]{1,0:T(8,128)S(1)}, f32[800,128]{1,0:T(8,128)S(1)}, u32[]{:S(2)}, u32[]{:S(2)}) collective-permute-start(f32[800,128]{1,0:T(8,128)S(1)} %get-tuple-element.59), channel_id=1, source_target_pairs={{0,1},{1,0},{2,3},{3,2},{4,5},{5,4},{6,7},{7,6},{8,9},{9,8},{10,11... | collective-permute-start | bytes 1228808 | tf_op jit(solution)/shard_map/ppermute | solution.py:379
  10.5 8.4 %collective-permute-start.1 = (f32[400,128]{1,0:T(8,128)S(1)}, f32[400,128]{1,0:T(8,128)S(1)}, u32[]{:S(2)}, u32[]{:S(2)}) collective-permute-start(f32[400,128]{1,0:T(8,128)S(1)} %get-tuple-element.61), channel_id=1, source_target_pairs={{0,2},{1,3},{2,0},{3,1},{4,6},{5,7},{6,4},{7,5},{8,10},{9,11},{10,... | collective-permute-start | bytes 614408 | tf_op jit(solution)/shard_map/ppermute | solution.py:379
  16.2 8.8 %collective-permute-start.3 = (f32[136,512]{1,0:T(8,128)S(1)}, f32[136,512]{1,0:T(8,128)S(1)}, u32[]{:S(2)}, u32[]{:S(2)}) collective-permute-start(f32[136,512]{1,0:T(8,128)S(1)} %get-tuple-element.73), channel_id=1, source_target_pairs={{0,1},{1,2},{2,3},{3,4},{4,5},{5,6},{6,7},{7,8},{8,9},{9,10},{10,1... | collective-permute-start | bytes 835592 | tf_op jit(solution)/shard_map/ppermute | solution.py:464
  18.9 4.7 %collective-permute-start.2 = (f32[200,128]{1,0:T(8,128)S(1)}, f32[200,128]{1,0:T(8,128)S(1)}, u32[]{:S(2)}, u32[]{:S(2)}) collective-permute-start(f32[200,128]{1,0:T(8,128)S(1)} %get-tuple-element.72), channel_id=1, source_target_pairs={{0,4},{1,5},{2,6},{3,7},{4,0},{5,1},{6,2},{7,3},{8,12},{9,13},{10,... | collective-permute-start | bytes 307208 | tf_op jit(solution)/shard_map/ppermute | solution.py:379
  20.7 11.1 %collective-permute-start.5 = (f32[136,512]{1,0:T(8,128)S(1)}, f32[136,512]{1,0:T(8,128)S(1)}, u32[]{:S(2)}, u32[]{:S(2)}) collective-permute-start(f32[136,512]{1,0:T(8,128)S(1)} %get-tuple-element.77), channel_id=1, source_target_pairs={{0,1},{1,2},{2,3},{3,4},{4,5},{5,6},{6,7},{7,8},{8,9},{9,10},{10,1... | collective-permute-start | bytes 835592 | tf_op jit(solution)/shard_map/ppermute | solution.py:464
  25.0 11.4 %collective-permute-start.7 = (f32[136,512]{1,0:T(8,128)S(1)}, f32[136,512]{1,0:T(8,128)S(1)}, u32[]{:S(2)}, u32[]{:S(2)}) collective-permute-start(f32[136,512]{1,0:T(8,128)S(1)} %get-tuple-element.79), channel_id=1, source_target_pairs={{0,1},{1,2},{2,3},{3,4},{4,5},{5,6},{6,7},{7,8},{8,9},{9,10},{10,1... | collective-permute-start | bytes 835592 | tf_op jit(solution)/shard_map/ppermute | solution.py:464
  25.0 6.7 %collective-permute-start.4 = (f32[200,128]{1,0:T(8,128)S(1)}, f32[200,128]{1,0:T(8,128)S(1)}, u32[]{:S(2)}, u32[]{:S(2)}) collective-permute-start(f32[200,128]{1,0:T(8,128)S(1)} %add.12), channel_id=1, source_target_pairs={{0,8},{1,9},{2,10},{3,11},{4,12},{5,13},{6,14},{7,15},{8,0},{9,1},... | collective-permute-start | bytes 307208 | tf_op jit(solution)/shard_map/ppermute | solution.py:379
  31.7 4.7 %collective-permute-start.6 = (f32[200,128]{1,0:T(8,128)S(1)}, f32[200,128]{1,0:T(8,128)S(1)}, u32[]{:S(2)}, u32[]{:S(2)}) collective-permute-start(f32[200,128]{1,0:T(8,128)S(1)} %add.13.mine_ref), channel_id=1, source_target_pairs={{0,4},{1,5},{2,6},{3,7},{4,0},{5,1},{6,2},{7,3},{8,12},{9,13},{10,... | collective-permute-start | bytes 307208 | tf_op jit(solution)/shard_map/ppermute | solution.py:379
  36.5 11.6 %collective-permute-start.8 = (f32[400,128]{1,0:T(8,128)S(1)}, f32[400,128]{1,0:T(8,128)S(1)}, u32[]{:S(2)}, u32[]{:S(2)}) collective-permute-start(f32[400,128]{1,0:T(8,128)S(1)} %join.4.mine_ref), channel_id=1, source_target_pairs={{0,2},{1,3},{2,0},{3,1},{4,6},{5,7},{6,4},{7,5},{8,10},{9,11},{10,... | collective-permute-start | bytes 614408 | tf_op jit(solution)/shard_map/ppermute | solution.py:379
  48.1 2.4 %collective-permute-start.9 = (f32[800,128]{1,0:T(8,128)S(1)}, f32[800,128]{1,0:T(8,128)S(1)}, u32[]{:S(2)}, u32[]{:S(2)}) collective-permute-start(f32[800,128]{1,0:T(8,128)S(1)} %join.5.mine_ref), channel_id=1, source_target_pairs={{0,1},{1,0},{2,3},{3,2},{4,5},{5,4},{6,7},{7,6},{8,9},{9,8},{10,11... | collective-permute-start | bytes 1228808 | tf_op jit(solution)/shard_map/ppermute | solution.py:379
  55.5 1.9 %collective-permute-start.10 = (f32[800,128]{1,0:T(8,128)S(1)}, f32[800,128]{1,0:T(8,128)S(1)}, u32[]{:S(2)}, u32[]{:S(2)}) collective-permute-start(f32[800,128]{1,0:T(8,128)S(1)} %get-tuple-element.88), channel_id=1, source_target_pairs={{0,1},{1,0},{2,3},{3,2},{4,5},{5,4},{6,7},{7,6},{8,9},{9,8},{10,11... | collective-permute-start | bytes 1228808 | tf_op jit(solution)/shard_map/ppermute | solution.py:379
  57.5 7.4 %collective-permute-start.11 = (f32[400,128]{1,0:T(8,128)S(1)}, f32[400,128]{1,0:T(8,128)S(1)}, u32[]{:S(2)}, u32[]{:S(2)}) collective-permute-start(f32[400,128]{1,0:T(8,128)S(1)} %get-tuple-element.90), channel_id=1, source_target_pairs={{0,2},{1,3},{2,0},{3,1},{4,6},{5,7},{6,4},{7,5},{8,10},{9,11},{10,... | collective-permute-start | bytes 614408 | tf_op jit(solution)/shard_map/ppermute | solution.py:379
  65.0 4.7 %collective-permute-start.12 = (f32[200,128]{1,0:T(8,128)S(1)}, f32[200,128]{1,0:T(8,128)S(1)}, u32[]{:S(2)}, u32[]{:S(2)}) collective-permute-start(f32[200,128]{1,0:T(8,128)S(1)} %get-tuple-element.107), channel_id=1, source_target_pairs={{0,4},{1,5},{2,6},{3,7},{4,0},{5,1},{6,2},{7,3},{8,12},{9,13},{10,... | collective-permute-start | bytes 307208 | tf_op jit(solution)/shard_map/ppermute | solution.py:379
  69.7 6.7 %collective-permute-start.13 = (f32[200,128]{1,0:T(8,128)S(1)}, f32[200,128]{1,0:T(8,128)S(1)}, u32[]{:S(2)}, u32[]{:S(2)}) collective-permute-start(f32[200,128]{1,0:T(8,128)S(1)} %add.14), channel_id=1, source_target_pairs={{0,8},{1,9},{2,10},{3,11},{4,12},{5,13},{6,14},{7,15},{8,0},{9,1},... | collective-permute-start | bytes 307208 | tf_op jit(solution)/shard_map/ppermute | solution.py:379
  76.5 4.7 %collective-permute-start.14 = (f32[200,128]{1,0:T(8,128)S(1)}, f32[200,128]{1,0:T(8,128)S(1)}, u32[]{:S(2)}, u32[]{:S(2)}) collective-permute-start(f32[200,128]{1,0:T(8,128)S(1)} %add.15.mine_ref), channel_id=1, source_target_pairs={{0,4},{1,5},{2,6},{3,7},{4,0},{5,1},{6,2},{7,3},{8,12},{9,13},{10,... | collective-permute-start | bytes 307208 | tf_op jit(solution)/shard_map/ppermute | solution.py:379
  81.2 5.8 %collective-permute-start.15 = (f32[400,128]{1,0:T(8,128)S(1)}, f32[400,128]{1,0:T(8,128)S(1)}, u32[]{:S(2)}, u32[]{:S(2)}) collective-permute-start(f32[400,128]{1,0:T(8,128)S(1)} %join.6.mine_ref), channel_id=1, source_target_pairs={{0,2},{1,3},{2,0},{3,1},{4,6},{5,7},{6,4},{7,5},{8,10},{9,11},{10,... | collective-permute-start | bytes 614408 | tf_op jit(solution)/shard_map/ppermute | solution.py:379
  87.1 1.8 %collective-permute-start.16 = (f32[800,128]{1,0:T(8,128)S(1)}, f32[800,128]{1,0:T(8,128)S(1)}, u32[]{:S(2)}, u32[]{:S(2)}) collective-permute-start(f32[800,128]{1,0:T(8,128)S(1)} %join.7.mine_ref), channel_id=1, source_target_pairs={{0,1},{1,0},{2,3},{3,2},{4,5},{5,4},{6,7},{7,6},{8,9},{9,8},{10,11... | collective-permute-start | bytes 1228808 | tf_op jit(solution)/shard_map/ppermute | solution.py:379
  (3 other events, 3.5 us)

commit v3 on v2

--- a/solution.py
+++ b/solution.py
@@ -13,7 +13,7 @@
 LANES = 128
 SPLITS = 3
 PIECES = 3
-LAG = 2
+LAG = 3
 f32 = jnp.float32
 bf16 = jnp.bfloat16
 NN = ((1,), (0,))
@@ -61,8 +61,18 @@
     return param - grad * (learn_rate / (jnp.sqrt(new_state) + epsilon)), new_state
 
 
-def gather(upper, lower, selector):
-    return dot(upper, selector, NN) + dot(lower, selector, NN)
+def both(values):
+    return jnp.concatenate(split(values), axis=0)
+
+
+def gather(halves, selector):
+    found = dot(halves, selector, NN)
+    return found[: found.shape[0] // 2] + found[found.shape[0] // 2 :]
+
+
+def add_up(values, selector):
+    total = dot(both(values), selector, NT)
+    return total[: total.shape[0] // 2] + total[total.shape[0] // 2 :]
 
 
 def padded_lanes(count):
@@ -98,7 +108,7 @@
     w_ref[:, e] = w
     query_grad = dot(tail_hi, w, NN) + pos_grad * t
     y_ref[:, e] = conj_product(query_grad, r)
-    return split(conj_product(query_grad, h))
+    return conj_product(query_grad, h)
 
 
 def times_kernel(neg_ref, times_ref):
@@ -113,49 +123,49 @@
 def front_kernel(
     step, head_ref, rel_ref, tail_ref, src_ref, kind_ref, dst_ref, times_ref,
     keep_ref, send_ref, y_ref, q_ref, w_ref, pg_ref,
-    head_hi, head_lo, tail_hi, tail_lo, rel_hi, rel_lo, rel_pad, total,
+    head_both, tail_both, rel_both, rel_pad, total,
 ):
     rows = head_ref.shape[1]
     kinds = rel_ref.shape[1]
     rel_pad[...] = jnp.zeros_like(rel_pad)
-    head_hi[...], head_lo[...] = split(head_ref[...])
     rel_pad[:, 0:kinds] = rel_ref[...]
-    rel_hi[...], rel_lo[...] = split(rel_pad[...])
-    tail_hi[...], tail_lo[...] = split(tail_ref[...])
+    head_both[...] = both(head_ref[...])
+    rel_both[...] = both(rel_pad[...])
+    tail_both[...] = both(tail_ref[...])
+    tail_hi = tail_both[0 : tail_ref.shape[0], :]
     tail_rows = tail_ref[...].T.astype(bf16)
     spans = times_ref.shape[1] // src_ref.shape[0]
     span = src_ref.shape[1] // spans
     for s in range(spans):
         e = slice(s * span, (s + 1) * span)
-        h = gather(head_hi[...], head_lo[...], one_hot(src_ref[step : step + 1, e], rows))
+        h = gather(head_both[...], one_hot(src_ref[step : step + 1, e], rows))
         kind_hot = one_hot(kind_ref[step : step + 1, e], rel_pad.shape[1])
-        r = gather(rel_hi[...], rel_lo[...], kind_hot)
-        t = gather(tail_hi[...], tail_lo[...], one_hot(dst_ref[step : step + 1, e], rows))
+        r = gather(rel_both[...], kind_hot)
+        t = gather(tail_both[...], one_hot(dst_ref[step : step + 1, e], rows))
         at = step * spans + s
-        x_hi, x_lo = span_grads(
-            h, r, t, tail_hi[...], tail_rows, times_ref[:, at : at + 1],
+        x = span_grads(
+            h, r, t, tail_hi, tail_rows, times_ref[:, at : at + 1],
             e, y_ref, q_ref, w_ref, pg_ref,
         )
-        spread(total, dot(x_hi, kind_hot, NT) + dot(x_lo, kind_hot, NT), s)
+        spread(total, add_up(x, kind_hot), s)
     bit = lax.axis_index("blk") & 1
     keep_ref[...] = total[bit]
     send_ref[...] = total[1 - bit]
 
 
 def pick_heads_kernel(step, head_ref, src_ref, h_ref):
-    head_hi, head_lo = split(head_ref[...])
     src_hot = one_hot(src_ref[step : step + 1, :], head_ref.shape[1])
-    h_ref[...] = gather(head_hi, head_lo, src_hot)
+    h_ref[...] = gather(both(head_ref[...]), src_hot)
 
 
 def pick_tails_kernel(step, width, dst_ref, *refs):
     *tail_refs, t_ref, tail_hi_ref, tail_rows_ref = refs
     rows = tail_refs[0].shape[1]
     tail = whole(tail_refs, width)
-    tail_hi, tail_lo = split(tail)
-    tail_hi_ref[...] = tail_hi
+    halves = both(tail)
+    tail_hi_ref[...] = halves[0:width]
     tail_rows_ref[...] = tail.T.astype(bf16)
-    t_ref[...] = gather(tail_hi, tail_lo, one_hot(dst_ref[step : step + 1, :], rows))
+    t_ref[...] = gather(halves, one_hot(dst_ref[step : step + 1, :], rows))
 
 
 def updated_relations(rel_ref, state_ref, mine_ref, other_ref, rel_out, state_out, total, grad):
@@ -175,7 +185,7 @@
     step, rel_ref, state_ref, mine_ref, other_ref, kind_ref,
     h_ref, t_ref, tail_hi_ref, tail_rows_ref, times_ref,
     rel_out, state_out, keep_ref, send_ref, y_ref, q_ref, w_ref, pg_ref,
-    rel_hi, rel_lo, rel_pad, total,
+    rel_both, rel_pad, total,
 ):
     kinds = rel_ref.shape[1]
     updated_relations(
@@ -183,18 +193,18 @@
     )
     rel_pad[...] = jnp.zeros_like(rel_pad)
     rel_pad[:, 0:kinds] = rel_out[...]
-    rel_hi[...], rel_lo[...] = split(rel_pad[...])
+    rel_both[...] = both(rel_pad[...])
     spans = times_ref.shape[1] // kind_ref.shape[0]
     span = h_ref.shape[1] // spans
     for s in range(spans):
         e = slice(s * span, (s + 1) * span)
         kind_hot = one_hot(kind_ref[step : step + 1, e], rel_pad.shape[1])
-        r = gather(rel_hi[...], rel_lo[...], kind_hot)
-        x_hi, x_lo = span_grads(
+        r = gather(rel_both[...], kind_hot)
+        x = span_grads(
             h_ref[:, e], r, t_ref[:, e], tail_hi_ref[...], tail_rows_ref[...],
             times_ref[:, step * spans + s : step * spans + s + 1], e, y_ref, q_ref, w_ref, pg_ref,
         )
-        spread(total, dot(x_hi, kind_hot, NT) + dot(x_lo, kind_hot, NT), s)
+        spread(total, add_up(x, kind_hot), s)
     bit = lax.axis_index("blk") & 1
     keep_ref[...] = total[bit]
     send_ref[...] = total[1 - bit]
@@ -210,16 +220,12 @@
 ):
     tail_refs, head_out, head_state_out, outs = refs[:parts], *refs[parts : parts + 2], refs[parts + 2 :]
     width, rows = head_ref.shape
-    y_hi, y_lo = split(y_ref[...])
     src_hot = one_hot(src_ref[step : step + 1, :], rows)
-    head_grad = dot(y_hi, src_hot, NT) + dot(y_lo, src_hot, NT)
+    head_grad = add_up(y_ref[...], src_hot)
     head_out[...], head_state_out[...] = adagrad(head_ref[...], head_state_ref[...], head_grad)
     query = q_ref[...]
-    p_hi, p_lo = split(query * pg_ref[...])
     dst_hot = one_hot(dst_ref[step : step + 1, :], rows)
-    tail_grad = (
-        dot(query.astype(bf16), w_ref[...], NT) + dot(p_hi, dst_hot, NT) + dot(p_lo, dst_hot, NT)
-    )
+    tail_grad = dot(query.astype(bf16), w_ref[...], NT) + add_up(query * pg_ref[...], dst_hot)
     tail, state = adagrad(whole(tail_refs, width), tail_state_ref[...], tail_grad)
     if len(outs) == 2:
         outs[0][...], outs[1][...] = tail, state
@@ -282,8 +288,8 @@
         out_shape=made_shapes(width, rows, edges, half),
         in_specs=[VMEM] * 7,
         out_specs=[VMEM] * 6,
-        scratch_shapes=[pltpu.VMEM((width, rows), bf16)] * 4
-        + [pltpu.VMEM((width, lanes), bf16)] * 2
+        scratch_shapes=[pltpu.VMEM((2 * width, rows), bf16)] * 2
+        + [pltpu.VMEM((2 * width, lanes), bf16)]
         + [pltpu.VMEM((width, lanes), f32), pltpu.VMEM((2, half, LANES), f32)],
         compiler_params=settings(24),
         name="front",
@@ -332,7 +338,7 @@
         + made_shapes(width, rows, edges, half),
         in_specs=[VMEM] * 10,
         out_specs=[VMEM] * 8,
-        scratch_shapes=[pltpu.VMEM((width, lanes), bf16)] * 2
+        scratch_shapes=[pltpu.VMEM((2 * width, lanes), bf16)]
         + [pltpu.VMEM((width, lanes), f32), pltpu.VMEM((2, half, LANES), f32)],
         compiler_params=settings(24),
         name="main",
@@ -423,7 +429,7 @@
     )(mine, got)
 
 
-def reduce_halves(keep, send, beside, pieces):
+def reduce_halves(keep, send, beside, pieces, picked):
     levels = (lax.axis_size("blk") - 1).bit_length()
     splits = min(levels, SPLITS)
     waiting, rolled, count = list(pieces), [], 0
@@ -452,11 +458,13 @@
         total, got = exchange(total, 1 << level)
         total = total + got
     for level in reversed(range(1, splits)):
+        if level == 1:
+            total, picked = lax.optimization_barrier((total, picked))
         total, got = exchange(total, 1 << level)
         total = join(level, total, got)
     total, got = exchange(total, 1)
     rolled += [roll(piece) for piece in waiting]
-    return total, got, beside, rolled
+    return total, got, beside, rolled, picked
 
 
 def roll(value):
@@ -489,7 +497,6 @@
                 step, heads, tails[0], relations, edge_src, edge_rel, edge_dst, times
             )
         else:
-            h = pick_heads(step, heads, edge_src)
             picked = (h, *pick_tails(step, width, tails, edge_dst), times)
             relations, rel_state, keep, send, *made = main(
                 step, relations, rel_state, mine, other, edge_rel, picked
@@ -498,7 +505,8 @@
             step, joined, heads, head_state, tails, tail_state, edge_src, edge_dst, made
         )
         beside, pieces = ((heads,), rest) if joined else ((heads, *rest), [])
-        mine, other, beside, tails = reduce_halves(keep, send, beside, pieces)
+        h = pick_heads(step + 1, heads, edge_src) if joined else None
+        mine, other, beside, tails, h = reduce_halves(keep, send, beside, pieces, h)
         if joined:
             tail_state = tails[-1][-8:-7]
         else:

time: 90.3 us -> 88.6 us (0.981)
  waiting for transfers between devices: 46.8 us -> 45.6 us
    ppermute x3, waiting for transfers between devices: 1.41 us -> 0.01 us  [roll(): lax.ppermute(value, 'blk', [(i, (i + 1) % count) for i in range(count)])]
  transfers between devices with their start and end apart: 17 -> 17, of which waited for: 14 -> 14; matrix products, arithmetic and copies ran while one was open for 0% -> 0% of each run, Pallas kernels for 10% -> 9%
where the time goes in v3:
time: 88.6 us; the launch traced here: 88.3 us
  waiting for transfers between devices  45.6 us (51%)
  Pallas kernels  21.1 us (24%)
  starting transfers between devices  19.6 us (22%)
  local copies, waits for them, and re-layouts  1.09 us (1%)
    ppermute x14, waiting for transfers between devices, swap(): return lax.ppermute(value, 'blk', [(i, i ^ distance) for i in range(count)])  45.5 us
    ppermute x14, starting transfers between devices, swap(): return lax.ppermute(value, 'blk', [(i, i ^ distance) for i in range(count)])  19.4 us
    pallas_call x2, Pallas kernels, back(): pl.pallas_call(functools.partial(back_kernel, step, len(tails)), out_shap...  6.11 us
    pallas_call x1, Pallas kernels, front(): pl.pallas_call(functools.partial(front_kernel, step), out_shape=made_shap...  5.94 us
    pallas_call x1, Pallas kernels, main(): pl.pallas_call(functools.partial(main_kernel, step), out_shape=[shape(*re...  5.05 us
  transfers between devices with their start and end apart: 17, of which 14 were waited for; matrix products, arithmetic and copies ran while one was open for 0% of the time, Pallas kernels for 9%

profile of v3, /device:TPU:0, one launch (start us, length us, event | category | flops | bytes accessed | tf_op | source)
XLA Modules:
  0.0 88.3 jit_solution(13801314163488507484)
XLA Ops:
  2.3 5.9 %front.1 = (f32[800,128]{1,0:T(8,128)S(1)}, f32[800,128]{1,0:T(8,128)S(1)}, f32[400,1024]{1,0:T(8,128)S(1)}, f32[400,1024]{1,0:T(8,128)S(1)}, bf16[512,1024]{1,0:T(8,128)(2,1)S(1)}, /*index=5*/f32[1,1024]{1,0:T(1,128)S(1)}) custom-call(f32[400,512]{1,0:T(8,128)S(1)} %bitcast.14, f32[400,500]{1,0:T(8,128)S(1)} %bitcast.12, f32[400,512]{1,0:T(8,128)S(1)} %bitcast.16, ...), custom_call_target="tpu_custom_call" | custom-call | tf_op jit(solution)/shard_map/front/pallas_call | solution.py:286
  8.8 1.4 %collective-permute-done.got_ref = f32[800,128]{1,0:T(8,128)S(1)} collective-permute-done((f32[800,128]{1,0:T(8,128)S(1)}, f32[800,128]{1,0:T(8,128)S(1)}, u32[]{:S(2)}, u32[]{:S(2)}) %collective-permute-start) | collective-permute-done | bytes 409632 | tf_op jit(solution)/shard_map/ppermute | solution.py:385
  10.2 2.9 %collective-permute-start.1 = (f32[400,128]{1,0:T(8,128)S(1)}, f32[400,128]{1,0:T(8,128)S(1)}, u32[]{:S(2)}, u32[]{:S(2)}) collective-permute-start(f32[400,128]{1,0:T(8,128)S(1)} %get-tuple-element.63), channel_id=1, source_target_pairs={{0,2},{1,3},{2,0},{3,1},{4,6},{5,7},{6,4},{7,5},{8,10},{9,11},{10,... | collective-permute-start | bytes 614408 | tf_op jit(solution)/shard_map/ppermute | solution.py:385
  13.2 2.6 %back.2 = (f32[400,512]{1,0:T(8,128)S(1)}, f32[1,512]{1,0:T(1,128)S(1)}, f32[136,512]{1,0:T(8,128)S(1)}, f32[136,512]{1,0:T(8,128)S(1)}, f32[136,512]{1,0:T(8,128)S(1)}) custom-call(f32[400,512]{1,0:T(8,128)S(1)} %bitcast.15, f32[1,512]{1,0:T(1,128)S(1)} %bitcast.19, f32[1,512]{1,0:T(1,128)S(1)} %bitcast.20, s32[2,1024]{1,0:T(2,128)S(1)} %copy-done.4, ...), custom_call_target="tpu_custom_call" | custom-call | flops 2097152000 | bytes 4915200 | tf_op jit(solution)/shard_map/back/pallas_call | solution.py:357
  15.9 2.8 %collective-permute-done.1.got_ref = f32[400,128]{1,0:T(8,128)S(1)} collective-permute-done((f32[400,128]{1,0:T(8,128)S(1)}, f32[400,128]{1,0:T(8,128)S(1)}, u32[]{:S(2)}, u32[]{:S(2)}) %collective-permute-start.1) | collective-permute-done | bytes 204832 | tf_op jit(solution)/shard_map/ppermute | solution.py:385
  18.6 1.8 %collective-permute-start.2 = (f32[200,128]{1,0:T(8,128)S(1)}, f32[200,128]{1,0:T(8,128)S(1)}, u32[]{:S(2)}, u32[]{:S(2)}) collective-permute-start(f32[200,128]{1,0:T(8,128)S(1)} %get-tuple-element.74), channel_id=1, source_target_pairs={{0,4},{1,5},{2,6},{3,7},{4,0},{5,1},{6,2},{7,3},{8,12},{9,13},{10,... | collective-permute-start | bytes 307208 | tf_op jit(solution)/shard_map/ppermute | solution.py:385
  20.4 2.9 %collective-permute-done.2 = f32[200,128]{1,0:T(8,128)S(1)} collective-permute-done((f32[200,128]{1,0:T(8,128)S(1)}, f32[200,128]{1,0:T(8,128)S(1)}, u32[]{:S(2)}, u32[]{:S(2)}) %collective-permute-start.2) | collective-permute-done | bytes 102432 | tf_op jit(solution)/shard_map/ppermute | solution.py:385
  23.4 2.8 %collective-permute-start.3 = (f32[200,128]{1,0:T(8,128)S(1)}, f32[200,128]{1,0:T(8,128)S(1)}, u32[]{:S(2)}, u32[]{:S(2)}) collective-permute-start(f32[200,128]{1,0:T(8,128)S(1)} %add.12), channel_id=1, source_target_pairs={{0,8},{1,9},{2,10},{3,11},{4,12},{5,13},{6,14},{7,15},{8,0},{9,1},... | collective-permute-start | bytes 307208 | tf_op jit(solution)/shard_map/ppermute | solution.py:385
  26.2 4.7 %collective-permute-done.3 = f32[200,128]{1,0:T(8,128)S(1)} collective-permute-done((f32[200,128]{1,0:T(8,128)S(1)}, f32[200,128]{1,0:T(8,128)S(1)}, u32[]{:S(2)}, u32[]{:S(2)}) %collective-permute-start.3) | collective-permute-done | bytes 102432 | tf_op jit(solution)/shard_map/ppermute | solution.py:385
  32.2 3.4 %collective-permute-done.5.got_ref = f32[200,128]{1,0:T(8,128)S(1)} collective-permute-done((f32[200,128]{1,0:T(8,128)S(1)}, f32[200,128]{1,0:T(8,128)S(1)}, u32[]{:S(2)}, u32[]{:S(2)}) %collective-permute-start.5) | collective-permute-done | bytes 102432 | tf_op jit(solution)/shard_map/ppermute | solution.py:385
  35.6 7.0 %collective-permute-start.7 = (f32[400,128]{1,0:T(8,128)S(1)}, f32[400,128]{1,0:T(8,128)S(1)}, u32[]{:S(2)}, u32[]{:S(2)}) collective-permute-start(f32[400,128]{1,0:T(8,128)S(1)} %join.4.mine_ref), channel_id=1, source_target_pairs={{0,2},{1,3},{2,0},{3,1},{4,6},{5,7},{6,4},{7,5},{8,10},{9,11},{10,... | collective-permute-start | bytes 614408 | tf_op jit(solution)/shard_map/ppermute | solution.py:385
  42.6 5.2 %collective-permute-done.7.got_ref = f32[400,128]{1,0:T(8,128)S(1)} collective-permute-done((f32[400,128]{1,0:T(8,128)S(1)}, f32[400,128]{1,0:T(8,128)S(1)}, u32[]{:S(2)}, u32[]{:S(2)}) %collective-permute-start.7) | collective-permute-done | bytes 204832 | tf_op jit(solution)/shard_map/ppermute | solution.py:385
  49.6 5.1 %main.1 = (f32[400,500]{1,0:T(8,128)S(1)}, f32[1,500]{1,0:T(1,128)S(1)}, f32[800,128]{1,0:T(8,128)S(1)}, f32[800,128]{1,0:T(8,128)S(1)}, f32[400,1024]{1,0:T(8,1...) custom-call(f32[400,500]{1,0:T(8,128)S(1)} %bitcast.13, ...), custom_call_target="tpu_custom_call" | custom-call | tf_op jit(solution)/shard_map/main/pallas_call | solution.py:335
  54.9 1.6 %collective-permute-done.10.got_ref = f32[800,128]{1,0:T(8,128)S(1)} collective-permute-done((f32[800,128]{1,0:T(8,128)S(1)}, f32[800,128]{1,0:T(8,128)S(1)}, u32[]{:S(2)}, u32[]{:S(2)}) %collective-permute-start.10) | collective-permute-done | bytes 409632 | tf_op jit(solution)/shard_map/ppermute | solution.py:385
  56.6 1.8 %collective-permute-start.11 = (f32[400,128]{1,0:T(8,128)S(1)}, f32[400,128]{1,0:T(8,128)S(1)}, u32[]{:S(2)}, u32[]{:S(2)}) collective-permute-start(f32[400,128]{1,0:T(8,128)S(1)} %get-tuple-element.94), channel_id=1, source_target_pairs={{0,2},{1,3},{2,0},{3,1},{4,6},{5,7},{6,4},{7,5},{8,10},{9,11},{10,... | collective-permute-start | bytes 614408 | tf_op jit(solution)/shard_map/ppermute | solution.py:385
  58.4 3.5 %back.3 = (f32[400,512]{1,0:T(8,128)}, f32[1,512]{1,0:T(1,128)}, f32[400,512]{1,0:T(8,128)}, f32[1,512]{1,0:T(1,128)}) custom-call(f32[400,512]{1,0:T(8,128)S(1)} %get-tuple-element.70.head_ref, f32[1,512]{1,0:T(1,128)S(1)} %get-tuple-element.96.head_state_ref, f32[1,512]{1,0:T(1,128)S(1)} %slice.3.tail_state_ref, s32[2,1024]{1,0:T(2,128)S(1)} %copy-done.4, ...), custom_call_target="tpu_custom_call" | custom-call | flops 2097152000 | bytes 4915200 | tf_op jit(solution)/shard_map/back/pallas_call | solution.py:357
  61.9 1.9 %collective-permute-done.11.got_ref = f32[400,128]{1,0:T(8,128)S(1)} collective-permute-done((f32[400,128]{1,0:T(8,128)S(1)}, f32[400,128]{1,0:T(8,128)S(1)}, u32[]{:S(2)}, u32[]{:S(2)}) %collective-permute-start.11) | collective-permute-done | bytes 204832 | tf_op jit(solution)/shard_map/ppermute | solution.py:385
  63.9 4.6 %collective-permute-done.12 = f32[200,128]{1,0:T(8,128)S(1)} collective-permute-done((f32[200,128]{1,0:T(8,128)S(1)}, f32[200,128]{1,0:T(8,128)S(1)}, u32[]{:S(2)}, u32[]{:S(2)}) %collective-permute-start.12) | collective-permute-done | bytes 102432 | tf_op jit(solution)/shard_map/ppermute | solution.py:385
  68.6 6.1 %collective-permute-done.13 = f32[200,128]{1,0:T(8,128)S(1)} collective-permute-done((f32[200,128]{1,0:T(8,128)S(1)}, f32[200,128]{1,0:T(8,128)S(1)}, u32[]{:S(2)}, u32[]{:S(2)}) %collective-permute-start.13) | collective-permute-done | bytes 102432 | tf_op jit(solution)/shard_map/ppermute | solution.py:385
  74.8 4.6 %collective-permute-done.14.got_ref = f32[200,128]{1,0:T(8,128)S(1)} collective-permute-done((f32[200,128]{1,0:T(8,128)S(1)}, f32[200,128]{1,0:T(8,128)S(1)}, u32[]{:S(2)}, u32[]{:S(2)}) %collective-permute-start.14) | collective-permute-done | bytes 102432 | tf_op jit(solution)/shard_map/ppermute | solution.py:385
  79.5 1.8 %collective-permute-start.15 = (f32[400,128]{1,0:T(8,128)S(1)}, f32[400,128]{1,0:T(8,128)S(1)}, u32[]{:S(2)}, u32[]{:S(2)}) collective-permute-start(f32[400,128]{1,0:T(8,128)S(1)} %join.6.mine_ref), channel_id=1, source_target_pairs={{0,2},{1,3},{2,0},{3,1},{4,6},{5,7},{6,4},{7,5},{8,10},{9,11},{10,... | collective-permute-start | bytes 614408 | tf_op jit(solution)/shard_map/ppermute | solution.py:385
  81.3 4.0 %collective-permute-done.15.got_ref = f32[400,128]{1,0:T(8,128)S(1)} collective-permute-done((f32[400,128]{1,0:T(8,128)S(1)}, f32[400,128]{1,0:T(8,128)S(1)}, u32[]{:S(2)}, u32[]{:S(2)}) %collective-permute-start.15) | collective-permute-done | bytes 204832 | tf_op jit(solution)/shard_map/ppermute | solution.py:385
  85.4 1.7 %collective-permute-done.16.other_ref = f32[800,128]{1,0:T(8,128)S(1)} collective-permute-done((f32[800,128]{1,0:T(8,128)S(1)}, f32[800,128]{1,0:T(8,128)S(1)}, u32[]{:S(2)}, u32[]{:S(2)}) %collective-permute-start.16) | collective-permute-done | bytes 409632 | tf_op jit(solution)/shard_map/ppermute | solution.py:385
  87.1 1.2 %relations.1 = (f32[400,500]{1,0:T(8,128)}, f32[1,500]{1,0:T(1,128)}) custom-call(f32[400,500]{1,0:T(8,128)S(1)} %get-tuple-element.108.rel_ref, f32[1,500]{1,0:T(1,128)S(1)} %get-tuple-element.109.state_ref, f32[800,128]{1,0:T(8,128)S(1)} %join.7.mine_ref, f32[800,128]{1,0:T(8,128)S(1)} %collective-permute-done.16.other_ref), custom_call_target="tpu_custom_call" | custom-call | tf_op jit(solution)/shard_map/relations/pallas_call | solution.py:370
  (51 shorter events, 6.2 us)
Async XLA Ops:
  0.7 1.6 %copy-start.2 = (f32[512,400]{0,1:T(8,128)S(1)}, f32[512,400]{0,1:T(8,128)}, u32[]{:S(2)}) copy-start(f32[512,400]{0,1:T(8,128)} %param.12) | copy-start | bytes 2457604
  0.7 1.6 %copy-start.4 = (s32[2,1024]{1,0:T(2,128)S(1)}, s32[2,1024]{1,0:T(2,128)}, u32[]{:S(2)}) copy-start(s32[2,1024]{1,0:T(2,128)} %src_ref.7) | copy-start | bytes 24580
  0.7 1.6 %copy-start.3 = (s32[2,1024]{1,0:T(2,128)S(1)}, s32[2,1024]{1,0:T(2,128)}, u32[]{:S(2)}) copy-start(s32[2,1024]{1,0:T(2,128)} %kind_ref.3) | copy-start | bytes 24580
  0.7 1.6 %copy-start.5 = (s32[2,1024]{1,0:T(2,128)S(1)}, s32[2,1024]{1,0:T(2,128)}, u32[]{:S(2)}) copy-start(s32[2,1024]{1,0:T(2,128)} %dst_ref.7) | copy-start | bytes 24580
  2.3 10.9 %copy-start.8 = (f32[512]{0:T(512)S(1)}, f32[512]{0:T(512)}, u32[]{:S(2)}) copy-start(f32[512]{0:T(512)} %param.11) | copy-start | bytes 6148
  2.3 10.9 %copy-start.9 = (f32[512]{0:T(512)S(1)}, f32[512]{0:T(512)}, u32[]{:S(2)}) copy-start(f32[512]{0:T(512)} %param.13) | copy-start | bytes 6148
  8.3 1.9 %collective-permute-start = (f32[800,128]{1,0:T(8,128)S(1)}, f32[800,128]{1,0:T(8,128)S(1)}, u32[]{:S(2)}, u32[]{:S(2)}) collective-permute-start(f32[800,128]{1,0:T(8,128)S(1)} %get-tuple-element.61), channel_id=1, source_target_pairs={{0,1},{1,0},{2,3},{3,2},{4,5},{5,4},{6,7},{7,6},{8,9},{9,8},{10,11... | collective-permute-start | bytes 1228808 | tf_op jit(solution)/shard_map/ppermute | solution.py:385
  10.2 8.4 %collective-permute-start.1 = (f32[400,128]{1,0:T(8,128)S(1)}, f32[400,128]{1,0:T(8,128)S(1)}, u32[]{:S(2)}, u32[]{:S(2)}) collective-permute-start(f32[400,128]{1,0:T(8,128)S(1)} %get-tuple-element.63), channel_id=1, source_target_pairs={{0,2},{1,3},{2,0},{3,1},{4,6},{5,7},{6,4},{7,5},{8,10},{9,11},{10,... | collective-permute-start | bytes 614408 | tf_op jit(solution)/shard_map/ppermute | solution.py:385
  15.8 15.1 %collective-permute-start.4 = (f32[136,512]{1,0:T(8,128)S(1)}, f32[136,512]{1,0:T(8,128)S(1)}, u32[]{:S(2)}, u32[]{:S(2)}) collective-permute-start(f32[136,512]{1,0:T(8,128)S(1)} %get-tuple-element.77), channel_id=1, source_target_pairs={{0,1},{1,2},{2,3},{3,4},{4,5},{5,6},{6,7},{7,8},{8,9},{9,10},{10,1... | collective-permute-start | bytes 835592 | tf_op jit(solution)/shard_map/ppermute | solution.py:472
  18.6 4.7 %collective-permute-start.2 = (f32[200,128]{1,0:T(8,128)S(1)}, f32[200,128]{1,0:T(8,128)S(1)}, u32[]{:S(2)}, u32[]{:S(2)}) collective-permute-start(f32[200,128]{1,0:T(8,128)S(1)} %get-tuple-element.74), channel_id=1, source_target_pairs={{0,4},{1,5},{2,6},{3,7},{4,0},{5,1},{6,2},{7,3},{8,12},{9,13},{10,... | collective-permute-start | bytes 307208 | tf_op jit(solution)/shard_map/ppermute | solution.py:385
  20.4 15.2 %collective-permute-start.6 = (f32[136,512]{1,0:T(8,128)S(1)}, f32[136,512]{1,0:T(8,128)S(1)}, u32[]{:S(2)}, u32[]{:S(2)}) collective-permute-start(f32[136,512]{1,0:T(8,128)S(1)} %get-tuple-element.80), channel_id=1, source_target_pairs={{0,1},{1,2},{2,3},{3,4},{4,5},{5,6},{6,7},{7,8},{8,9},{9,10},{10,1... | collective-permute-start | bytes 835592 | tf_op jit(solution)/shard_map/ppermute | solution.py:472
  23.4 7.5 %collective-permute-start.3 = (f32[200,128]{1,0:T(8,128)S(1)}, f32[200,128]{1,0:T(8,128)S(1)}, u32[]{:S(2)}, u32[]{:S(2)}) collective-permute-start(f32[200,128]{1,0:T(8,128)S(1)} %add.12), channel_id=1, source_target_pairs={{0,8},{1,9},{2,10},{3,11},{4,12},{5,13},{6,14},{7,15},{8,0},{9,1},... | collective-permute-start | bytes 307208 | tf_op jit(solution)/shard_map/ppermute | solution.py:385
  30.9 4.7 %collective-permute-start.5 = (f32[200,128]{1,0:T(8,128)S(1)}, f32[200,128]{1,0:T(8,128)S(1)}, u32[]{:S(2)}, u32[]{:S(2)}) collective-permute-start(f32[200,128]{1,0:T(8,128)S(1)} %add.13.mine_ref), channel_id=1, source_target_pairs={{0,4},{1,5},{2,6},{3,7},{4,0},{5,1},{6,2},{7,3},{8,12},{9,13},{10,... | collective-permute-start | bytes 307208 | tf_op jit(solution)/shard_map/ppermute | solution.py:385
  31.0 16.8 %collective-permute-start.8 = (f32[136,512]{1,0:T(8,128)S(1)}, f32[136,512]{1,0:T(8,128)S(1)}, u32[]{:S(2)}, u32[]{:S(2)}) collective-permute-start(f32[136,512]{1,0:T(8,128)S(1)} %get-tuple-element.82), channel_id=1, source_target_pairs={{0,1},{1,2},{2,3},{3,4},{4,5},{5,6},{6,7},{7,8},{8,9},{9,10},{10,1... | collective-permute-start | bytes 835592 | tf_op jit(solution)/shard_map/ppermute | solution.py:472
  35.6 12.1 %collective-permute-start.7 = (f32[400,128]{1,0:T(8,128)S(1)}, f32[400,128]{1,0:T(8,128)S(1)}, u32[]{:S(2)}, u32[]{:S(2)}) collective-permute-start(f32[400,128]{1,0:T(8,128)S(1)} %join.4.mine_ref), channel_id=1, source_target_pairs={{0,2},{1,3},{2,0},{3,1},{4,6},{5,7},{6,4},{7,5},{8,10},{9,11},{10,... | collective-permute-start | bytes 614408 | tf_op jit(solution)/shard_map/ppermute | solution.py:385
  47.8 1.8 %copy-start.6 = (f32[500]{0:T(512)S(1)}, f32[500]{0:T(512)}, u32[]{:S(2)}) copy-start(f32[500]{0:T(512)} %param.15) | copy-start | bytes 6004
  47.8 1.8 %collective-permute-start.9 = (f32[800,128]{1,0:T(8,128)S(1)}, f32[800,128]{1,0:T(8,128)S(1)}, u32[]{:S(2)}, u32[]{:S(2)}) collective-permute-start(f32[800,128]{1,0:T(8,128)S(1)} %join.5.mine_ref), channel_id=1, source_target_pairs={{0,1},{1,0},{2,3},{3,2},{4,5},{5,4},{6,7},{7,6},{8,9},{9,8},{10,11... | collective-permute-start | bytes 1228808 | tf_op jit(solution)/shard_map/ppermute | solution.py:385
  54.7 1.8 %collective-permute-start.10 = (f32[800,128]{1,0:T(8,128)S(1)}, f32[800,128]{1,0:T(8,128)S(1)}, u32[]{:S(2)}, u32[]{:S(2)}) collective-permute-start(f32[800,128]{1,0:T(8,128)S(1)} %get-tuple-element.92), channel_id=1, source_target_pairs={{0,1},{1,0},{2,3},{3,2},{4,5},{5,4},{6,7},{7,6},{8,9},{9,8},{10,11... | collective-permute-start | bytes 1228808 | tf_op jit(solution)/shard_map/ppermute | solution.py:385
  56.6 7.2 %collective-permute-start.11 = (f32[400,128]{1,0:T(8,128)S(1)}, f32[400,128]{1,0:T(8,128)S(1)}, u32[]{:S(2)}, u32[]{:S(2)}) collective-permute-start(f32[400,128]{1,0:T(8,128)S(1)} %get-tuple-element.94), channel_id=1, source_target_pairs={{0,2},{1,3},{2,0},{3,1},{4,6},{5,7},{6,4},{7,5},{8,10},{9,11},{10,... | collective-permute-start | bytes 614408 | tf_op jit(solution)/shard_map/ppermute | solution.py:385
  63.8 4.7 %collective-permute-start.12 = (f32[200,128]{1,0:T(8,128)S(1)}, f32[200,128]{1,0:T(8,128)S(1)}, u32[]{:S(2)}, u32[]{:S(2)}) collective-permute-start(f32[200,128]{1,0:T(8,128)S(1)} %get-tuple-element.111), channel_id=1, source_target_pairs={{0,4},{1,5},{2,6},{3,7},{4,0},{5,1},{6,2},{7,3},{8,12},{9,13},{10,... | collective-permute-start | bytes 307208 | tf_op jit(solution)/shard_map/ppermute | solution.py:385
  68.5 6.2 %collective-permute-start.13 = (f32[200,128]{1,0:T(8,128)S(1)}, f32[200,128]{1,0:T(8,128)S(1)}, u32[]{:S(2)}, u32[]{:S(2)}) collective-permute-start(f32[200,128]{1,0:T(8,128)S(1)} %add.14), channel_id=1, source_target_pairs={{0,8},{1,9},{2,10},{3,11},{4,12},{5,13},{6,14},{7,15},{8,0},{9,1},... | collective-permute-start | bytes 307208 | tf_op jit(solution)/shard_map/ppermute | solution.py:385
  74.7 4.7 %collective-permute-start.14 = (f32[200,128]{1,0:T(8,128)S(1)}, f32[200,128]{1,0:T(8,128)S(1)}, u32[]{:S(2)}, u32[]{:S(2)}) collective-permute-start(f32[200,128]{1,0:T(8,128)S(1)} %add.15.mine_ref), channel_id=1, source_target_pairs={{0,4},{1,5},{2,6},{3,7},{4,0},{5,1},{6,2},{7,3},{8,12},{9,13},{10,... | collective-permute-start | bytes 307208 | tf_op jit(solution)/shard_map/ppermute | solution.py:385
  79.5 5.8 %collective-permute-start.15 = (f32[400,128]{1,0:T(8,128)S(1)}, f32[400,128]{1,0:T(8,128)S(1)}, u32[]{:S(2)}, u32[]{:S(2)}) collective-permute-start(f32[400,128]{1,0:T(8,128)S(1)} %join.6.mine_ref), channel_id=1, source_target_pairs={{0,2},{1,3},{2,0},{3,1},{4,6},{5,7},{6,4},{7,5},{8,10},{9,11},{10,... | collective-permute-start | bytes 614408 | tf_op jit(solution)/shard_map/ppermute | solution.py:385
  85.3 1.8 %collective-permute-start.16 = (f32[800,128]{1,0:T(8,128)S(1)}, f32[800,128]{1,0:T(8,128)S(1)}, u32[]{:S(2)}, u32[]{:S(2)}) collective-permute-start(f32[800,128]{1,0:T(8,128)S(1)} %join.7.mine_ref), channel_id=1, source_target_pairs={{0,1},{1,0},{2,3},{3,2},{4,5},{5,4},{6,7},{7,6},{8,9},{9,8},{10,11... | collective-permute-start | bytes 1228808 | tf_op jit(solution)/shard_map/ppermute | solution.py:385
  (3 other events, 3.7 us)

commit v4 on v3

--- a/solution.py
+++ b/solution.py
@@ -95,20 +95,34 @@
     return jnp.sum(jnp.where(matches(drawn, rows), 1.0, 0.0), axis=1, keepdims=True)
 
 
-def span_grads(h, r, t, tail_hi, tail_rows, times, e, y_ref, q_ref, w_ref, pg_ref):
+def span_grads(found, tail_hi, tail_rows, times, e, y_ref, q_ref, w_ref, pg_ref):
+    h, r, t = found
     query = complex_product(h, r)
     q_ref[:, e] = query
     positive = jnp.sum(query * t, axis=0, keepdims=True)
     pos_grad = -1.0 / (1.0 + jnp.exp(positive))
     pg_ref[:, e] = pos_grad
+    yield
     scores = dot(tail_rows, query.astype(bf16), NN)
+    yield
     half_weight = 0.5 * neg_weight
     neg_grad = (half_weight * jnp.tanh(0.5 * scores) + half_weight).astype(bf16)
     w = (neg_grad.astype(f32) * times).astype(bf16)
     w_ref[:, e] = w
-    query_grad = dot(tail_hi, w, NN) + pos_grad * t
+    yield
+    query_grad = dot(tail_hi, w, NN)
+    yield
+    query_grad = query_grad + pos_grad * t
     y_ref[:, e] = conj_product(query_grad, r)
-    return conj_product(query_grad, h)
+    x = conj_product(query_grad, h)
+    yield
+    return x
+
+
+def in_turn(works):
+    works = list(works)
+    while works:
+        works = [work for work in works if next(work, works) is not works]
 
 
 def times_kernel(neg_ref, times_ref):
@@ -136,18 +150,24 @@
     tail_rows = tail_ref[...].T.astype(bf16)
     spans = times_ref.shape[1] // src_ref.shape[0]
     span = src_ref.shape[1] // spans
-    for s in range(spans):
+
+    def work(s):
         e = slice(s * span, (s + 1) * span)
         h = gather(head_both[...], one_hot(src_ref[step : step + 1, e], rows))
+        yield
+        t = gather(tail_both[...], one_hot(dst_ref[step : step + 1, e], rows))
+        yield
         kind_hot = one_hot(kind_ref[step : step + 1, e], rel_pad.shape[1])
         r = gather(rel_both[...], kind_hot)
-        t = gather(tail_both[...], one_hot(dst_ref[step : step + 1, e], rows))
+        yield
         at = step * spans + s
-        x = span_grads(
-            h, r, t, tail_hi, tail_rows, times_ref[:, at : at + 1],
-            e, y_ref, q_ref, w_ref, pg_ref,
+        times = times_ref[:, at : at + 1]
+        x = yield from span_grads(
+            (h, r, t), tail_hi, tail_rows, times, e, y_ref, q_ref, w_ref, pg_ref
         )
         spread(total, add_up(x, kind_hot), s)
+
+    in_turn(work(s) for s in range(spans))
     bit = lax.axis_index("blk") & 1
     keep_ref[...] = total[bit]
     send_ref[...] = total[1 - bit]
@@ -196,15 +216,20 @@
     rel_both[...] = both(rel_pad[...])
     spans = times_ref.shape[1] // kind_ref.shape[0]
     span = h_ref.shape[1] // spans
-    for s in range(spans):
+
+    def work(s):
         e = slice(s * span, (s + 1) * span)
         kind_hot = one_hot(kind_ref[step : step + 1, e], rel_pad.shape[1])
         r = gather(rel_both[...], kind_hot)
-        x = span_grads(
-            h_ref[:, e], r, t_ref[:, e], tail_hi_ref[...], tail_rows_ref[...],
-            times_ref[:, step * spans + s : step * spans + s + 1], e, y_ref, q_ref, w_ref, pg_ref,
+        yield
+        at = step * spans + s
+        x = yield from span_grads(
+            (h_ref[:, e], r, t_ref[:, e]), tail_hi_ref[...], tail_rows_ref[...],
+            times_ref[:, at : at + 1], e, y_ref, q_ref, w_ref, pg_ref,
         )
         spread(total, add_up(x, kind_hot), s)
+
+    in_turn(work(s) for s in range(spans))
     bit = lax.axis_index("blk") & 1
     keep_ref[...] = total[bit]
     send_ref[...] = total[1 - bit]

time: 88.6 us -> 87.4 us (0.986)
  Pallas kernels: 21.1 us -> 20 us
where the time goes in v4:
time: 87.4 us; the launch traced here: 87.2 us
  waiting for transfers between devices  45.6 us (52%)
  Pallas kernels  20 us (23%)
  starting transfers between devices  19.6 us (22%)
  local copies, waits for them, and re-layouts  1.09 us (1%)
  between operations  0.88 us (1%)
    ppermute x14, waiting for transfers between devices, swap(): return lax.ppermute(value, 'blk', [(i, i ^ distance) for i in range(count)])  45.5 us
    ppermute x14, starting transfers between devices, swap(): return lax.ppermute(value, 'blk', [(i, i ^ distance) for i in range(count)])  19.4 us
    pallas_call x2, Pallas kernels, back(): pl.pallas_call(functools.partial(back_kernel, step, len(tails)), out_shap...  6.12 us
    pallas_call x1, Pallas kernels, front(): pl.pallas_call(functools.partial(front_kernel, step), out_shape=made_shap...  5.49 us
    pallas_call x1, Pallas kernels, main(): pl.pallas_call(functools.partial(main_kernel, step), out_shape=[shape(*re...  4.37 us
  transfers between devices with their start and end apart: 17, of which 14 were waited for; matrix products, arithmetic and copies ran while one was open for 0% of the time, Pallas kernels for 9%

profile of v4, /device:TPU:0, one launch (start us, length us, event | category | flops | bytes accessed | tf_op | source)
XLA Modules:
  0.0 87.2 jit_solution(1369902588914526545)
XLA Ops:
  2.3 5.5 %front.1 = (f32[800,128]{1,0:T(8,128)S(1)}, f32[800,128]{1,0:T(8,128)S(1)}, f32[400,1024]{1,0:T(8,128)S(1)}, f32[400,1024]{1,0:T(8,128)S(1)}, bf16[512,1024]{1,0:T(8,128)(2,1)S(1)}, /*index=5*/f32[1,1024]{1,0:T(1,128)S(1)}) custom-call(f32[400,512]{1,0:T(8,128)S(1)} %bitcast.14, f32[400,500]{1,0:T(8,128)S(1)} %bitcast.12, f32[400,512]{1,0:T(8,128)S(1)} %bitcast.16, ...), custom_call_target="tpu_custom_call" | custom-call | tf_op jit(solution)/shard_map/front/pallas_call | solution.py:311
  8.3 1.4 %collective-permute-done.got_ref = f32[800,128]{1,0:T(8,128)S(1)} collective-permute-done((f32[800,128]{1,0:T(8,128)S(1)}, f32[800,128]{1,0:T(8,128)S(1)}, u32[]{:S(2)}, u32[]{:S(2)}) %collective-permute-start) | collective-permute-done | bytes 409632 | tf_op jit(solution)/shard_map/ppermute | solution.py:410
  9.8 2.9 %collective-permute-start.1 = (f32[400,128]{1,0:T(8,128)S(1)}, f32[400,128]{1,0:T(8,128)S(1)}, u32[]{:S(2)}, u32[]{:S(2)}) collective-permute-start(f32[400,128]{1,0:T(8,128)S(1)} %get-tuple-element.63), channel_id=1, source_target_pairs={{0,2},{1,3},{2,0},{3,1},{4,6},{5,7},{6,4},{7,5},{8,10},{9,11},{10,... | collective-permute-start | bytes 614408 | tf_op jit(solution)/shard_map/ppermute | solution.py:410
  12.7 2.6 %back.2 = (f32[400,512]{1,0:T(8,128)S(1)}, f32[1,512]{1,0:T(1,128)S(1)}, f32[136,512]{1,0:T(8,128)S(1)}, f32[136,512]{1,0:T(8,128)S(1)}, f32[136,512]{1,0:T(8,128)S(1)}) custom-call(f32[400,512]{1,0:T(8,128)S(1)} %bitcast.15, f32[1,512]{1,0:T(1,128)S(1)} %bitcast.19, f32[1,512]{1,0:T(1,128)S(1)} %bitcast.20, s32[2,1024]{1,0:T(2,128)S(1)} %copy-done.4, ...), custom_call_target="tpu_custom_call" | custom-call | flops 2097152000 | bytes 4915200 | tf_op jit(solution)/shard_map/back/pallas_call | solution.py:382
  15.4 2.8 %collective-permute-done.1.got_ref = f32[400,128]{1,0:T(8,128)S(1)} collective-permute-done((f32[400,128]{1,0:T(8,128)S(1)}, f32[400,128]{1,0:T(8,128)S(1)}, u32[]{:S(2)}, u32[]{:S(2)}) %collective-permute-start.1) | collective-permute-done | bytes 204832 | tf_op jit(solution)/shard_map/ppermute | solution.py:410
  18.2 1.8 %collective-permute-start.2 = (f32[200,128]{1,0:T(8,128)S(1)}, f32[200,128]{1,0:T(8,128)S(1)}, u32[]{:S(2)}, u32[]{:S(2)}) collective-permute-start(f32[200,128]{1,0:T(8,128)S(1)} %get-tuple-element.74), channel_id=1, source_target_pairs={{0,4},{1,5},{2,6},{3,7},{4,0},{5,1},{6,2},{7,3},{8,12},{9,13},{10,... | collective-permute-start | bytes 307208 | tf_op jit(solution)/shard_map/ppermute | solution.py:410
  20.0 2.9 %collective-permute-done.2 = f32[200,128]{1,0:T(8,128)S(1)} collective-permute-done((f32[200,128]{1,0:T(8,128)S(1)}, f32[200,128]{1,0:T(8,128)S(1)}, u32[]{:S(2)}, u32[]{:S(2)}) %collective-permute-start.2) | collective-permute-done | bytes 102432 | tf_op jit(solution)/shard_map/ppermute | solution.py:410
  22.9 2.8 %collective-permute-start.3 = (f32[200,128]{1,0:T(8,128)S(1)}, f32[200,128]{1,0:T(8,128)S(1)}, u32[]{:S(2)}, u32[]{:S(2)}) collective-permute-start(f32[200,128]{1,0:T(8,128)S(1)} %add.12), channel_id=1, source_target_pairs={{0,8},{1,9},{2,10},{3,11},{4,12},{5,13},{6,14},{7,15},{8,0},{9,1},... | collective-permute-start | bytes 307208 | tf_op jit(solution)/shard_map/ppermute | solution.py:410
  25.7 4.6 %collective-permute-done.3 = f32[200,128]{1,0:T(8,128)S(1)} collective-permute-done((f32[200,128]{1,0:T(8,128)S(1)}, f32[200,128]{1,0:T(8,128)S(1)}, u32[]{:S(2)}, u32[]{:S(2)}) %collective-permute-start.3) | collective-permute-done | bytes 102432 | tf_op jit(solution)/shard_map/ppermute | solution.py:410
  31.8 3.4 %collective-permute-done.5.got_ref = f32[200,128]{1,0:T(8,128)S(1)} collective-permute-done((f32[200,128]{1,0:T(8,128)S(1)}, f32[200,128]{1,0:T(8,128)S(1)}, u32[]{:S(2)}, u32[]{:S(2)}) %collective-permute-start.5) | collective-permute-done | bytes 102432 | tf_op jit(solution)/shard_map/ppermute | solution.py:410
  35.2 7.0 %collective-permute-start.7 = (f32[400,128]{1,0:T(8,128)S(1)}, f32[400,128]{1,0:T(8,128)S(1)}, u32[]{:S(2)}, u32[]{:S(2)}) collective-permute-start(f32[400,128]{1,0:T(8,128)S(1)} %join.4.mine_ref), channel_id=1, source_target_pairs={{0,2},{1,3},{2,0},{3,1},{4,6},{5,7},{6,4},{7,5},{8,10},{9,11},{10,... | collective-permute-start | bytes 614408 | tf_op jit(solution)/shard_map/ppermute | solution.py:410
  42.2 5.2 %collective-permute-done.7.got_ref = f32[400,128]{1,0:T(8,128)S(1)} collective-permute-done((f32[400,128]{1,0:T(8,128)S(1)}, f32[400,128]{1,0:T(8,128)S(1)}, u32[]{:S(2)}, u32[]{:S(2)}) %collective-permute-start.7) | collective-permute-done | bytes 204832 | tf_op jit(solution)/shard_map/ppermute | solution.py:410
  49.2 4.4 %main.1 = (f32[400,500]{1,0:T(8,128)S(1)}, f32[1,500]{1,0:T(1,128)S(1)}, f32[800,128]{1,0:T(8,128)S(1)}, f32[800,128]{1,0:T(8,128)S(1)}, f32[400,1024]{1,0:T(8,1...) custom-call(f32[400,500]{1,0:T(8,128)S(1)} %bitcast.13, ...), custom_call_target="tpu_custom_call" | custom-call | tf_op jit(solution)/shard_map/main/pallas_call | solution.py:360
  53.8 1.6 %collective-permute-done.10.got_ref = f32[800,128]{1,0:T(8,128)S(1)} collective-permute-done((f32[800,128]{1,0:T(8,128)S(1)}, f32[800,128]{1,0:T(8,128)S(1)}, u32[]{:S(2)}, u32[]{:S(2)}) %collective-permute-start.10) | collective-permute-done | bytes 409632 | tf_op jit(solution)/shard_map/ppermute | solution.py:410
  55.4 1.8 %collective-permute-start.11 = (f32[400,128]{1,0:T(8,128)S(1)}, f32[400,128]{1,0:T(8,128)S(1)}, u32[]{:S(2)}, u32[]{:S(2)}) collective-permute-start(f32[400,128]{1,0:T(8,128)S(1)} %get-tuple-element.94), channel_id=1, source_target_pairs={{0,2},{1,3},{2,0},{3,1},{4,6},{5,7},{6,4},{7,5},{8,10},{9,11},{10,... | collective-permute-start | bytes 614408 | tf_op jit(solution)/shard_map/ppermute | solution.py:410
  57.2 3.5 %back.3 = (f32[400,512]{1,0:T(8,128)}, f32[1,512]{1,0:T(1,128)}, f32[400,512]{1,0:T(8,128)}, f32[1,512]{1,0:T(1,128)}) custom-call(f32[400,512]{1,0:T(8,128)S(1)} %get-tuple-element.70.head_ref, f32[1,512]{1,0:T(1,128)S(1)} %get-tuple-element.96.head_state_ref, f32[1,512]{1,0:T(1,128)S(1)} %slice.3.tail_state_ref, s32[2,1024]{1,0:T(2,128)S(1)} %copy-done.4, ...), custom_call_target="tpu_custom_call" | custom-call | flops 2097152000 | bytes 4915200 | tf_op jit(solution)/shard_map/back/pallas_call | solution.py:382
  60.7 1.9 %collective-permute-done.11.got_ref = f32[400,128]{1,0:T(8,128)S(1)} collective-permute-done((f32[400,128]{1,0:T(8,128)S(1)}, f32[400,128]{1,0:T(8,128)S(1)}, u32[]{:S(2)}, u32[]{:S(2)}) %collective-permute-start.11) | collective-permute-done | bytes 204832 | tf_op jit(solution)/shard_map/ppermute | solution.py:410
  62.7 4.6 %collective-permute-done.12 = f32[200,128]{1,0:T(8,128)S(1)} collective-permute-done((f32[200,128]{1,0:T(8,128)S(1)}, f32[200,128]{1,0:T(8,128)S(1)}, u32[]{:S(2)}, u32[]{:S(2)}) %collective-permute-start.12) | collective-permute-done | bytes 102432 | tf_op jit(solution)/shard_map/ppermute | solution.py:410
  67.5 6.1 %collective-permute-done.13 = f32[200,128]{1,0:T(8,128)S(1)} collective-permute-done((f32[200,128]{1,0:T(8,128)S(1)}, f32[200,128]{1,0:T(8,128)S(1)}, u32[]{:S(2)}, u32[]{:S(2)}) %collective-permute-start.13) | collective-permute-done | bytes 102432 | tf_op jit(solution)/shard_map/ppermute | solution.py:410
  73.7 4.6 %collective-permute-done.14.got_ref = f32[200,128]{1,0:T(8,128)S(1)} collective-permute-done((f32[200,128]{1,0:T(8,128)S(1)}, f32[200,128]{1,0:T(8,128)S(1)}, u32[]{:S(2)}, u32[]{:S(2)}) %collective-permute-start.14) | collective-permute-done | bytes 102432 | tf_op jit(solution)/shard_map/ppermute | solution.py:410
  78.3 1.8 %collective-permute-start.15 = (f32[400,128]{1,0:T(8,128)S(1)}, f32[400,128]{1,0:T(8,128)S(1)}, u32[]{:S(2)}, u32[]{:S(2)}) collective-permute-start(f32[400,128]{1,0:T(8,128)S(1)} %join.6.mine_ref), channel_id=1, source_target_pairs={{0,2},{1,3},{2,0},{3,1},{4,6},{5,7},{6,4},{7,5},{8,10},{9,11},{10,... | collective-permute-start | bytes 614408 | tf_op jit(solution)/shard_map/ppermute | solution.py:410
  80.1 4.0 %collective-permute-done.15.got_ref = f32[400,128]{1,0:T(8,128)S(1)} collective-permute-done((f32[400,128]{1,0:T(8,128)S(1)}, f32[400,128]{1,0:T(8,128)S(1)}, u32[]{:S(2)}, u32[]{:S(2)}) %collective-permute-start.15) | collective-permute-done | bytes 204832 | tf_op jit(solution)/shard_map/ppermute | solution.py:410
  84.3 1.7 %collective-permute-done.16.other_ref = f32[800,128]{1,0:T(8,128)S(1)} collective-permute-done((f32[800,128]{1,0:T(8,128)S(1)}, f32[800,128]{1,0:T(8,128)S(1)}, u32[]{:S(2)}, u32[]{:S(2)}) %collective-permute-start.16) | collective-permute-done | bytes 409632 | tf_op jit(solution)/shard_map/ppermute | solution.py:410
  86.0 1.2 %relations.1 = (f32[400,500]{1,0:T(8,128)}, f32[1,500]{1,0:T(1,128)}) custom-call(f32[400,500]{1,0:T(8,128)S(1)} %get-tuple-element.108.rel_ref, f32[1,500]{1,0:T(1,128)S(1)} %get-tuple-element.109.state_ref, f32[800,128]{1,0:T(8,128)S(1)} %join.7.mine_ref, f32[800,128]{1,0:T(8,128)S(1)} %collective-permute-done.16.other_ref), custom_call_target="tpu_custom_call" | custom-call | tf_op jit(solution)/shard_map/relations/pallas_call | solution.py:395
  (51 shorter events, 6.2 us)
Async XLA Ops:
  0.7 1.6 %copy-start.2 = (f32[512,400]{0,1:T(8,128)S(1)}, f32[512,400]{0,1:T(8,128)}, u32[]{:S(2)}) copy-start(f32[512,400]{0,1:T(8,128)} %param.12) | copy-start | bytes 2457604
  0.7 1.6 %copy-start.4 = (s32[2,1024]{1,0:T(2,128)S(1)}, s32[2,1024]{1,0:T(2,128)}, u32[]{:S(2)}) copy-start(s32[2,1024]{1,0:T(2,128)} %src_ref.7) | copy-start | bytes 24580
  0.7 1.6 %copy-start.3 = (s32[2,1024]{1,0:T(2,128)S(1)}, s32[2,1024]{1,0:T(2,128)}, u32[]{:S(2)}) copy-start(s32[2,1024]{1,0:T(2,128)} %kind_ref.3) | copy-start | bytes 24580
  0.7 1.6 %copy-start.5 = (s32[2,1024]{1,0:T(2,128)S(1)}, s32[2,1024]{1,0:T(2,128)}, u32[]{:S(2)}) copy-start(s32[2,1024]{1,0:T(2,128)} %dst_ref.7) | copy-start | bytes 24580
  2.3 10.4 %copy-start.8 = (f32[512]{0:T(512)S(1)}, f32[512]{0:T(512)}, u32[]{:S(2)}) copy-start(f32[512]{0:T(512)} %param.11) | copy-start | bytes 6148
  2.3 10.4 %copy-start.9 = (f32[512]{0:T(512)S(1)}, f32[512]{0:T(512)}, u32[]{:S(2)}) copy-start(f32[512]{0:T(512)} %param.13) | copy-start | bytes 6148
  7.8 1.9 %collective-permute-start = (f32[800,128]{1,0:T(8,128)S(1)}, f32[800,128]{1,0:T(8,128)S(1)}, u32[]{:S(2)}, u32[]{:S(2)}) collective-permute-start(f32[800,128]{1,0:T(8,128)S(1)} %get-tuple-element.61), channel_id=1, source_target_pairs={{0,1},{1,0},{2,3},{3,2},{4,5},{5,4},{6,7},{7,6},{8,9},{9,8},{10,11... | collective-permute-start | bytes 1228808 | tf_op jit(solution)/shard_map/ppermute | solution.py:410
  9.8 8.4 %collective-permute-start.1 = (f32[400,128]{1,0:T(8,128)S(1)}, f32[400,128]{1,0:T(8,128)S(1)}, u32[]{:S(2)}, u32[]{:S(2)}) collective-permute-start(f32[400,128]{1,0:T(8,128)S(1)} %get-tuple-element.63), channel_id=1, source_target_pairs={{0,2},{1,3},{2,0},{3,1},{4,6},{5,7},{6,4},{7,5},{8,10},{9,11},{10,... | collective-permute-start | bytes 614408 | tf_op jit(solution)/shard_map/ppermute | solution.py:410
  15.3 15.1 %collective-permute-start.4 = (f32[136,512]{1,0:T(8,128)S(1)}, f32[136,512]{1,0:T(8,128)S(1)}, u32[]{:S(2)}, u32[]{:S(2)}) collective-permute-start(f32[136,512]{1,0:T(8,128)S(1)} %get-tuple-element.77), channel_id=1, source_target_pairs={{0,1},{1,2},{2,3},{3,4},{4,5},{5,6},{6,7},{7,8},{8,9},{9,10},{10,1... | collective-permute-start | bytes 835592 | tf_op jit(solution)/shard_map/ppermute | solution.py:497
  18.2 4.7 %collective-permute-start.2 = (f32[200,128]{1,0:T(8,128)S(1)}, f32[200,128]{1,0:T(8,128)S(1)}, u32[]{:S(2)}, u32[]{:S(2)}) collective-permute-start(f32[200,128]{1,0:T(8,128)S(1)} %get-tuple-element.74), channel_id=1, source_target_pairs={{0,4},{1,5},{2,6},{3,7},{4,0},{5,1},{6,2},{7,3},{8,12},{9,13},{10,... | collective-permute-start | bytes 307208 | tf_op jit(solution)/shard_map/ppermute | solution.py:410
  20.0 15.2 %collective-permute-start.6 = (f32[136,512]{1,0:T(8,128)S(1)}, f32[136,512]{1,0:T(8,128)S(1)}, u32[]{:S(2)}, u32[]{:S(2)}) collective-permute-start(f32[136,512]{1,0:T(8,128)S(1)} %get-tuple-element.80), channel_id=1, source_target_pairs={{0,1},{1,2},{2,3},{3,4},{4,5},{5,6},{6,7},{7,8},{8,9},{9,10},{10,1... | collective-permute-start | bytes 835592 | tf_op jit(solution)/shard_map/ppermute | solution.py:497
  22.9 7.5 %collective-permute-start.3 = (f32[200,128]{1,0:T(8,128)S(1)}, f32[200,128]{1,0:T(8,128)S(1)}, u32[]{:S(2)}, u32[]{:S(2)}) collective-permute-start(f32[200,128]{1,0:T(8,128)S(1)} %add.12), channel_id=1, source_target_pairs={{0,8},{1,9},{2,10},{3,11},{4,12},{5,13},{6,14},{7,15},{8,0},{9,1},... | collective-permute-start | bytes 307208 | tf_op jit(solution)/shard_map/ppermute | solution.py:410
  30.4 4.7 %collective-permute-start.5 = (f32[200,128]{1,0:T(8,128)S(1)}, f32[200,128]{1,0:T(8,128)S(1)}, u32[]{:S(2)}, u32[]{:S(2)}) collective-permute-start(f32[200,128]{1,0:T(8,128)S(1)} %add.13.mine_ref), channel_id=1, source_target_pairs={{0,4},{1,5},{2,6},{3,7},{4,0},{5,1},{6,2},{7,3},{8,12},{9,13},{10,... | collective-permute-start | bytes 307208 | tf_op jit(solution)/shard_map/ppermute | solution.py:410
  30.6 16.8 %collective-permute-start.8 = (f32[136,512]{1,0:T(8,128)S(1)}, f32[136,512]{1,0:T(8,128)S(1)}, u32[]{:S(2)}, u32[]{:S(2)}) collective-permute-start(f32[136,512]{1,0:T(8,128)S(1)} %get-tuple-element.82), channel_id=1, source_target_pairs={{0,1},{1,2},{2,3},{3,4},{4,5},{5,6},{6,7},{7,8},{8,9},{9,10},{10,1... | collective-permute-start | bytes 835592 | tf_op jit(solution)/shard_map/ppermute | solution.py:497
  35.2 12.1 %collective-permute-start.7 = (f32[400,128]{1,0:T(8,128)S(1)}, f32[400,128]{1,0:T(8,128)S(1)}, u32[]{:S(2)}, u32[]{:S(2)}) collective-permute-start(f32[400,128]{1,0:T(8,128)S(1)} %join.4.mine_ref), channel_id=1, source_target_pairs={{0,2},{1,3},{2,0},{3,1},{4,6},{5,7},{6,4},{7,5},{8,10},{9,11},{10,... | collective-permute-start | bytes 614408 | tf_op jit(solution)/shard_map/ppermute | solution.py:410
  47.4 1.8 %copy-start.6 = (f32[500]{0:T(512)S(1)}, f32[500]{0:T(512)}, u32[]{:S(2)}) copy-start(f32[500]{0:T(512)} %param.15) | copy-start | bytes 6004
  47.4 1.8 %collective-permute-start.9 = (f32[800,128]{1,0:T(8,128)S(1)}, f32[800,128]{1,0:T(8,128)S(1)}, u32[]{:S(2)}, u32[]{:S(2)}) collective-permute-start(f32[800,128]{1,0:T(8,128)S(1)} %join.5.mine_ref), channel_id=1, source_target_pairs={{0,1},{1,0},{2,3},{3,2},{4,5},{5,4},{6,7},{7,6},{8,9},{9,8},{10,11... | collective-permute-start | bytes 1228808 | tf_op jit(solution)/shard_map/ppermute | solution.py:410
  53.6 1.8 %collective-permute-start.10 = (f32[800,128]{1,0:T(8,128)S(1)}, f32[800,128]{1,0:T(8,128)S(1)}, u32[]{:S(2)}, u32[]{:S(2)}) collective-permute-start(f32[800,128]{1,0:T(8,128)S(1)} %get-tuple-element.92), channel_id=1, source_target_pairs={{0,1},{1,0},{2,3},{3,2},{4,5},{5,4},{6,7},{7,6},{8,9},{9,8},{10,11... | collective-permute-start | bytes 1228808 | tf_op jit(solution)/shard_map/ppermute | solution.py:410
  55.4 7.2 %collective-permute-start.11 = (f32[400,128]{1,0:T(8,128)S(1)}, f32[400,128]{1,0:T(8,128)S(1)}, u32[]{:S(2)}, u32[]{:S(2)}) collective-permute-start(f32[400,128]{1,0:T(8,128)S(1)} %get-tuple-element.94), channel_id=1, source_target_pairs={{0,2},{1,3},{2,0},{3,1},{4,6},{5,7},{6,4},{7,5},{8,10},{9,11},{10,... | collective-permute-start | bytes 614408 | tf_op jit(solution)/shard_map/ppermute | solution.py:410
  62.7 4.7 %collective-permute-start.12 = (f32[200,128]{1,0:T(8,128)S(1)}, f32[200,128]{1,0:T(8,128)S(1)}, u32[]{:S(2)}, u32[]{:S(2)}) collective-permute-start(f32[200,128]{1,0:T(8,128)S(1)} %get-tuple-element.111), channel_id=1, source_target_pairs={{0,4},{1,5},{2,6},{3,7},{4,0},{5,1},{6,2},{7,3},{8,12},{9,13},{10,... | collective-permute-start | bytes 307208 | tf_op jit(solution)/shard_map/ppermute | solution.py:410
  67.4 6.2 %collective-permute-start.13 = (f32[200,128]{1,0:T(8,128)S(1)}, f32[200,128]{1,0:T(8,128)S(1)}, u32[]{:S(2)}, u32[]{:S(2)}) collective-permute-start(f32[200,128]{1,0:T(8,128)S(1)} %add.14), channel_id=1, source_target_pairs={{0,8},{1,9},{2,10},{3,11},{4,12},{5,13},{6,14},{7,15},{8,0},{9,1},... | collective-permute-start | bytes 307208 | tf_op jit(solution)/shard_map/ppermute | solution.py:410
  73.6 4.7 %collective-permute-start.14 = (f32[200,128]{1,0:T(8,128)S(1)}, f32[200,128]{1,0:T(8,128)S(1)}, u32[]{:S(2)}, u32[]{:S(2)}) collective-permute-start(f32[200,128]{1,0:T(8,128)S(1)} %add.15.mine_ref), channel_id=1, source_target_pairs={{0,4},{1,5},{2,6},{3,7},{4,0},{5,1},{6,2},{7,3},{8,12},{9,13},{10,... | collective-permute-start | bytes 307208 | tf_op jit(solution)/shard_map/ppermute | solution.py:410
  78.3 5.8 %collective-permute-start.15 = (f32[400,128]{1,0:T(8,128)S(1)}, f32[400,128]{1,0:T(8,128)S(1)}, u32[]{:S(2)}, u32[]{:S(2)}) collective-permute-start(f32[400,128]{1,0:T(8,128)S(1)} %join.6.mine_ref), channel_id=1, source_target_pairs={{0,2},{1,3},{2,0},{3,1},{4,6},{5,7},{6,4},{7,5},{8,10},{9,11},{10,... | collective-permute-start | bytes 614408 | tf_op jit(solution)/shard_map/ppermute | solution.py:410
  84.2 1.8 %collective-permute-start.16 = (f32[800,128]{1,0:T(8,128)S(1)}, f32[800,128]{1,0:T(8,128)S(1)}, u32[]{:S(2)}, u32[]{:S(2)}) collective-permute-start(f32[800,128]{1,0:T(8,128)S(1)} %join.7.mine_ref), channel_id=1, source_target_pairs={{0,1},{1,0},{2,3},{3,2},{4,5},{5,4},{6,7},{7,6},{8,9},{9,8},{10,11... | collective-permute-start | bytes 1228808 | tf_op jit(solution)/shard_map/ppermute | solution.py:410
  (3 other events, 3.7 us)

commit v5 on v4

--- a/solution.py
+++ b/solution.py
@@ -488,6 +488,121 @@
         total, got = exchange(total, 1 << level)
         total = join(level, total, got)
     total, got = exchange(total, 1)
+    rolled += [roll(piece) for piece in waiting]
+    return total, got, beside, rolled, picked
+
+
+def two_parts(rows):
+    first = -(-rows // 64) * 32
+    return first, rows - first
+
+
+def part_kernel(levels, sizes, *refs):
+    if len(refs) == 6:
+        keep_ref, got_ref, *outs = refs
+        values = (keep_ref, got_ref), (keep_ref, got_ref)
+        starts = (0, sizes[0])
+    else:
+        values, outs = (refs[0:2], refs[2:4]), refs[4:]
+        starts = (0, 0)
+    for k, ((keep, got), start) in enumerate(zip(values, starts)):
+        kept, sent = outs[2 * k], outs[2 * k + 1]
+        half = kept.shape[0]
+        own, others = place(levels[k], half)
+        for at, out in ((own, kept), (others, sent)):
+            rows = pl.ds(pl.multiple_of(start + at, 8), half)
+            out[...] = keep[rows, :] + got[rows, :]
+
+
+def split_parts(levels, sizes, arrays):
+    lanes = arrays[0].shape[1]
+    return pl.pallas_call(
+        functools.partial(part_kernel, levels, sizes),
+        out_shape=[shape(sizes[k] // 2, lanes) for k in (0, 0, 1, 1)],
+        in_specs=[VMEM] * len(arrays),
+        out_specs=[VMEM] * 4,
+        compiler_params=settings(4),
+        cost_estimate=cost(arrays[0].size // 2, 16 * arrays[0].size),
+        name="halve",
+    )(*arrays)
+
+
+def add_kernel(keep_a, got_a, keep_b, got_b, total):
+    rows = keep_a.shape[0]
+    total[0:rows, :] = keep_a[...] + got_a[...]
+    total[rows:, :] = keep_b[...] + got_b[...]
+
+
+def apart_kernel(total, got, part_a, part_b):
+    rows = part_a.shape[0]
+    part_a[...] = total[0:rows, :] + got[0:rows, :]
+    part_b[...] = total[rows:, :] + got[rows:, :]
+
+
+def join_parts_kernel(levels, mine_a, got_a, mine_b, got_b, *outs):
+    start = 0
+    for k, (mine, got) in enumerate(((mine_a, got_a), (mine_b, got_b))):
+        half = mine.shape[0]
+        own, others = place(levels[k], half)
+        out = outs[k if len(outs) == 2 else 0]
+        out[pl.ds(pl.multiple_of(start + own, 8), half), :] = mine[...]
+        out[pl.ds(pl.multiple_of(start + others, 8), half), :] = got[...]
+        start += 2 * half if len(outs) == 1 else 0
+
+
+def small(kernel, name, rows, *arrays):
+    lanes = arrays[0].shape[1]
+    return pl.pallas_call(
+        kernel,
+        out_shape=[shape(count, lanes) for count in rows],
+        in_specs=[VMEM] * len(arrays),
+        out_specs=[VMEM] * len(rows),
+        compiler_params=settings(4),
+        cost_estimate=cost(sum(rows) * lanes, 12 * sum(rows) * lanes),
+        name=name,
+    )(*arrays)
+
+
+def reduce_parts(keep, send, beside, pieces, picked):
+    levels = (lax.axis_size("blk") - 1).bit_length()
+    waiting, rolled, count = list(pieces), [], 0
+
+    def exchange(values, distances):
+        nonlocal waiting, count
+        due = count - LAG
+        count += 1
+        if 0 <= due < len(rolled):
+            values, rolled[due] = lax.optimization_barrier((values, rolled[due]))
+        if rolled and waiting:
+            values, waiting = lax.optimization_barrier((values, waiting))
+        got = [swap(value, distance) for value, distance in zip(values, distances)]
+        if waiting:
+            rolled.append(roll(waiting.pop(0)))
+        return values, got
+
+    sizes = two_parts(keep.shape[0])
+    got = swap(send, 1)
+    keep_a, send_a, keep_b, send_b = split_parts((1, 2), sizes, (keep, got))
+    _, (got_a, got_b) = exchange([send_a, send_b], (2, 4))
+    halves = tuple(size // 2 for size in sizes)
+    keep_a, send_a, keep_b, send_b = split_parts((2, 1), halves, (keep_a, got_a, keep_b, got_b))
+    (send_a, send_b), beside = lax.optimization_barrier(([send_a, send_b], beside))
+    _, (got_a, got_b) = exchange([send_a, send_b], (4, 2))
+    quarters = tuple(size // 4 for size in sizes)
+    (total,) = small(add_kernel, "add", [sum(quarters)], keep_a, got_a, keep_b, got_b)
+    for level in range(3, levels - 1):
+        (total,), (got,) = exchange([total], (1 << level,))
+        total = total + got
+    (total,), (got,) = exchange([total], (1 << (levels - 1),))
+    parts = small(apart_kernel, "apart", quarters, total, got)
+    (part_a, part_b), (got_a, got_b) = exchange(list(parts), (4, 2))
+    join = functools.partial(join_parts_kernel, (2, 1))
+    parts = small(join, "join", halves, part_a, got_a, part_b, got_b)
+    parts, picked = lax.optimization_barrier((list(parts), picked))
+    (part_a, part_b), (got_a, got_b) = exchange(parts, (2, 4))
+    join = functools.partial(join_parts_kernel, (1, 2))
+    (total,) = small(join, "join", [sum(sizes)], part_a, got_a, part_b, got_b)
+    (total,), (got,) = exchange([total], (1,))
     rolled += [roll(piece) for piece in waiting]
     return total, got, beside, rolled, picked
 
@@ -531,7 +646,7 @@
         )
         beside, pieces = ((heads,), rest) if joined else ((heads, *rest), [])
         h = pick_heads(step + 1, heads, edge_src) if joined else None
-        mine, other, beside, tails, h = reduce_halves(keep, send, beside, pieces, h)
+        mine, other, beside, tails, h = (reduce_halves if joined else reduce_parts)(keep, send, beside, pieces, h)
         if joined:
             tail_state = tails[-1][-8:-7]
         else:

time: 87.4 us -> 86.9 us (level)
  waiting for transfers between devices: 45.6 us -> 42.8 us
  starting transfers between devices: 19.6 us -> 21.8 us
    ppermute x14 -> x18, waiting for transfers between devices: 45.5 us -> 42.8 us  [swap(): return lax.ppermute(value, 'blk', [(i, i ^ distance) for i in range(count)])]
    ppermute x14 -> x18, starting transfers between devices: 19.4 us -> 21.6 us  [swap(): return lax.ppermute(value, 'blk', [(i, i ^ distance) for i in range(count)])]
  transfers between devices with their start and end apart: 17 -> 21, of which waited for: 14 -> 14; matrix products, arithmetic and copies ran while one was open for 0% -> 0% of each run, Pallas kernels for 9% -> 10%
where the time goes in v5:
time: 86.9 us; the launch traced here: 86.6 us
  waiting for transfers between devices  42.8 us (49%)
  starting transfers between devices  21.8 us (25%)
  Pallas kernels  20.1 us (23%)
  local copies, waits for them, and re-layouts  1.09 us (1%)
  between operations  0.87 us (1%)
    ppermute x18, waiting for transfers between devices, swap(): return lax.ppermute(value, 'blk', [(i, i ^ distance) for i in range(count)])  42.8 us
    ppermute x18, starting transfers between devices, swap(): return lax.ppermute(value, 'blk', [(i, i ^ distance) for i in range(count)])  21.6 us
    pallas_call x2, Pallas kernels, back(): pl.pallas_call(functools.partial(back_kernel, step, len(tails)), out_shap...  6.12 us
    pallas_call x1, Pallas kernels, front(): pl.pallas_call(functools.partial(front_kernel, step), out_shape=made_shap...  5.49 us
    pallas_call x1, Pallas kernels, main(): pl.pallas_call(functools.partial(main_kernel, step), out_shape=[shape(*re...  4.37 us
  transfers between devices with their start and end apart: 21, of which 14 were waited for; matrix products, arithmetic and copies ran while one was open for 0% of the time, Pallas kernels for 10%

profile of v5, /device:TPU:0, one launch (start us, length us, event | category | flops | bytes accessed | tf_op | source)
XLA Modules:
  0.0 86.6 jit_solution(15259550755873297060)
XLA Ops:
  2.3 5.5 %front.1 = (f32[800,128]{1,0:T(8,128)S(1)}, f32[800,128]{1,0:T(8,128)S(1)}, f32[400,1024]{1,0:T(8,128)S(1)}, f32[400,1024]{1,0:T(8,128)S(1)}, bf16[512,1024]{1,0:T(8,128)(2,1)S(1)}, /*index=5*/f32[1,1024]{1,0:T(1,128)S(1)}) custom-call(f32[400,512]{1,0:T(8,128)S(1)} %bitcast.14, f32[400,500]{1,0:T(8,128)S(1)} %bitcast.12, f32[400,512]{1,0:T(8,128)S(1)} %bitcast.16, ...), custom_call_target="tpu_custom_call" | custom-call | tf_op jit(solution)/shard_map/front/pallas_call | solution.py:311
  8.3 1.4 %collective-permute-done.got_ref = f32[800,128]{1,0:T(8,128)S(1)} collective-permute-done((f32[800,128]{1,0:T(8,128)S(1)}, f32[800,128]{1,0:T(8,128)S(1)}, u32[]{:S(2)}, u32[]{:S(2)}) %collective-permute-start) | collective-permute-done | bytes 409632 | tf_op jit(solution)/shard_map/ppermute | solution.py:410
  9.8 2.9 %collective-permute-start.1 = (f32[400,128]{1,0:T(8,128)S(1)}, f32[400,128]{1,0:T(8,128)S(1)}, u32[]{:S(2)}, u32[]{:S(2)}) collective-permute-start(f32[400,128]{1,0:T(8,128)S(1)} %get-tuple-element.72), channel_id=1, source_target_pairs={{0,2},{1,3},{2,0},{3,1},{4,6},{5,7},{6,4},{7,5},{8,10},{9,11},{10,... | collective-permute-start | bytes 614408 | tf_op jit(solution)/shard_map/ppermute | solution.py:410
  12.7 2.6 %back.2 = (f32[400,512]{1,0:T(8,128)S(1)}, f32[1,512]{1,0:T(1,128)S(1)}, f32[136,512]{1,0:T(8,128)S(1)}, f32[136,512]{1,0:T(8,128)S(1)}, f32[136,512]{1,0:T(8,128)S(1)}) custom-call(f32[400,512]{1,0:T(8,128)S(1)} %bitcast.15, f32[1,512]{1,0:T(1,128)S(1)} %bitcast.19, f32[1,512]{1,0:T(1,128)S(1)} %bitcast.20, s32[2,1024]{1,0:T(2,128)S(1)} %copy-done.4, ...), custom_call_target="tpu_custom_call" | custom-call | flops 2097152000 | bytes 4915200 | tf_op jit(solution)/shard_map/back/pallas_call | solution.py:382
  15.4 2.8 %collective-permute-done.1.got_ref = f32[400,128]{1,0:T(8,128)S(1)} collective-permute-done((f32[400,128]{1,0:T(8,128)S(1)}, f32[400,128]{1,0:T(8,128)S(1)}, u32[]{:S(2)}, u32[]{:S(2)}) %collective-permute-start.1) | collective-permute-done | bytes 204832 | tf_op jit(solution)/shard_map/ppermute | solution.py:410
  18.2 1.8 %collective-permute-start.2 = (f32[200,128]{1,0:T(8,128)S(1)}, f32[200,128]{1,0:T(8,128)S(1)}, u32[]{:S(2)}, u32[]{:S(2)}) collective-permute-start(f32[200,128]{1,0:T(8,128)S(1)} %get-tuple-element.83), channel_id=1, source_target_pairs={{0,4},{1,5},{2,6},{3,7},{4,0},{5,1},{6,2},{7,3},{8,12},{9,13},{10,... | collective-permute-start | bytes 307208 | tf_op jit(solution)/shard_map/ppermute | solution.py:410
  20.0 2.9 %collective-permute-done.2 = f32[200,128]{1,0:T(8,128)S(1)} collective-permute-done((f32[200,128]{1,0:T(8,128)S(1)}, f32[200,128]{1,0:T(8,128)S(1)}, u32[]{:S(2)}, u32[]{:S(2)}) %collective-permute-start.2) | collective-permute-done | bytes 102432 | tf_op jit(solution)/shard_map/ppermute | solution.py:410
  22.9 2.8 %collective-permute-start.3 = (f32[200,128]{1,0:T(8,128)S(1)}, f32[200,128]{1,0:T(8,128)S(1)}, u32[]{:S(2)}, u32[]{:S(2)}) collective-permute-start(f32[200,128]{1,0:T(8,128)S(1)} %add.7), channel_id=1, source_target_pairs={{0,8},{1,9},{2,10},{3,11},{4,12},{5,13},{6,14},{7,15},{8,0},{9,1},... | collective-permute-start | bytes 307208 | tf_op jit(solution)/shard_map/ppermute | solution.py:410
  25.7 4.6 %collective-permute-done.3 = f32[200,128]{1,0:T(8,128)S(1)} collective-permute-done((f32[200,128]{1,0:T(8,128)S(1)}, f32[200,128]{1,0:T(8,128)S(1)}, u32[]{:S(2)}, u32[]{:S(2)}) %collective-permute-start.3) | collective-permute-done | bytes 102432 | tf_op jit(solution)/shard_map/ppermute | solution.py:410
  31.8 3.4 %collective-permute-done.5.got_ref = f32[200,128]{1,0:T(8,128)S(1)} collective-permute-done((f32[200,128]{1,0:T(8,128)S(1)}, f32[200,128]{1,0:T(8,128)S(1)}, u32[]{:S(2)}, u32[]{:S(2)}) %collective-permute-start.5) | collective-permute-done | bytes 102432 | tf_op jit(solution)/shard_map/ppermute | solution.py:410
  35.2 7.0 %collective-permute-start.7 = (f32[400,128]{1,0:T(8,128)S(1)}, f32[400,128]{1,0:T(8,128)S(1)}, u32[]{:S(2)}, u32[]{:S(2)}) collective-permute-start(f32[400,128]{1,0:T(8,128)S(1)} %join.4.mine_ref), channel_id=1, source_target_pairs={{0,2},{1,3},{2,0},{3,1},{4,6},{5,7},{6,4},{7,5},{8,10},{9,11},{10,... | collective-permute-start | bytes 614408 | tf_op jit(solution)/shard_map/ppermute | solution.py:410
  42.2 5.2 %collective-permute-done.7.got_ref = f32[400,128]{1,0:T(8,128)S(1)} collective-permute-done((f32[400,128]{1,0:T(8,128)S(1)}, f32[400,128]{1,0:T(8,128)S(1)}, u32[]{:S(2)}, u32[]{:S(2)}) %collective-permute-start.7) | collective-permute-done | bytes 204832 | tf_op jit(solution)/shard_map/ppermute | solution.py:410
  49.2 4.4 %main.1 = (f32[400,500]{1,0:T(8,128)S(1)}, f32[1,500]{1,0:T(1,128)S(1)}, f32[800,128]{1,0:T(8,128)S(1)}, f32[800,128]{1,0:T(8,128)S(1)}, f32[400,1024]{1,0:T(8,1...) custom-call(f32[400,500]{1,0:T(8,128)S(1)} %bitcast.13, ...), custom_call_target="tpu_custom_call" | custom-call | tf_op jit(solution)/shard_map/main/pallas_call | solution.py:360
  53.8 1.6 %collective-permute-done.10.refs_1_ = f32[800,128]{1,0:T(8,128)S(1)} collective-permute-done((f32[800,128]{1,0:T(8,128)S(1)}, f32[800,128]{1,0:T(8,128)S(1)}, u32[]{:S(2)}, u32[]{:S(2)}) %collective-permute-start.10) | collective-permute-done | bytes 409632 | tf_op jit(solution)/shard_map/ppermute | solution.py:410
  55.4 1.8 %collective-permute-start.11 = (f32[208,128]{1,0:T(8,128)S(1)}, f32[208,128]{1,0:T(8,128)S(1)}, u32[]{:S(2)}, u32[]{:S(2)}) collective-permute-start(f32[208,128]{1,0:T(8,128)S(1)} %get-tuple-element.103), channel_id=1, source_target_pairs={{0,2},{1,3},{2,0},{3,1},{4,6},{5,7},{6,4},{7,5},{8,10},{9,11},{10,... | collective-permute-start | bytes 319496 | tf_op jit(solution)/shard_map/ppermute | solution.py:410
  57.2 3.5 %back.3 = (f32[400,512]{1,0:T(8,128)}, f32[1,512]{1,0:T(1,128)}, f32[400,512]{1,0:T(8,128)}, f32[1,512]{1,0:T(1,128)}) custom-call(f32[400,512]{1,0:T(8,128)S(1)} %get-tuple-element.79.head_ref, f32[1,512]{1,0:T(1,128)S(1)} %get-tuple-element.108.head_state_ref, f32[1,512]{1,0:T(1,128)S(1)} %slice.3.tail_state_ref, s32[2,1024]{1,0:T(2,128)S(1)} %copy-done.4, ...), custom_call_target="tpu_custom_call" | custom-call | flops 2097152000 | bytes 4915200 | tf_op jit(solution)/shard_map/back/pallas_call | solution.py:382
  60.8 1.1 %collective-permute-done.12.refs_3_ = f32[192,128]{1,0:T(8,128)S(1)} collective-permute-done((f32[192,128]{1,0:T(8,128)S(1)}, f32[192,128]{1,0:T(8,128)S(1)}, u32[]{:S(2)}, u32[]{:S(2)}) %collective-permute-start.12) | collective-permute-done | bytes 98336 | tf_op jit(solution)/shard_map/ppermute | solution.py:410
  63.2 3.8 %collective-permute-done.14.got_b = f32[96,128]{1,0:T(8,128)S(1)} collective-permute-done((f32[96,128]{1,0:T(8,128)S(1)}, f32[96,128]{1,0:T(8,128)S(1)}, u32[]{:S(2)}, u32[]{:S(2)}) %collective-permute-start.14) | collective-permute-done | bytes 49184 | tf_op jit(solution)/shard_map/ppermute | solution.py:410
  67.1 6.6 %collective-permute-done.15.got = f32[200,128]{1,0:T(8,128)S(1)} collective-permute-done((f32[200,128]{1,0:T(8,128)S(1)}, f32[200,128]{1,0:T(8,128)S(1)}, u32[]{:S(2)}, u32[]{:S(2)}) %collective-permute-start.15) | collective-permute-done | bytes 102432 | tf_op jit(solution)/shard_map/ppermute | solution.py:410
  74.8 3.7 %collective-permute-done.17.got_b = f32[96,128]{1,0:T(8,128)S(1)} collective-permute-done((f32[96,128]{1,0:T(8,128)S(1)}, f32[96,128]{1,0:T(8,128)S(1)}, u32[]{:S(2)}, u32[]{:S(2)}) %collective-permute-start.17) | collective-permute-done | bytes 49184 | tf_op jit(solution)/shard_map/ppermute | solution.py:410
  79.0 1.4 %collective-permute-start.19 = (f32[192,128]{1,0:T(8,128)S(1)}, f32[192,128]{1,0:T(8,128)S(1)}, u32[]{:S(2)}, u32[]{:S(2)}) collective-permute-start(f32[192,128]{1,0:T(8,128)S(1)} %get-tuple-element.129.mine_b), channel_id=1, source_target_pairs={{0,4},{1,5},{2,6},{3,7},{4,0},{5,1},{6,2},{7,3},{8,12},{9,13},{10,... | collective-permute-start | bytes 294920 | tf_op jit(solution)/shard_map/ppermute | solution.py:410
  80.3 3.2 %collective-permute-done.19.got_b = f32[192,128]{1,0:T(8,128)S(1)} collective-permute-done((f32[192,128]{1,0:T(8,128)S(1)}, f32[192,128]{1,0:T(8,128)S(1)}, u32[]{:S(2)}, u32[]{:S(2)}) %collective-permute-start.19) | collective-permute-done | bytes 98336 | tf_op jit(solution)/shard_map/ppermute | solution.py:410
  83.7 1.7 %collective-permute-done.20.other_ref = f32[800,128]{1,0:T(8,128)S(1)} collective-permute-done((f32[800,128]{1,0:T(8,128)S(1)}, f32[800,128]{1,0:T(8,128)S(1)}, u32[]{:S(2)}, u32[]{:S(2)}) %collective-permute-start.20) | collective-permute-done | bytes 409632 | tf_op jit(solution)/shard_map/ppermute | solution.py:410
  85.4 1.2 %relations.1 = (f32[400,500]{1,0:T(8,128)}, f32[1,500]{1,0:T(1,128)}) custom-call(f32[400,500]{1,0:T(8,128)S(1)} %get-tuple-element.120.rel_ref, f32[1,500]{1,0:T(1,128)S(1)} %get-tuple-element.121.state_ref, f32[800,128]{1,0:T(8,128)S(1)} %join.7.mine_ref, f32[800,128]{1,0:T(8,128)S(1)} %collective-permute-done.20.other_ref), custom_call_target="tpu_custom_call" | custom-call | tf_op jit(solution)/shard_map/relations/pallas_call | solution.py:395
  (59 shorter events, 8.8 us)
Async XLA Ops:
  2.3 10.4 %copy-start.8 = (f32[512]{0:T(512)S(1)}, f32[512]{0:T(512)}, u32[]{:S(2)}) copy-start(f32[512]{0:T(512)} %param.11) | copy-start | bytes 6148
  2.3 10.4 %copy-start.9 = (f32[512]{0:T(512)S(1)}, f32[512]{0:T(512)}, u32[]{:S(2)}) copy-start(f32[512]{0:T(512)} %param.13) | copy-start | bytes 6148
  7.8 1.9 %collective-permute-start = (f32[800,128]{1,0:T(8,128)S(1)}, f32[800,128]{1,0:T(8,128)S(1)}, u32[]{:S(2)}, u32[]{:S(2)}) collective-permute-start(f32[800,128]{1,0:T(8,128)S(1)} %get-tuple-element.70), channel_id=1, source_target_pairs={{0,1},{1,0},{2,3},{3,2},{4,5},{5,4},{6,7},{7,6},{8,9},{9,8},{10,11... | collective-permute-start | bytes 1228808 | tf_op jit(solution)/shard_map/ppermute | solution.py:410
  9.8 8.4 %collective-permute-start.1 = (f32[400,128]{1,0:T(8,128)S(1)}, f32[400,128]{1,0:T(8,128)S(1)}, u32[]{:S(2)}, u32[]{:S(2)}) collective-permute-start(f32[400,128]{1,0:T(8,128)S(1)} %get-tuple-element.72), channel_id=1, source_target_pairs={{0,2},{1,3},{2,0},{3,1},{4,6},{5,7},{6,4},{7,5},{8,10},{9,11},{10,... | collective-permute-start | bytes 614408 | tf_op jit(solution)/shard_map/ppermute | solution.py:410
  15.3 15.1 %collective-permute-start.4 = (f32[136,512]{1,0:T(8,128)S(1)}, f32[136,512]{1,0:T(8,128)S(1)}, u32[]{:S(2)}, u32[]{:S(2)}) collective-permute-start(f32[136,512]{1,0:T(8,128)S(1)} %get-tuple-element.86), channel_id=1, source_target_pairs={{0,1},{1,2},{2,3},{3,4},{4,5},{5,6},{6,7},{7,8},{8,9},{9,10},{10,1... | collective-permute-start | bytes 835592 | tf_op jit(solution)/shard_map/ppermute | solution.py:612
  18.2 4.7 %collective-permute-start.2 = (f32[200,128]{1,0:T(8,128)S(1)}, f32[200,128]{1,0:T(8,128)S(1)}, u32[]{:S(2)}, u32[]{:S(2)}) collective-permute-start(f32[200,128]{1,0:T(8,128)S(1)} %get-tuple-element.83), channel_id=1, source_target_pairs={{0,4},{1,5},{2,6},{3,7},{4,0},{5,1},{6,2},{7,3},{8,12},{9,13},{10,... | collective-permute-start | bytes 307208 | tf_op jit(solution)/shard_map/ppermute | solution.py:410
  20.0 15.2 %collective-permute-start.6 = (f32[136,512]{1,0:T(8,128)S(1)}, f32[136,512]{1,0:T(8,128)S(1)}, u32[]{:S(2)}, u32[]{:S(2)}) collective-permute-start(f32[136,512]{1,0:T(8,128)S(1)} %get-tuple-element.89), channel_id=1, source_target_pairs={{0,1},{1,2},{2,3},{3,4},{4,5},{5,6},{6,7},{7,8},{8,9},{9,10},{10,1... | collective-permute-start | bytes 835592 | tf_op jit(solution)/shard_map/ppermute | solution.py:612
  22.9 7.5 %collective-permute-start.3 = (f32[200,128]{1,0:T(8,128)S(1)}, f32[200,128]{1,0:T(8,128)S(1)}, u32[]{:S(2)}, u32[]{:S(2)}) collective-permute-start(f32[200,128]{1,0:T(8,128)S(1)} %add.7), channel_id=1, source_target_pairs={{0,8},{1,9},{2,10},{3,11},{4,12},{5,13},{6,14},{7,15},{8,0},{9,1},... | collective-permute-start | bytes 307208 | tf_op jit(solution)/shard_map/ppermute | solution.py:410
  30.4 4.7 %collective-permute-start.5 = (f32[200,128]{1,0:T(8,128)S(1)}, f32[200,128]{1,0:T(8,128)S(1)}, u32[]{:S(2)}, u32[]{:S(2)}) collective-permute-start(f32[200,128]{1,0:T(8,128)S(1)} %add.8.mine_ref), channel_id=1, source_target_pairs={{0,4},{1,5},{2,6},{3,7},{4,0},{5,1},{6,2},{7,3},{8,12},{9,13},{10,... | collective-permute-start | bytes 307208 | tf_op jit(solution)/shard_map/ppermute | solution.py:410
  30.6 16.8 %collective-permute-start.8 = (f32[136,512]{1,0:T(8,128)S(1)}, f32[136,512]{1,0:T(8,128)S(1)}, u32[]{:S(2)}, u32[]{:S(2)}) collective-permute-start(f32[136,512]{1,0:T(8,128)S(1)} %get-tuple-element.91), channel_id=1, source_target_pairs={{0,1},{1,2},{2,3},{3,4},{4,5},{5,6},{6,7},{7,8},{8,9},{9,10},{10,1... | collective-permute-start | bytes 835592 | tf_op jit(solution)/shard_map/ppermute | solution.py:612
  35.2 12.1 %collective-permute-start.7 = (f32[400,128]{1,0:T(8,128)S(1)}, f32[400,128]{1,0:T(8,128)S(1)}, u32[]{:S(2)}, u32[]{:S(2)}) collective-permute-start(f32[400,128]{1,0:T(8,128)S(1)} %join.4.mine_ref), channel_id=1, source_target_pairs={{0,2},{1,3},{2,0},{3,1},{4,6},{5,7},{6,4},{7,5},{8,10},{9,11},{10,... | collective-permute-start | bytes 614408 | tf_op jit(solution)/shard_map/ppermute | solution.py:410
  47.4 1.8 %copy-start.6 = (f32[500]{0:T(512)S(1)}, f32[500]{0:T(512)}, u32[]{:S(2)}) copy-start(f32[500]{0:T(512)} %param.15) | copy-start | bytes 6004
  47.4 1.8 %collective-permute-start.9 = (f32[800,128]{1,0:T(8,128)S(1)}, f32[800,128]{1,0:T(8,128)S(1)}, u32[]{:S(2)}, u32[]{:S(2)}) collective-permute-start(f32[800,128]{1,0:T(8,128)S(1)} %join.5.mine_ref), channel_id=1, source_target_pairs={{0,1},{1,0},{2,3},{3,2},{4,5},{5,4},{6,7},{7,6},{8,9},{9,8},{10,11... | collective-permute-start | bytes 1228808 | tf_op jit(solution)/shard_map/ppermute | solution.py:410
  53.6 1.8 %collective-permute-start.10 = (f32[800,128]{1,0:T(8,128)S(1)}, f32[800,128]{1,0:T(8,128)S(1)}, u32[]{:S(2)}, u32[]{:S(2)}) collective-permute-start(f32[800,128]{1,0:T(8,128)S(1)} %get-tuple-element.101), channel_id=1, source_target_pairs={{0,1},{1,0},{2,3},{3,2},{4,5},{5,4},{6,7},{7,6},{8,9},{9,8},{10,11... | collective-permute-start | bytes 1228808 | tf_op jit(solution)/shard_map/ppermute | solution.py:410
  55.4 6.4 %collective-permute-start.11 = (f32[208,128]{1,0:T(8,128)S(1)}, f32[208,128]{1,0:T(8,128)S(1)}, u32[]{:S(2)}, u32[]{:S(2)}) collective-permute-start(f32[208,128]{1,0:T(8,128)S(1)} %get-tuple-element.103), channel_id=1, source_target_pairs={{0,2},{1,3},{2,0},{3,1},{4,6},{5,7},{6,4},{7,5},{8,10},{9,11},{10,... | collective-permute-start | bytes 319496 | tf_op jit(solution)/shard_map/ppermute | solution.py:410
  57.2 4.6 %collective-permute-start.12 = (f32[192,128]{1,0:T(8,128)S(1)}, f32[192,128]{1,0:T(8,128)S(1)}, u32[]{:S(2)}, u32[]{:S(2)}) collective-permute-start(f32[192,128]{1,0:T(8,128)S(1)} %get-tuple-element.105), channel_id=1, source_target_pairs={{0,4},{1,5},{2,6},{3,7},{4,0},{5,1},{6,2},{7,3},{8,12},{9,13},{10,... | collective-permute-start | bytes 294920 | tf_op jit(solution)/shard_map/ppermute | solution.py:410
  61.9 5.1 %collective-permute-start.13 = (f32[104,128]{1,0:T(8,128)S(1)}, f32[104,128]{1,0:T(8,128)S(1)}, u32[]{:S(2)}, u32[]{:S(2)}) collective-permute-start(f32[104,128]{1,0:T(8,128)S(1)} %get-tuple-element.123), channel_id=1, source_target_pairs={{0,4},{1,5},{2,6},{3,7},{4,0},{5,1},{6,2},{7,3},{8,12},{9,13},{10,... | collective-permute-start | bytes 159752 | tf_op jit(solution)/shard_map/ppermute | solution.py:410
  62.9 4.1 %collective-permute-start.14 = (f32[96,128]{1,0:T(8,128)S(1)}, f32[96,128]{1,0:T(8,128)S(1)}, u32[]{:S(2)}, u32[]{:S(2)}) collective-permute-start(f32[96,128]{1,0:T(8,128)S(1)} %get-tuple-element.125), channel_id=1, source_target_pairs={{0,2},{1,3},{2,0},{3,1},{4,6},{5,7},{6,4},{7,5},{8,10},{9,11},{10,... | collective-permute-start | bytes 147464 | tf_op jit(solution)/shard_map/ppermute | solution.py:410
  67.0 6.7 %collective-permute-start.15 = (f32[200,128]{1,0:T(8,128)S(1)}, f32[200,128]{1,0:T(8,128)S(1)}, u32[]{:S(2)}, u32[]{:S(2)}) collective-permute-start(f32[200,128]{1,0:T(8,128)S(1)} %add.9.total), channel_id=1, source_target_pairs={{0,8},{1,9},{2,10},{3,11},{4,12},{5,13},{6,14},{7,15},{8,0},{9,1},... | collective-permute-start | bytes 307208 | tf_op jit(solution)/shard_map/ppermute | solution.py:410
  73.8 4.7 %collective-permute-start.16 = (f32[104,128]{1,0:T(8,128)S(1)}, f32[104,128]{1,0:T(8,128)S(1)}, u32[]{:S(2)}, u32[]{:S(2)}) collective-permute-start(f32[104,128]{1,0:T(8,128)S(1)} %get-tuple-element.126.mine_a), channel_id=1, source_target_pairs={{0,4},{1,5},{2,6},{3,7},{4,0},{5,1},{6,2},{7,3},{8,12},{9,13},{10,... | collective-permute-start | bytes 159752 | tf_op jit(solution)/shard_map/ppermute | solution.py:410
  74.4 4.1 %collective-permute-start.17 = (f32[96,128]{1,0:T(8,128)S(1)}, f32[96,128]{1,0:T(8,128)S(1)}, u32[]{:S(2)}, u32[]{:S(2)}) collective-permute-start(f32[96,128]{1,0:T(8,128)S(1)} %get-tuple-element.127.mine_b), channel_id=1, source_target_pairs={{0,2},{1,3},{2,0},{3,1},{4,6},{5,7},{6,4},{7,5},{8,10},{9,11},{10,... | collective-permute-start | bytes 147464 | tf_op jit(solution)/shard_map/ppermute | solution.py:410
  78.5 5.1 %collective-permute-start.18 = (f32[208,128]{1,0:T(8,128)S(1)}, f32[208,128]{1,0:T(8,128)S(1)}, u32[]{:S(2)}, u32[]{:S(2)}) collective-permute-start(f32[208,128]{1,0:T(8,128)S(1)} %get-tuple-element.128.mine_a), channel_id=1, source_target_pairs={{0,2},{1,3},{2,0},{3,1},{4,6},{5,7},{6,4},{7,5},{8,10},{9,11},{10,... | collective-permute-start | bytes 319496 | tf_op jit(solution)/shard_map/ppermute | solution.py:410
  79.0 4.6 %collective-permute-start.19 = (f32[192,128]{1,0:T(8,128)S(1)}, f32[192,128]{1,0:T(8,128)S(1)}, u32[]{:S(2)}, u32[]{:S(2)}) collective-permute-start(f32[192,128]{1,0:T(8,128)S(1)} %get-tuple-element.129.mine_b), channel_id=1, source_target_pairs={{0,4},{1,5},{2,6},{3,7},{4,0},{5,1},{6,2},{7,3},{8,12},{9,13},{10,... | collective-permute-start | bytes 294920 | tf_op jit(solution)/shard_map/ppermute | solution.py:410
  83.6 1.8 %collective-permute-start.20 = (f32[800,128]{1,0:T(8,128)S(1)}, f32[800,128]{1,0:T(8,128)S(1)}, u32[]{:S(2)}, u32[]{:S(2)}) collective-permute-start(f32[800,128]{1,0:T(8,128)S(1)} %join.7.mine_ref), channel_id=1, source_target_pairs={{0,1},{1,0},{2,3},{3,2},{4,5},{5,4},{6,7},{7,6},{8,9},{9,8},{10,11... | collective-permute-start | bytes 1228808 | tf_op jit(solution)/shard_map/ppermute | solution.py:410
  (7 other events, 10.2 us)

commit v6 on v5

--- a/solution.py
+++ b/solution.py
@@ -473,17 +473,17 @@
         return value, got
 
     got = swap(send, 1)
-    for level in range(1, splits):
+    for level in range(splits - 1, 0, -1):
         keep, send = halve(level, keep, got)
-        if level == 2:
+        if level == splits - 2:
             send, beside = lax.optimization_barrier((send, beside))
         send, got = exchange(send, 1 << level)
     total = keep + got
     for level in range(splits, levels):
         total, got = exchange(total, 1 << level)
         total = total + got
-    for level in reversed(range(1, splits)):
-        if level == 1:
+    for level in range(1, splits):
+        if level == splits - 1:
             total, picked = lax.optimization_barrier((total, picked))
         total, got = exchange(total, 1 << level)
         total = join(level, total, got)

time: 86.9 us -> 86 us (0.990)
  no operation moved by 1% of the time
where the time goes in v6:
time: 86 us; the launch traced here: 85.8 us
  waiting for transfers between devices  42.3 us (49%)
  starting transfers between devices  21.5 us (25%)
  Pallas kernels  20.1 us (23%)
  local copies, waits for them, and re-layouts  1.09 us (1%)
  between operations  0.86 us (1%)
    ppermute x18, waiting for transfers between devices, swap(): return lax.ppermute(value, 'blk', [(i, i ^ distance) for i in range(count)])  42.3 us
    ppermute x18, starting transfers between devices, swap(): return lax.ppermute(value, 'blk', [(i, i ^ distance) for i in range(count)])  21.4 us
    pallas_call x2, Pallas kernels, back(): pl.pallas_call(functools.partial(back_kernel, step, len(tails)), out_shap...  6.12 us
    pallas_call x1, Pallas kernels, front(): pl.pallas_call(functools.partial(front_kernel, step), out_shape=made_shap...  5.49 us
    pallas_call x1, Pallas kernels, main(): pl.pallas_call(functools.partial(main_kernel, step), out_shape=[shape(*re...  4.37 us
  transfers between devices with their start and end apart: 21, of which 14 were waited for; matrix products, arithmetic and copies ran while one was open for 0% of the time, Pallas kernels for 10%

profile of v6, /device:TPU:0, one launch (start us, length us, event | category | flops | bytes accessed | tf_op | source)
XLA Modules:
  0.0 85.8 jit_solution(10084024370945983196)
XLA Ops:
  2.3 5.5 %front.1 = (f32[800,128]{1,0:T(8,128)S(1)}, f32[800,128]{1,0:T(8,128)S(1)}, f32[400,1024]{1,0:T(8,128)S(1)}, f32[400,1024]{1,0:T(8,128)S(1)}, bf16[512,1024]{1,0:T(8,128)(2,1)S(1)}, /*index=5*/f32[1,1024]{1,0:T(1,128)S(1)}) custom-call(f32[400,512]{1,0:T(8,128)S(1)} %bitcast.14, f32[400,500]{1,0:T(8,128)S(1)} %bitcast.12, f32[400,512]{1,0:T(8,128)S(1)} %bitcast.16, ...), custom_call_target="tpu_custom_call" | custom-call | tf_op jit(solution)/shard_map/front/pallas_call | solution.py:311
  8.3 1.4 %collective-permute-done.got_ref = f32[800,128]{1,0:T(8,128)S(1)} collective-permute-done((f32[800,128]{1,0:T(8,128)S(1)}, f32[800,128]{1,0:T(8,128)S(1)}, u32[]{:S(2)}, u32[]{:S(2)}) %collective-permute-start) | collective-permute-done | bytes 409632 | tf_op jit(solution)/shard_map/ppermute | solution.py:410
  9.8 3.0 %collective-permute-start.1 = (f32[400,128]{1,0:T(8,128)S(1)}, f32[400,128]{1,0:T(8,128)S(1)}, u32[]{:S(2)}, u32[]{:S(2)}) collective-permute-start(f32[400,128]{1,0:T(8,128)S(1)} %get-tuple-element.72), channel_id=1, source_target_pairs={{0,4},{1,5},{2,6},{3,7},{4,0},{5,1},{6,2},{7,3},{8,12},{9,13},{10,... | collective-permute-start | bytes 614408 | tf_op jit(solution)/shard_map/ppermute | solution.py:410
  12.8 2.6 %back.2 = (f32[400,512]{1,0:T(8,128)S(1)}, f32[1,512]{1,0:T(1,128)S(1)}, f32[136,512]{1,0:T(8,128)S(1)}, f32[136,512]{1,0:T(8,128)S(1)}, f32[136,512]{1,0:T(8,128)S(1)}) custom-call(f32[400,512]{1,0:T(8,128)S(1)} %bitcast.15, f32[1,512]{1,0:T(1,128)S(1)} %bitcast.19, f32[1,512]{1,0:T(1,128)S(1)} %bitcast.20, s32[2,1024]{1,0:T(2,128)S(1)} %copy-done.4, ...), custom_call_target="tpu_custom_call" | custom-call | flops 2097152000 | bytes 4915200 | tf_op jit(solution)/shard_map/back/pallas_call | solution.py:382
  15.5 2.7 %collective-permute-done.1.got_ref = f32[400,128]{1,0:T(8,128)S(1)} collective-permute-done((f32[400,128]{1,0:T(8,128)S(1)}, f32[400,128]{1,0:T(8,128)S(1)}, u32[]{:S(2)}, u32[]{:S(2)}) %collective-permute-start.1) | collective-permute-done | bytes 204832 | tf_op jit(solution)/shard_map/ppermute | solution.py:410
  18.2 1.8 %collective-permute-start.2 = (f32[200,128]{1,0:T(8,128)S(1)}, f32[200,128]{1,0:T(8,128)S(1)}, u32[]{:S(2)}, u32[]{:S(2)}) collective-permute-start(f32[200,128]{1,0:T(8,128)S(1)} %get-tuple-element.83), channel_id=1, source_target_pairs={{0,2},{1,3},{2,0},{3,1},{4,6},{5,7},{6,4},{7,5},{8,10},{9,11},{10,... | collective-permute-start | bytes 307208 | tf_op jit(solution)/shard_map/ppermute | solution.py:410
  19.9 5.7 %collective-permute-done.2 = f32[200,128]{1,0:T(8,128)S(1)} collective-permute-done((f32[200,128]{1,0:T(8,128)S(1)}, f32[200,128]{1,0:T(8,128)S(1)}, u32[]{:S(2)}, u32[]{:S(2)}) %collective-permute-start.2) | collective-permute-done | bytes 102432 | tf_op jit(solution)/shard_map/ppermute | solution.py:410
  25.7 4.5 %collective-permute-start.3 = (f32[200,128]{1,0:T(8,128)S(1)}, f32[200,128]{1,0:T(8,128)S(1)}, u32[]{:S(2)}, u32[]{:S(2)}) collective-permute-start(f32[200,128]{1,0:T(8,128)S(1)} %add.7), channel_id=1, source_target_pairs={{0,8},{1,9},{2,10},{3,11},{4,12},{5,13},{6,14},{7,15},{8,0},{9,1},... | collective-permute-start | bytes 307208 | tf_op jit(solution)/shard_map/ppermute | solution.py:410
  30.2 3.3 %collective-permute-done.3 = f32[200,128]{1,0:T(8,128)S(1)} collective-permute-done((f32[200,128]{1,0:T(8,128)S(1)}, f32[200,128]{1,0:T(8,128)S(1)}, u32[]{:S(2)}, u32[]{:S(2)}) %collective-permute-start.3) | collective-permute-done | bytes 102432 | tf_op jit(solution)/shard_map/ppermute | solution.py:410
  34.9 3.3 %collective-permute-done.5.got_ref = f32[200,128]{1,0:T(8,128)S(1)} collective-permute-done((f32[200,128]{1,0:T(8,128)S(1)}, f32[200,128]{1,0:T(8,128)S(1)}, u32[]{:S(2)}, u32[]{:S(2)}) %collective-permute-start.5) | collective-permute-done | bytes 102432 | tf_op jit(solution)/shard_map/ppermute | solution.py:410
  38.3 5.7 %collective-permute-done.7.got_ref = f32[400,128]{1,0:T(8,128)S(1)} collective-permute-done((f32[400,128]{1,0:T(8,128)S(1)}, f32[400,128]{1,0:T(8,128)S(1)}, u32[]{:S(2)}, u32[]{:S(2)}) %collective-permute-start.7) | collective-permute-done | bytes 204832 | tf_op jit(solution)/shard_map/ppermute | solution.py:410
  45.9 4.4 %main.1 = (f32[400,500]{1,0:T(8,128)S(1)}, f32[1,500]{1,0:T(1,128)S(1)}, f32[800,128]{1,0:T(8,128)S(1)}, f32[800,128]{1,0:T(8,128)S(1)}, f32[400,1024]{1,0:T(8,1...) custom-call(f32[400,500]{1,0:T(8,128)S(1)} %bitcast.13, ...), custom_call_target="tpu_custom_call" | custom-call | tf_op jit(solution)/shard_map/main/pallas_call | solution.py:360
  50.5 1.6 %collective-permute-done.10.refs_1_ = f32[800,128]{1,0:T(8,128)S(1)} collective-permute-done((f32[800,128]{1,0:T(8,128)S(1)}, f32[800,128]{1,0:T(8,128)S(1)}, u32[]{:S(2)}, u32[]{:S(2)}) %collective-permute-start.10) | collective-permute-done | bytes 409632 | tf_op jit(solution)/shard_map/ppermute | solution.py:410
  52.2 3.5 %collective-permute-start.11 = (f32[208,128]{1,0:T(8,128)S(1)}, f32[208,128]{1,0:T(8,128)S(1)}, u32[]{:S(2)}, u32[]{:S(2)}) collective-permute-start(f32[208,128]{1,0:T(8,128)S(1)} %get-tuple-element.103), channel_id=1, source_target_pairs={{0,2},{1,3},{2,0},{3,1},{4,6},{5,7},{6,4},{7,5},{8,10},{9,11},{10,... | collective-permute-start | bytes 319496 | tf_op jit(solution)/shard_map/ppermute | solution.py:410
  55.6 3.5 %back.3 = (f32[400,512]{1,0:T(8,128)}, f32[1,512]{1,0:T(1,128)}, f32[400,512]{1,0:T(8,128)}, f32[1,512]{1,0:T(1,128)}) custom-call(f32[400,512]{1,0:T(8,128)S(1)} %get-tuple-element.79.head_ref, f32[1,512]{1,0:T(1,128)S(1)} %get-tuple-element.108.head_state_ref, f32[1,512]{1,0:T(1,128)S(1)} %slice.3.tail_state_ref, s32[2,1024]{1,0:T(2,128)S(1)} %copy-done.4, ...), custom_call_target="tpu_custom_call" | custom-call | flops 2097152000 | bytes 4915200 | tf_op jit(solution)/shard_map/back/pallas_call | solution.py:382
  61.4 4.0 %collective-permute-done.14.got_b = f32[96,128]{1,0:T(8,128)S(1)} collective-permute-done((f32[96,128]{1,0:T(8,128)S(1)}, f32[96,128]{1,0:T(8,128)S(1)}, u32[]{:S(2)}, u32[]{:S(2)}) %collective-permute-start.14) | collective-permute-done | bytes 49184 | tf_op jit(solution)/shard_map/ppermute | solution.py:410
  65.4 2.2 %collective-permute-start.15 = (f32[200,128]{1,0:T(8,128)S(1)}, f32[200,128]{1,0:T(8,128)S(1)}, u32[]{:S(2)}, u32[]{:S(2)}) collective-permute-start(f32[200,128]{1,0:T(8,128)S(1)} %add.9.total), channel_id=1, source_target_pairs={{0,8},{1,9},{2,10},{3,11},{4,12},{5,13},{6,14},{7,15},{8,0},{9,1},... | collective-permute-start | bytes 307208 | tf_op jit(solution)/shard_map/ppermute | solution.py:410
  67.6 4.6 %collective-permute-done.15.got = f32[200,128]{1,0:T(8,128)S(1)} collective-permute-done((f32[200,128]{1,0:T(8,128)S(1)}, f32[200,128]{1,0:T(8,128)S(1)}, u32[]{:S(2)}, u32[]{:S(2)}) %collective-permute-start.15) | collective-permute-done | bytes 102432 | tf_op jit(solution)/shard_map/ppermute | solution.py:410
  72.3 1.3 %collective-permute-start.17 = (f32[96,128]{1,0:T(8,128)S(1)}, f32[96,128]{1,0:T(8,128)S(1)}, u32[]{:S(2)}, u32[]{:S(2)}) collective-permute-start(f32[96,128]{1,0:T(8,128)S(1)} %get-tuple-element.127.mine_b), channel_id=1, source_target_pairs={{0,2},{1,3},{2,0},{3,1},{4,6},{5,7},{6,4},{7,5},{8,10},{9,11},{10,... | collective-permute-start | bytes 147464 | tf_op jit(solution)/shard_map/ppermute | solution.py:410
  73.6 3.2 %collective-permute-done.17.got_b = f32[96,128]{1,0:T(8,128)S(1)} collective-permute-done((f32[96,128]{1,0:T(8,128)S(1)}, f32[96,128]{1,0:T(8,128)S(1)}, u32[]{:S(2)}, u32[]{:S(2)}) %collective-permute-start.17) | collective-permute-done | bytes 49184 | tf_op jit(solution)/shard_map/ppermute | solution.py:410
  76.9 1.2 %collective-permute-start.18 = (f32[208,128]{1,0:T(8,128)S(1)}, f32[208,128]{1,0:T(8,128)S(1)}, u32[]{:S(2)}, u32[]{:S(2)}) collective-permute-start(f32[208,128]{1,0:T(8,128)S(1)} %get-tuple-element.128.mine_a), channel_id=1, source_target_pairs={{0,2},{1,3},{2,0},{3,1},{4,6},{5,7},{6,4},{7,5},{8,10},{9,11},{10,... | collective-permute-start | bytes 319496 | tf_op jit(solution)/shard_map/ppermute | solution.py:410
  78.1 1.4 %collective-permute-start.19 = (f32[192,128]{1,0:T(8,128)S(1)}, f32[192,128]{1,0:T(8,128)S(1)}, u32[]{:S(2)}, u32[]{:S(2)}) collective-permute-start(f32[192,128]{1,0:T(8,128)S(1)} %get-tuple-element.129.mine_b), channel_id=1, source_target_pairs={{0,4},{1,5},{2,6},{3,7},{4,0},{5,1},{6,2},{7,3},{8,12},{9,13},{10,... | collective-permute-start | bytes 294920 | tf_op jit(solution)/shard_map/ppermute | solution.py:410
  79.6 3.2 %collective-permute-done.19.got_b = f32[192,128]{1,0:T(8,128)S(1)} collective-permute-done((f32[192,128]{1,0:T(8,128)S(1)}, f32[192,128]{1,0:T(8,128)S(1)}, u32[]{:S(2)}, u32[]{:S(2)}) %collective-permute-start.19) | collective-permute-done | bytes 98336 | tf_op jit(solution)/shard_map/ppermute | solution.py:410
  82.9 1.7 %collective-permute-done.20.other_ref = f32[800,128]{1,0:T(8,128)S(1)} collective-permute-done((f32[800,128]{1,0:T(8,128)S(1)}, f32[800,128]{1,0:T(8,128)S(1)}, u32[]{:S(2)}, u32[]{:S(2)}) %collective-permute-start.20) | collective-permute-done | bytes 409632 | tf_op jit(solution)/shard_map/ppermute | solution.py:410
  (59 shorter events, 9.7 us)
Async XLA Ops:
  2.3 10.5 %copy-start.8 = (f32[512]{0:T(512)S(1)}, f32[512]{0:T(512)}, u32[]{:S(2)}) copy-start(f32[512]{0:T(512)} %param.11) | copy-start | bytes 6148
  2.3 10.5 %copy-start.9 = (f32[512]{0:T(512)S(1)}, f32[512]{0:T(512)}, u32[]{:S(2)}) copy-start(f32[512]{0:T(512)} %param.13) | copy-start | bytes 6148
  7.8 1.9 %collective-permute-start = (f32[800,128]{1,0:T(8,128)S(1)}, f32[800,128]{1,0:T(8,128)S(1)}, u32[]{:S(2)}, u32[]{:S(2)}) collective-permute-start(f32[800,128]{1,0:T(8,128)S(1)} %get-tuple-element.70), channel_id=1, source_target_pairs={{0,1},{1,0},{2,3},{3,2},{4,5},{5,4},{6,7},{7,6},{8,9},{9,8},{10,11... | collective-permute-start | bytes 1228808 | tf_op jit(solution)/shard_map/ppermute | solution.py:410
  9.8 8.4 %collective-permute-start.1 = (f32[400,128]{1,0:T(8,128)S(1)}, f32[400,128]{1,0:T(8,128)S(1)}, u32[]{:S(2)}, u32[]{:S(2)}) collective-permute-start(f32[400,128]{1,0:T(8,128)S(1)} %get-tuple-element.72), channel_id=1, source_target_pairs={{0,4},{1,5},{2,6},{3,7},{4,0},{5,1},{6,2},{7,3},{8,12},{9,13},{10,... | collective-permute-start | bytes 614408 | tf_op jit(solution)/shard_map/ppermute | solution.py:410
  15.4 18.1 %collective-permute-start.4 = (f32[136,512]{1,0:T(8,128)S(1)}, f32[136,512]{1,0:T(8,128)S(1)}, u32[]{:S(2)}, u32[]{:S(2)}) collective-permute-start(f32[136,512]{1,0:T(8,128)S(1)} %get-tuple-element.86), channel_id=1, source_target_pairs={{0,1},{1,2},{2,3},{3,4},{4,5},{5,6},{6,7},{7,8},{8,9},{9,10},{10,1... | collective-permute-start | bytes 835592 | tf_op jit(solution)/shard_map/ppermute | solution.py:612
  18.2 7.5 %collective-permute-start.2 = (f32[200,128]{1,0:T(8,128)S(1)}, f32[200,128]{1,0:T(8,128)S(1)}, u32[]{:S(2)}, u32[]{:S(2)}) collective-permute-start(f32[200,128]{1,0:T(8,128)S(1)} %get-tuple-element.83), channel_id=1, source_target_pairs={{0,2},{1,3},{2,0},{3,1},{4,6},{5,7},{6,4},{7,5},{8,10},{9,11},{10,... | collective-permute-start | bytes 307208 | tf_op jit(solution)/shard_map/ppermute | solution.py:410
  19.9 18.3 %collective-permute-start.6 = (f32[136,512]{1,0:T(8,128)S(1)}, f32[136,512]{1,0:T(8,128)S(1)}, u32[]{:S(2)}, u32[]{:S(2)}) collective-permute-start(f32[136,512]{1,0:T(8,128)S(1)} %get-tuple-element.89), channel_id=1, source_target_pairs={{0,1},{1,2},{2,3},{3,4},{4,5},{5,6},{6,7},{7,8},{8,9},{9,10},{10,1... | collective-permute-start | bytes 835592 | tf_op jit(solution)/shard_map/ppermute | solution.py:612
  25.7 7.8 %collective-permute-start.3 = (f32[200,128]{1,0:T(8,128)S(1)}, f32[200,128]{1,0:T(8,128)S(1)}, u32[]{:S(2)}, u32[]{:S(2)}) collective-permute-start(f32[200,128]{1,0:T(8,128)S(1)} %add.7), channel_id=1, source_target_pairs={{0,8},{1,9},{2,10},{3,11},{4,12},{5,13},{6,14},{7,15},{8,0},{9,1},... | collective-permute-start | bytes 307208 | tf_op jit(solution)/shard_map/ppermute | solution.py:410
  33.5 4.7 %collective-permute-start.5 = (f32[200,128]{1,0:T(8,128)S(1)}, f32[200,128]{1,0:T(8,128)S(1)}, u32[]{:S(2)}, u32[]{:S(2)}) collective-permute-start(f32[200,128]{1,0:T(8,128)S(1)} %add.8.mine_ref), channel_id=1, source_target_pairs={{0,2},{1,3},{2,0},{3,1},{4,6},{5,7},{6,4},{7,5},{8,10},{9,11},{10,... | collective-permute-start | bytes 307208 | tf_op jit(solution)/shard_map/ppermute | solution.py:410
  33.8 10.3 %collective-permute-start.8 = (f32[136,512]{1,0:T(8,128)S(1)}, f32[136,512]{1,0:T(8,128)S(1)}, u32[]{:S(2)}, u32[]{:S(2)}) collective-permute-start(f32[136,512]{1,0:T(8,128)S(1)} %get-tuple-element.91), channel_id=1, source_target_pairs={{0,1},{1,2},{2,3},{3,4},{4,5},{5,6},{6,7},{7,8},{8,9},{9,10},{10,1... | collective-permute-start | bytes 835592 | tf_op jit(solution)/shard_map/ppermute | solution.py:612
  38.2 5.8 %collective-permute-start.7 = (f32[400,128]{1,0:T(8,128)S(1)}, f32[400,128]{1,0:T(8,128)S(1)}, u32[]{:S(2)}, u32[]{:S(2)}) collective-permute-start(f32[400,128]{1,0:T(8,128)S(1)} %join.4.mine_ref), channel_id=1, source_target_pairs={{0,4},{1,5},{2,6},{3,7},{4,0},{5,1},{6,2},{7,3},{8,12},{9,13},{10,... | collective-permute-start | bytes 614408 | tf_op jit(solution)/shard_map/ppermute | solution.py:410
  44.1 1.8 %copy-start.6 = (f32[500]{0:T(512)S(1)}, f32[500]{0:T(512)}, u32[]{:S(2)}) copy-start(f32[500]{0:T(512)} %param.15) | copy-start | bytes 6004
  44.1 1.8 %collective-permute-start.9 = (f32[800,128]{1,0:T(8,128)S(1)}, f32[800,128]{1,0:T(8,128)S(1)}, u32[]{:S(2)}, u32[]{:S(2)}) collective-permute-start(f32[800,128]{1,0:T(8,128)S(1)} %join.5.mine_ref), channel_id=1, source_target_pairs={{0,1},{1,0},{2,3},{3,2},{4,5},{5,4},{6,7},{7,6},{8,9},{9,8},{10,11... | collective-permute-start | bytes 1228808 | tf_op jit(solution)/shard_map/ppermute | solution.py:410
  50.3 1.8 %collective-permute-start.10 = (f32[800,128]{1,0:T(8,128)S(1)}, f32[800,128]{1,0:T(8,128)S(1)}, u32[]{:S(2)}, u32[]{:S(2)}) collective-permute-start(f32[800,128]{1,0:T(8,128)S(1)} %get-tuple-element.101), channel_id=1, source_target_pairs={{0,1},{1,0},{2,3},{3,2},{4,5},{5,4},{6,7},{7,6},{8,9},{9,8},{10,11... | collective-permute-start | bytes 1228808 | tf_op jit(solution)/shard_map/ppermute | solution.py:410
  52.2 8.1 %collective-permute-start.11 = (f32[208,128]{1,0:T(8,128)S(1)}, f32[208,128]{1,0:T(8,128)S(1)}, u32[]{:S(2)}, u32[]{:S(2)}) collective-permute-start(f32[208,128]{1,0:T(8,128)S(1)} %get-tuple-element.103), channel_id=1, source_target_pairs={{0,2},{1,3},{2,0},{3,1},{4,6},{5,7},{6,4},{7,5},{8,10},{9,11},{10,... | collective-permute-start | bytes 319496 | tf_op jit(solution)/shard_map/ppermute | solution.py:410
  55.6 4.6 %collective-permute-start.12 = (f32[192,128]{1,0:T(8,128)S(1)}, f32[192,128]{1,0:T(8,128)S(1)}, u32[]{:S(2)}, u32[]{:S(2)}) collective-permute-start(f32[192,128]{1,0:T(8,128)S(1)} %get-tuple-element.105), channel_id=1, source_target_pairs={{0,4},{1,5},{2,6},{3,7},{4,0},{5,1},{6,2},{7,3},{8,12},{9,13},{10,... | collective-permute-start | bytes 294920 | tf_op jit(solution)/shard_map/ppermute | solution.py:410
  60.3 5.1 %collective-permute-start.13 = (f32[104,128]{1,0:T(8,128)S(1)}, f32[104,128]{1,0:T(8,128)S(1)}, u32[]{:S(2)}, u32[]{:S(2)}) collective-permute-start(f32[104,128]{1,0:T(8,128)S(1)} %get-tuple-element.123), channel_id=1, source_target_pairs={{0,4},{1,5},{2,6},{3,7},{4,0},{5,1},{6,2},{7,3},{8,12},{9,13},{10,... | collective-permute-start | bytes 159752 | tf_op jit(solution)/shard_map/ppermute | solution.py:410
  61.3 4.1 %collective-permute-start.14 = (f32[96,128]{1,0:T(8,128)S(1)}, f32[96,128]{1,0:T(8,128)S(1)}, u32[]{:S(2)}, u32[]{:S(2)}) collective-permute-start(f32[96,128]{1,0:T(8,128)S(1)} %get-tuple-element.125), channel_id=1, source_target_pairs={{0,2},{1,3},{2,0},{3,1},{4,6},{5,7},{6,4},{7,5},{8,10},{9,11},{10,... | collective-permute-start | bytes 147464 | tf_op jit(solution)/shard_map/ppermute | solution.py:410
  65.4 6.8 %collective-permute-start.15 = (f32[200,128]{1,0:T(8,128)S(1)}, f32[200,128]{1,0:T(8,128)S(1)}, u32[]{:S(2)}, u32[]{:S(2)}) collective-permute-start(f32[200,128]{1,0:T(8,128)S(1)} %add.9.total), channel_id=1, source_target_pairs={{0,8},{1,9},{2,10},{3,11},{4,12},{5,13},{6,14},{7,15},{8,0},{9,1},... | collective-permute-start | bytes 307208 | tf_op jit(solution)/shard_map/ppermute | solution.py:410
  72.2 4.7 %collective-permute-start.16 = (f32[104,128]{1,0:T(8,128)S(1)}, f32[104,128]{1,0:T(8,128)S(1)}, u32[]{:S(2)}, u32[]{:S(2)}) collective-permute-start(f32[104,128]{1,0:T(8,128)S(1)} %get-tuple-element.126.mine_a), channel_id=1, source_target_pairs={{0,4},{1,5},{2,6},{3,7},{4,0},{5,1},{6,2},{7,3},{8,12},{9,13},{10,... | collective-permute-start | bytes 159752 | tf_op jit(solution)/shard_map/ppermute | solution.py:410
  72.3 4.5 %collective-permute-start.17 = (f32[96,128]{1,0:T(8,128)S(1)}, f32[96,128]{1,0:T(8,128)S(1)}, u32[]{:S(2)}, u32[]{:S(2)}) collective-permute-start(f32[96,128]{1,0:T(8,128)S(1)} %get-tuple-element.127.mine_b), channel_id=1, source_target_pairs={{0,2},{1,3},{2,0},{3,1},{4,6},{5,7},{6,4},{7,5},{8,10},{9,11},{10,... | collective-permute-start | bytes 147464 | tf_op jit(solution)/shard_map/ppermute | solution.py:410
  76.9 5.8 %collective-permute-start.18 = (f32[208,128]{1,0:T(8,128)S(1)}, f32[208,128]{1,0:T(8,128)S(1)}, u32[]{:S(2)}, u32[]{:S(2)}) collective-permute-start(f32[208,128]{1,0:T(8,128)S(1)} %get-tuple-element.128.mine_a), channel_id=1, source_target_pairs={{0,2},{1,3},{2,0},{3,1},{4,6},{5,7},{6,4},{7,5},{8,10},{9,11},{10,... | collective-permute-start | bytes 319496 | tf_op jit(solution)/shard_map/ppermute | solution.py:410
  78.1 4.6 %collective-permute-start.19 = (f32[192,128]{1,0:T(8,128)S(1)}, f32[192,128]{1,0:T(8,128)S(1)}, u32[]{:S(2)}, u32[]{:S(2)}) collective-permute-start(f32[192,128]{1,0:T(8,128)S(1)} %get-tuple-element.129.mine_b), channel_id=1, source_target_pairs={{0,4},{1,5},{2,6},{3,7},{4,0},{5,1},{6,2},{7,3},{8,12},{9,13},{10,... | collective-permute-start | bytes 294920 | tf_op jit(solution)/shard_map/ppermute | solution.py:410
  82.8 1.8 %collective-permute-start.20 = (f32[800,128]{1,0:T(8,128)S(1)}, f32[800,128]{1,0:T(8,128)S(1)}, u32[]{:S(2)}, u32[]{:S(2)}) collective-permute-start(f32[800,128]{1,0:T(8,128)S(1)} %join.7.mine_ref), channel_id=1, source_target_pairs={{0,1},{1,0},{2,3},{3,2},{4,5},{5,4},{6,7},{7,6},{8,9},{9,8},{10,11... | collective-permute-start | bytes 1228808 | tf_op jit(solution)/shard_map/ppermute | solution.py:410
  (7 other events, 10.2 us)
